TPU v7x, 32 devices: a whole 2x2x4 slice. The times are simulated.
32 devices in a mesh: seq: 4 (over y, x), batch: 8 (over z, core).
Axes of the slice: x: 2, y: 2, z: 4, core: 2. Of those that a mesh axis runs over, the one named last changes fastest.
Arguments:
- tokens: bfloat16 [8, 2048, 768], P('batch', 'seq'), may hold values from -6 to 6
- segment_ids: int32 [8, 2048], P('batch', 'seq'), may hold values from 0 to 10, as said below
- span_starts: int32 [8, 32], P('batch', 'seq'), may hold values from 0 to 1, as said below
- first_gain: float32 [768], replicated, may hold values from 0.5 to 1.5
- first_shift: float32 [768], replicated, may hold values from -3 to 3
- second_gain: float32 [768], replicated, may hold values from 0.5 to 1.5
- second_shift: float32 [768], replicated, may hold values from -3 to 3
- input_weight: bfloat16 [768, 2304], replicated, may hold values from -0.21875 to 0.21875
- input_bias: float32 [2304], replicated, may hold values from -3 to 3
- feature_freq: float32 [64, 64], replicated, may hold values from -4 to 4
- feature_weight: float32 [12, 64], replicated, may hold values from 0.5 to 2
- output_weight: bfloat16 [768, 768], replicated, may hold values from -1.75 to 1.75
- output_bias: float32 [768], replicated, may hold values from -3 to 3
- up_weight: bfloat16 [768, 3072], replicated, may hold values from -0.21875 to 0.21875
- up_bias: float32 [3072], replicated, may hold values from -3 to 3
- down_weight: bfloat16 [3072, 768], replicated, may hold values from -0.109375 to 0.109375
- down_bias: float32 [768], replicated, may hold values from -3 to 3
- cotangent: bfloat16 [8, 2048, 768], P('batch', 'seq'), may hold values from -6 to 6
Outputs:
- result: bfloat16 [8, 2048, 768], P('batch', 'seq')
- tokens_grad: bfloat16 [8, 2048, 768], P('batch', 'seq')
- first_gain_grad: float32 [768], replicated
- first_shift_grad: float32 [768], replicated
- second_gain_grad: float32 [768], replicated
- second_shift_grad: float32 [768], replicated
- input_weight_grad: float32 [768, 2304], replicated
- input_bias_grad: float32 [2304], replicated
- feature_weight_grad: float32 [12, 64], replicated
- output_weight_grad: float32 [768, 768], replicated
- output_bias_grad: float32 [768], replicated
- up_weight_grad: float32 [768, 3072], replicated
- up_bias_grad: float32 [3072], replicated
- down_weight_grad: float32 [3072, 768], replicated
- down_bias_grad: float32 [768], replicated
Inputs may be any that keep to these rules, and one draw needn't show every extreme that they name: `segment_ids`: along each sequence the ids start at 0 and rise by one exactly where a document begins; every sequence holds the same number of documents, and documents run across span and device boundaries. `span_starts`: 1 exactly where the span's first token has another segment id than the token before it, and for each sequence's first span.
All inputs are finite; a program needn't handle non-finite values.
Results may differ from a plain program's by a relative error of at most 0.012.
The roundings to bfloat16 on the way count: a program that leaves them out, or rounds other values in their place, can miss the bound.
Values sent between devices are 32-bit elements; how exact they have to be, the bound alone decides.
No kernel may reach another device: no remote copies, remote signals or barrier semaphores. Data moves between devices by JAX's collectives and lax.ppermute only.
A program may use at most 192 MiB of HBM per device.

v0:
```python
import functools
import math

import jax
import jax.numpy as jnp
import numpy as np
from jax import lax
from jax.experimental import pallas as pl
from jax.experimental.pallas import tpu as pltpu
from jax.sharding import PartitionSpec as P

ROT = 16
HIGH = lax.Precision.HIGHEST
EPSILON = 1e-05
ROT_BASE = 10000.0
F32 = jnp.float32
B16 = jnp.bfloat16
GROUP = 4
EXTRA = 16
NN, NT, TN = ((1,), (0,)), ((1,), (1,)), ((0,), (0,))
TILE = 8
VMEM_LIMIT = 24 * 1024 * 1024
STEP_LIMIT = 14 * 1024 * 1024
BIG_LIMIT = 60 * 1024 * 1024
FREE = pl.CostEstimate(flops=0, bytes_accessed=0, transcendentals=0)

AXES = ("seq", "batch")


def bit_groups():
    seqs, batches = lax.axis_size("seq"), lax.axis_size("batch")
    seq_bits = [batches << k for k in range(seqs.bit_length() - 1)]
    batch_bits = [1 << k for k in range(batches.bit_length() - 1)]
    return batch_bits[:1], seq_bits, batch_bits[1:]


def own_index():
    return lax.axis_index("seq") * lax.axis_size("batch") + lax.axis_index("batch")


def swap(array, bit):
    count = lax.axis_size("seq") * lax.axis_size("batch")
    return lax.ppermute(array, AXES, [(i, i ^ bit) for i in range(count)])


def bit_value(bit):
    return (own_index() & bit) // bit


def device_bits():
    core, seqs, rest = bit_groups()
    count = len(core + seqs + rest)
    return (own_index() >> jnp.arange(count, dtype=jnp.int32)) & 1


def place_of(at, bits):
    total = at.get(0, 0)
    for bit, factor in at.items():
        if bit:
            total = total + factor * bits[bit.bit_length() - 1]
    return total


def shifted(at, bit, factor):
    moved = dict(at)
    moved[bit] = moved.get(bit, 0) + factor
    return moved


def block_spec(shape, block, index):
    tail = (0,) * (len(shape) - 1)
    return pl.BlockSpec((block,) + tuple(shape[1:]), lambda i, bits: (index(i, bits),) + tail)


def sum_tiles(bits, outputs, deps):
    totals = [sum(count for count, _ in segments) for _, segments in outputs]
    arrays, specs, plan, out_specs, out_shape = [], [], [], [], []
    for owner, (block, segments) in enumerate(outputs):
        begin = 0
        for count, terms in segments:
            blocks, slots = count // block, []
            for array, at in terms:
                at = {bit: factor // block for bit, factor in at.items()}

                def index(i, bits, at=at, begin=begin, blocks=blocks):
                    return place_of(at, bits) + jnp.clip(i - begin, 0, blocks - 1)

                specs.append(block_spec(array.shape, block, index))
                slots.append(len(arrays))
                arrays.append(array)
            plan.append((owner, begin, blocks, slots))
            begin += blocks
        shape = (totals[owner],) + arrays[-1].shape[1:]
        out_shape.append(jax.ShapeDtypeStruct(shape, F32))
        out_specs.append(block_spec(shape, block, lambda i, bits, n=begin: jnp.minimum(i, n - 1)))
    steps = max(begin + blocks for _, begin, blocks, _ in plan)

    def kernel(_, *refs):
        ins, outs = refs[: len(arrays)], refs[len(arrays) + len(deps) :]
        i = pl.program_id(0)
        for owner, begin, blocks, slots in plan:

            def add(owner=owner, slots=slots):
                total = ins[slots[0]][...]
                for slot in slots[1:]:
                    total = total + ins[slot][...]
                outs[owner][...] = total

            if begin == 0 and blocks == steps:
                add()
            else:
                pl.when((i >= begin) & (i < begin + blocks))(add)

    got = pl.pallas_call(
        kernel,
        grid_spec=pltpu.PrefetchScalarGridSpec(
            num_scalar_prefetch=1,
            grid=(steps,),
            in_specs=specs + unused(deps),
            out_specs=out_specs,
        ),
        out_shape=out_shape,
        compiler_params=params(STEP_LIMIT),
        cost_estimate=FREE,
        name="sum_tiles",
    )(bits, *arrays, *deps)
    return list(got)


def interleave(bits, pairs, order, merge, block, deps):
    count, shape = pairs[0][0].shape[0], pairs[0][0].shape[1:]
    groups = len(pairs)
    tail = (0,) * len(shape)
    flat = [x for pair in pairs for x in pair]

    def kernel(bits, *refs):
        ins, outs = refs[: 2 * groups], refs[2 * groups + len(deps) :]
        for g, bit in enumerate(order):
            out = outs[0].at[g] if merge else outs[g]
            mine = bits[bit.bit_length() - 1]
            out[pl.ds(mine, 1)] = ins[2 * g][...][None]
            out[pl.ds(1 - mine, 1)] = ins[2 * g + 1][...][None]

    if merge:
        out_specs = [
            pl.BlockSpec((groups, 2, block) + shape, lambda i, bits: (0, 0, i) + tail)
        ]
        out_shape = [jax.ShapeDtypeStruct((groups, 2, count) + shape, F32)]
    else:
        out_specs = [pl.BlockSpec((2, block) + shape, lambda i, bits: (0, i) + tail)] * groups
        out_shape = [jax.ShapeDtypeStruct((2, count) + shape, F32)] * groups
    got = pl.pallas_call(
        kernel,
        grid_spec=pltpu.PrefetchScalarGridSpec(
            num_scalar_prefetch=1,
            grid=(count // block,),
            in_specs=[block_spec(x.shape, block, lambda i, bits: i) for x in flat] + unused(deps),
            out_specs=out_specs,
        ),
        out_shape=out_shape,
        compiler_params=params(STEP_LIMIT),
        cost_estimate=FREE,
        name="interleave",
    )(bits, *flat, *deps)
    if merge:
        return got[0].reshape((groups * 2 * count,) + shape)
    return [x.reshape((2 * count,) + shape) for x in got]


def put_half(bits, bit, own, part, shapes, moves, into, deps, chunks=6):
    half = part.shape[0]
    rows = half // chunks
    at = bit.bit_length() - 1
    count = len(shapes) if len(shapes) == 1 else 4

    def kernel(bits, part, *refs):
        outs, buffer, in_sems, out_sems = refs[len(into) + len(deps) : -3], *refs[-3:]
        which = bits[at] if own else 1 - bits[at]
        spans = [pl.ds(c * rows, rows) for c in range(chunks)]
        coming = [
            pltpu.make_async_copy(part.at[span], buffer.at[span], in_sems.at[c])
            for c, span in enumerate(spans)
        ]
        going = [
            [
                pltpu.make_async_copy(a, b, out_sems.at[c * count + m])
                for m, (a, b) in enumerate(moves(buffer, outs, which, span))
            ]
            for c, span in enumerate(spans)
        ]
        for copy in coming:
            copy.start()
        for copy, onward in zip(coming, going):
            copy.wait()
            for out in onward:
                out.start()
        for onward in going:
            for out in onward:
                out.wait()

    got = pl.pallas_call(
        kernel,
        grid_spec=pltpu.PrefetchScalarGridSpec(
            num_scalar_prefetch=1,
            grid=(1,),
            in_specs=unused([part] + into + deps),
            out_specs=unused(shapes),
            scratch_shapes=[
                pltpu.VMEM(part.shape, F32),
                pltpu.SemaphoreType.DMA((chunks,)),
                pltpu.SemaphoreType.DMA((chunks * count,)),
            ],
        ),
        out_shape=[jax.ShapeDtypeStruct((2, half) + s, F32) for s in shapes],
        input_output_aliases={2 + k: k for k in range(len(into))},
        compiler_params=params(STEP_LIMIT),
        cost_estimate=FREE,
        name="put_half",
    )(bits, part, *into, *deps)
    return list(got)


def move_up(part, outs, half, rows):
    return [(part.at[rows], outs[0].at[half, rows])]


def move_attention(part, outs, half, rows):
    width = part.shape[-1]
    pieces = [outs[0].at[half, rows, :, pl.ds(m * width, width)] for m in range(3)]
    pieces.append(outs[1].at[half, rows])
    return [(part.at[rows, m], piece) for m, piece in enumerate(pieces)]


class Reduction:
    def __init__(self, bits, send, keep, small=None):
        core, seqs, rest = bit_groups()
        ring = seqs + rest[:1]
        self.bits = bits
        self.core, self.tail = core[0], rest[1:]
        self.orders = [ring[k:] + ring[:k] for k in range(3)]
        self.left = keep.shape[0] // 3
        came = swap(send, self.core)
        self.terms = [[(keep, {0: g * self.left}), (came, {0: g * self.left})] for g in range(3)]
        self.small = small
        if small is not None:
            self.small_bits = ring + self.tail
            self.small_came = swap(small, self.core)

    def small_output(self):
        return [] if self.small is None else [(1, [(1, [(self.small, {}), (self.small_came, {})])])]

    def small_next(self, small):
        if small:
            (self.small,) = small
            bits = self.small_bits
            if bits:
                self.small_came, self.small_bits = swap(self.small, bits[0]), bits[1:]

    def scatter(self, step, deps):
        self.left //= 2
        outputs = []
        for g, order in enumerate(self.orders):
            bit = order[step]
            terms = [
                (t, shifted(shifted(at, 0, self.left), bit, -self.left)) for t, at in self.terms[g]
            ]
            outputs.append((min(2, max(self.left // 2, 1)), [(self.left, terms)]))
        sends = sum_tiles(self.bits, outputs + self.small_output(), deps)
        for g, order in enumerate(self.orders):
            bit = order[step]
            came = swap(sends[g], bit)
            self.terms[g] = [(t, shifted(at, bit, self.left)) for t, at in self.terms[g]]
            self.terms[g].append((came, {}))
        self.small_next(sends[3:])
        return sends[:1]

    def exchange(self, deps):
        segments = [(self.left, terms) for terms in self.terms]
        total, *small = sum_tiles(self.bits, [(self.left, segments)] + self.small_output(), deps)
        self.small_next(small)
        first = total
        for bit in self.tail[:-1]:
            total = total + swap(total, bit)
            if small:
                self.small_next([self.small + self.small_came])
        self.both = (total, swap(total, self.tail[-1]))
        return [first]

    def settle(self, deps):
        outputs = [
            (self.left, [(self.left, [(x, {0: g * self.left}) for x in self.both])])
            for g in range(3)
        ]
        self.pieces = sum_tiles(self.bits, outputs + self.small_output(), deps)
        self.small_next(self.pieces[3:])
        self.pieces = self.pieces[:3]
        self.next_swap(2)
        return self.pieces[:1]

    def next_swap(self, step):
        self.came = [swap(p, order[step]) for p, order in zip(self.pieces, self.orders)]

    def gather(self, step, deps):
        pairs = list(zip(self.pieces, self.came))
        order = [o[step] for o in self.orders]
        block = max(pairs[0][0].shape[0] // 4, 1) if step == 0 else max(pairs[0][0].shape[0] // 2, 1)
        self.pieces = interleave(self.bits, pairs, order, step == 0, block, deps)
        if step:
            self.next_swap(step - 1)
            return self.pieces[:1]
        self.came = swap(self.pieces, self.core)
        return [self.pieces]

    def finish_own(self, how, shapes, deps):
        self.out = put_half(self.bits, self.core, True, self.pieces, shapes, how, [], deps)
        return self.out[:1]

    def finish(self, how, shapes, deps):
        got = put_half(self.bits, self.core, False, self.came, shapes, how, self.out, deps)
        return [g.reshape(-1, s[-1]) for g, s in zip(got, shapes)]


def from_partners(array):
    return [swap(array, m * lax.axis_size("batch")) for m in range(1, lax.axis_size("seq"))]


def cosine_table(points):
    index = np.arange(points, dtype=np.float64)
    table = np.cos(math.pi * (index[None, :] + 0.5) * index[:, None] / points) * math.sqrt(
        2.0 / points
    )
    return (table * np.where(index[:, None] == 0, math.sqrt(0.5), 1.0)).astype(np.float32)


def rotary_freq():
    return (ROT_BASE ** (-2.0 * np.arange(ROT // 2) / ROT)).astype(np.float32)


def dot(a, b, dims, precision=None):
    return lax.dot_general(a, b, (dims, ((), ())), preferred_element_type=F32, precision=precision)


def params(limit=None):
    return pltpu.CompilerParams(vmem_limit_bytes=limit or VMEM_LIMIT)


def ordered(kernel, count, deps):
    def run(*refs):
        kernel(*refs[:count], *refs[count + len(deps) :])

    return run


def unused(deps):
    return [pl.BlockSpec(memory_space=pl.ANY)] * len(deps)


def full(shape):
    return pl.BlockSpec(shape, lambda *_: (0,) * len(shape))


def normalise(tokens):
    values = tokens.astype(F32)
    centre = jnp.mean(values, axis=-1, keepdims=True)
    centred = values - centre
    spread = jnp.mean(centred * centred, axis=-1, keepdims=True)
    rstd = lax.rsqrt(spread + EPSILON)
    return centred * rstd, rstd


def norm_kernel(
    offset, tok, g1, s1, g2, s2, in_bias, feat_weight, up_bias_in, table_t, freq, turns,
    first_t, second, second_t, proj, proj_t, angle, vec, up_bias,
):
    width = tok.shape[1]
    for r, ref in enumerate((g1, s1, g2, s2)):
        vec[r : r + 1] = ref[...].reshape(1, width)
    for r in range(3):
        vec[4 + r : 5 + r] = in_bias[r * width : (r + 1) * width].reshape(1, width)
    vec[7:8] = feat_weight[...]
    up_bias[...] = up_bias_in[...].reshape(up_bias.shape)
    xhat, _ = normalise(tok[...])
    one = (xhat * vec[0:1] + vec[1:2]).astype(B16)
    two = (xhat * vec[2:3] + vec[3:4]).astype(B16)
    second[...] = two
    first_t[...] = one.T
    second_t[...] = two.T
    table = dot(table_t[...], freq[...], NN, HIGH)
    size = table.shape[0]
    wide = GROUP * size
    row = lax.broadcasted_iota(jnp.int32, (wide, wide), 0) // size
    same = row == lax.broadcasted_iota(jnp.int32, (wide, wide), 1) // size
    for out, block in ((proj, table), (proj_t, table.T)):
        block = jnp.concatenate([block] * GROUP, axis=1)
        out[...] = jnp.where(same, jnp.concatenate([block] * GROUP, axis=0), 0.0)
    length = tok.shape[0]
    at = lax.broadcasted_iota(jnp.int32, (ROT // 2, length), 1) + offset[0]
    turn = at.astype(F32) * turns[...]
    angle[0] = jnp.cos(turn)
    angle[1] = jnp.sin(turn)


def norms(offset, tok, small, freq):
    rows, width = tok.shape
    size = freq.shape[0]
    wide = GROUP * size
    return pl.pallas_call(
        norm_kernel,
        in_specs=[pl.BlockSpec(memory_space=pltpu.SMEM)] + [pl.BlockSpec()] * (4 + len(small)),
        out_shape=(
            jax.ShapeDtypeStruct((width, rows), B16),
            jax.ShapeDtypeStruct((rows, width), B16),
            jax.ShapeDtypeStruct((width, rows), B16),
            jax.ShapeDtypeStruct((wide, wide), F32),
            jax.ShapeDtypeStruct((wide, wide), F32),
            jax.ShapeDtypeStruct((2, ROT // 2, rows), F32),
            jax.ShapeDtypeStruct((8, width), F32),
            jax.ShapeDtypeStruct((1, small[-1].size), F32),
        ),
        compiler_params=params(BIG_LIMIT),
        name="norms",
    )(offset, tok, *small, jnp.asarray(cosine_table(size).T), freq,
      jnp.asarray(rotary_freq()[:, None]))


def mlp_kernel(second, cot, up, up_bias, down, act, d_hidden, down_grad, bias_grad):
    hidden = dot(second[...], up[...], NN) + up_bias[...]
    phi = 0.5 + 0.5 * lax.erf(hidden * math.sqrt(0.5))
    density = jnp.exp(hidden * hidden * -0.5) * (1.0 / math.sqrt(2.0 * math.pi))
    active = (hidden * phi).astype(B16)
    d_active = dot(cot[...], down[...], NT)
    d_low = (d_active * (phi + hidden * density)).astype(B16)
    act[...] = active
    d_hidden[...] = d_low
    down_grad[...] = dot(active, cot[...], TN)
    bias_grad[...] = jnp.sum(d_low.astype(F32), axis=0, keepdims=True)


def mlp_part(second, cot, up, up_bias, down, tile):
    rows, width = second.shape
    hidden = up.shape[1]
    return pl.pallas_call(
        mlp_kernel,
        grid=(hidden // tile,),
        in_specs=[
            full((rows, width)),
            full((rows, width)),
            pl.BlockSpec((width, tile), lambda j: (0, j)),
            pl.BlockSpec((1, tile), lambda j: (0, j)),
            pl.BlockSpec((tile, width), lambda j: (j, 0)),
        ],
        out_specs=[
            pl.BlockSpec((rows, tile), lambda j: (0, j)),
            pl.BlockSpec((rows, tile), lambda j: (0, j)),
            pl.BlockSpec((tile, width), lambda j: (j, 0)),
            pl.BlockSpec((1, tile), lambda j: (0, j)),
        ],
        out_shape=(
            jax.ShapeDtypeStruct((rows, hidden), B16),
            jax.ShapeDtypeStruct((rows, hidden), B16),
            pltpu.HBM((hidden, width), F32),
            jax.ShapeDtypeStruct((1, hidden), F32),
        ),
        compiler_params=params(),
        name="mlp",
    )(second, cot, up, up_bias, down)


def up_kernel(at, second_t, d_hidden, out):
    g = dot(second_t[...], d_hidden[...], NN)
    out[...] = g.reshape(out.shape)


def up_half(bits, bit, own, second_t, d_hidden, deps, steps=6):
    width, length = second_t.shape
    hidden = d_hidden.shape[1]
    half, tile = width // 2, hidden // steps
    at = bit.bit_length() - 1
    which = lambda bits: bits[at] if own else 1 - bits[at]
    return pl.pallas_call(
        ordered(up_kernel, 3, deps),
        grid_spec=pltpu.PrefetchScalarGridSpec(
            num_scalar_prefetch=1,
            grid=(steps,),
            in_specs=[
                pl.BlockSpec((half, length), lambda j, bits: (which(bits), 0)),
                pl.BlockSpec((length, tile), lambda j, bits: (0, j)),
            ]
            + unused(deps),
            out_specs=pl.BlockSpec((half // TILE, TILE, tile), lambda j, bits: (0, 0, j)),
        ),
        out_shape=jax.ShapeDtypeStruct((half // TILE, TILE, hidden), F32),
        compiler_params=params(),
        cost_estimate=FREE,
        name="up_half",
    )(bits, second_t, d_hidden, *deps)


def tail_kernel(active, d_hidden, up, down, out, d_second):
    one = dot(active[...], down[...], NN)
    two = dot(d_hidden[...], up[...], NT)

    @pl.when(pl.program_id(0) == 0)
    def _():
        out[...] = one
        d_second[...] = two

    @pl.when(pl.program_id(0) > 0)
    def _():
        out[...] += one
        d_second[...] += two


def mlp_tail(active, d_hidden, up, down, deps, steps=6):
    rows, hidden = active.shape
    width = up.shape[0]
    tile = hidden // steps
    wide = jax.ShapeDtypeStruct((rows, width), F32)
    return pl.pallas_call(
        ordered(tail_kernel, 4, deps),
        grid=(steps,),
        in_specs=[
            pl.BlockSpec((rows, tile), lambda j: (0, j)),
            pl.BlockSpec((rows, tile), lambda j: (0, j)),
            pl.BlockSpec((width, tile), lambda j: (0, j)),
            pl.BlockSpec((tile, width), lambda j: (j, 0)),
        ]
        + unused(deps),
        out_specs=[full((rows, width)), full((rows, width))],
        out_shape=(wide, wide),
        compiler_params=params(),
        cost_estimate=FREE,
        name="mlp_tail",
    )(active, d_hidden, up, down, *deps)


def result_kernel(tok, att, w_out, mlp_out, out_bias, down_bias, result):
    attn_out = dot(att[...], w_out[...], TN) + out_bias[...].reshape(1, -1)
    result[...] = (tok[...].astype(F32) + attn_out + (mlp_out[...] + down_bias[...].reshape(1, -1))).astype(B16)


def results(tok, att, w_out, mlp_out, out_bias, down_bias, deps):
    return pl.pallas_call(
        ordered(result_kernel, 6, deps),
        in_specs=[pl.BlockSpec()] * 6 + unused(deps),
        out_shape=jax.ShapeDtypeStruct(tok.shape, B16),
        compiler_params=params(),
        cost_estimate=FREE,
        name="results",
    )(tok, att, w_out, mlp_out, out_bias, down_bias, *deps)


def rotate(x, cosine, sine, back):
    half = ROT // 2
    a, b = x[:, :half], x[:, half:ROT]
    sine = -sine if back else sine
    return jnp.concatenate([a * cosine - b * sine, b * cosine + a * sine, x[:, ROT:]], axis=1)


def head_sums(x, size):
    cut = x.reshape(x.shape[0] // size, size, x.shape[1])
    total = jnp.sum(cut, axis=1, keepdims=True)
    return jnp.broadcast_to(total, cut.shape).reshape(x.shape)


def feature_kernel(
    size, first_t, wq, wk, wv, vec, proj_t, angle, seg, start,
    q_feat, k_feat, v_low, scaled, expo, summary,
):
    columns = vec[...].T
    bq, bk, bv, weight = (columns[:, c : c + 1] for c in range(4, 8))
    scale = math.sqrt(2.0 / size)
    feats = []
    for side, (w, bias, out) in enumerate(((wq, bq, q_feat), (wk, bk, k_feat))):
        x = dot(w[...], first_t[...], TN) + bias
        heads = x.shape[0] // size
        x = rotate(x.reshape(heads, size, x.shape[1]), angle[0], angle[1], False)
        sx = x.reshape(heads * size, x.shape[2]) * scale
        lifted = dot(proj_t[...], sx, NN, HIGH)
        e = jnp.exp(lifted - 0.5 * head_sums(sx * sx, size))
        phi = (weight * e).astype(B16)
        scaled[side] = sx
        expo[side] = e
        out[...] = phi
        feats.append(phi)
    value = (dot(wv[...], first_t[...], TN) + bv).astype(B16)
    v_low[...] = value
    ids = seg[...]
    length = ids.shape[1]
    last = (ids == ids[:, length - 1 :]).astype(F32)
    whole = jnp.where((ids[:, :1] == ids[:, length - 1 :]) & (start[0] == 0), 1.0, 0.0)
    key_last = (feats[1].astype(F32) * last).astype(B16)
    row = lax.broadcasted_iota(jnp.int32, (EXTRA, length), 0)
    ones = jnp.where(row == 0, 1.0, 0.0).astype(B16)
    tall = size + EXTRA
    rows = lax.broadcasted_iota(jnp.int32, (tall, 2 * size), 0)
    for pair in range(heads // 2):
        got = []
        for h in (2 * pair, 2 * pair + 1):
            v_ext = jnp.concatenate([value[h * size : (h + 1) * size], ones], axis=0)
            got.append(dot(v_ext, key_last[h * size : (h + 1) * size], NT))
        both = jnp.concatenate(got, axis=1)
        summary[pair] = jnp.where(rows == size + 1, whole, both)


def features(first_t, in_weight, vec, proj_t, angle, seg, start, size, deps):
    width, length = first_t.shape
    tile = GROUP * size
    steps = width // tile
    pairs = GROUP // 2
    column = lambda k: pl.BlockSpec((width, tile), lambda g: (0, k * steps + g))
    rows = pl.BlockSpec((tile, length), lambda g: (g, 0))
    two = pl.BlockSpec((2, tile, length), lambda g: (0, g, 0))
    low = jax.ShapeDtypeStruct((width, length), B16)
    wide = jax.ShapeDtypeStruct((2, width, length), F32)
    return pl.pallas_call(
        ordered(functools.partial(feature_kernel, size), 9, deps),
        grid=(steps,),
        in_specs=[
            full((width, length)),
            column(0), column(1), column(2),
            pl.BlockSpec((8, tile), lambda g: (0, g)),
            full((tile, tile)),
            full(angle.shape), full(seg.shape),
            pl.BlockSpec(memory_space=pltpu.SMEM),
        ]
        + unused(deps),
        out_specs=[
            rows, rows, rows, two, two,
            pl.BlockSpec((pairs, size + EXTRA, 2 * size), lambda g: (g, 0, 0)),
        ],
        out_shape=(
            low, low, low, wide, wide,
            jax.ShapeDtypeStruct((steps * pairs, size + EXTRA, 2 * size), F32),
        ),
        compiler_params=params(),
        cost_estimate=FREE,
        name="features",
    )(first_t, in_weight, in_weight, in_weight, vec, proj_t, angle, seg, start, *deps)


def chain_gates(flags, place, forward):
    count = len(flags)
    gates = [None]
    for m in range(1, count):
        other = place ^ m
        gate = jnp.where(other < place if forward else other > place, 1.0, 0.0)
        for n in range(1, count):
            if n != m:
                mid = place ^ n
                inside = (
                    (mid > other) & (mid < place) if forward else (mid < other) & (mid > place)
                )
                gate = gate * jnp.where(inside, flags[n], 1.0)
        gates.append(gate)
    return gates


def joined(refs, gates, pair):
    total = None
    for ref, gate in zip(refs, gates[1:]):
        term = jnp.where(gate != 0.0, ref[pair] * gate, 0.0)
        total = term if total is None else total + term
    return total


def halves(x):
    high = x.astype(B16).astype(F32)
    return high, x - high


def attention_kernel(size, partners, place, start, *refs):
    refs = list(refs)
    q_feat, k_feat, v_low, w_out, cot, seg, seg_col = refs[:7]
    came = refs[7 : 7 + partners]
    att, dq_out, dk_out, dv_out, here_out, gate_out, mask = refs[7 + partners :]
    length = seg.shape[1]
    block = 256
    ids = seg[...]

    @pl.when(pl.program_id(0) == 0)
    def _():
        key_at = lax.broadcasted_iota(jnp.int32, (length, length), 0)
        query_at = lax.broadcasted_iota(jnp.int32, (length, length), 1)
        same = (seg_col[...] == ids) & (key_at <= query_at)
        mask[...] = jnp.where(same, 1.0, 0.0)

    flags = [None] + [ref[0, size + 1 : size + 2, :] for ref in came]
    ahead = chain_gates(flags, place[0], True)
    behind = chain_gates(flags, place[0], False)
    for m in range(partners):
        gate_out[m] = jnp.broadcast_to(behind[m + 1], gate_out.shape[1:])
    keep = jnp.where((ids == ids[:, :1]) & (start[0] == 0), 1.0, 0.0)
    d_att = dot(w_out[...], cot[...], NT)
    tall = size + EXTRA
    row_s = lax.broadcasted_iota(jnp.int32, (tall, size), 0)
    row_d = lax.broadcasted_iota(jnp.int32, (EXTRA, length), 0)
    blocks = [(t * block, (t + 1) * block) for t in range(length // block)]
    for pair in range(GROUP // 2):
        state_pair = joined(came, ahead, pair)
        here_pair = []
        for h in (2 * pair, 2 * pair + 1):
            rows = slice(h * size, (h + 1) * size)
            state = state_pair[:, (h % 2) * size : (h % 2 + 1) * size]
            n_high, n_low = halves(state[size : size + 1])
            ext = jnp.where(row_s < size, state, 0.0)
            ext = ext + jnp.where((row_s == size) | (row_s == size + 2), n_high, 0.0)
            ext = (ext + jnp.where(row_s == size + 1, n_low, 0.0)).astype(B16)
            q, k, v = q_feat[rows], k_feat[rows], v_low[rows]
            outside = dot(ext, q, NN)
            scores, d_nums, d_dens = [], [], []
            for lo, hi in blocks:
                raw = dot(k[:, :hi], q[:, lo:hi], TN) * mask[:hi, lo:hi]
                s_low = raw.astype(B16)
                kept = keep[:, lo:hi]
                out_part = outside[:, lo:hi]
                denom = jnp.sum(raw, axis=0, keepdims=True) + kept * (
                    out_part[size : size + 1] + out_part[size + 1 : size + 2]
                )
                numer = dot(v[:, :hi], s_low, NN) + kept * out_part[:size]
                inverse = 1.0 / denom
                attended = numer * inverse
                da = d_att[rows, lo:hi]
                att[rows, lo:hi] = attended.astype(B16)
                d_nums.append((da * inverse).astype(B16))
                d_dens.append(-jnp.sum(da * attended, axis=0, keepdims=True) * inverse)
                scores.append(s_low)
            d_num = jnp.concatenate(d_nums, axis=1)
            d_den = jnp.concatenate(d_dens, axis=1)
            d_high, d_low = halves(d_den)
            tail = jnp.where(row_d < 2, d_high, jnp.where(row_d == 2, d_low, 0.0)).astype(B16)
            dn_ext = jnp.concatenate([d_num, tail], axis=0)
            dq_state = dot(ext, dn_ext, TN)
            dv_parts = [None] * len(blocks)
            dk_parts = [None] * len(blocks)
            for n, (lo, hi) in enumerate(blocks):
                d_score = dot(v[:, :hi], d_num[:, lo:hi], TN) + d_den[:, lo:hi]
                d_score = (d_score * mask[:hi, lo:hi]).astype(B16)
                dq_out[rows, lo:hi] = (
                    dot(k[:, :hi], d_score, NN) + keep[:, lo:hi] * dq_state[:, lo:hi]
                )
                for m in range(n + 1):
                    a, b = blocks[m]
                    dv = dot(d_num[:, lo:hi], scores[n][a:b], NT)
                    dk = dot(q[:, lo:hi], d_score[a:b], NT)
                    dv_parts[m] = dv if dv_parts[m] is None else dv_parts[m] + dv
                    dk_parts[m] = dk if dk_parts[m] is None else dk_parts[m] + dk
            for m, (a, b) in enumerate(blocks):
                dv_out[rows, a:b] = dv_parts[m]
                dk_out[rows, a:b] = dk_parts[m]
            here = dot((dn_ext.astype(F32) * keep).astype(B16), q, NT)
            norm = here[size : size + 1] + here[size + 2 : size + 3]
            here_pair.append(jnp.where(row_s < size, here, jnp.where(row_s == size, norm, 0.0)))
        here_out[pair] = jnp.concatenate(here_pair, axis=1)


def attention(
    place, start, q_feat, k_feat, v_low, w_out, cot, seg, seg_col, came, size, groups, so_far, deps
):
    width, length = q_feat.shape
    tile = GROUP * size
    steps = width // tile
    first, count = groups
    pairs = GROUP // 2
    partners = len(came)
    rows = pl.BlockSpec((tile, length), lambda g: (first + g, 0))
    packed = pl.BlockSpec((pairs, size + EXTRA, 2 * size), lambda g: (first + g, 0, 0))
    wide = jax.ShapeDtypeStruct((width, length), F32)
    return pl.pallas_call(
        ordered(functools.partial(attention_kernel, size, partners), 9 + partners, so_far + deps),
        grid=(count,),
        in_specs=[
            pl.BlockSpec(memory_space=pltpu.SMEM),
            pl.BlockSpec(memory_space=pltpu.SMEM),
            rows, rows, rows,
            pl.BlockSpec((tile, width), lambda g: (first + g, 0)),
            full(cot.shape), full(seg.shape), full(seg_col.shape),
        ]
        + [packed] * partners
        + unused(so_far + deps),
        out_specs=[rows, rows, rows, rows, packed, full((partners, 8, 2 * size))],
        out_shape=(
            jax.ShapeDtypeStruct((width, length), B16),
            wide, wide, wide,
            jax.ShapeDtypeStruct((steps * pairs, size + EXTRA, 2 * size), F32),
            jax.ShapeDtypeStruct((partners, 8, 2 * size), F32),
        ),
        scratch_shapes=[pltpu.VMEM((length, length), F32)],
        input_output_aliases={9 + partners + k: k for k in range(len(so_far))},
        compiler_params=params(),
        cost_estimate=FREE,
        name="attention",
    )(place, start, q_feat, k_feat, v_low, w_out, cot, seg, seg_col, *came, *so_far, *deps)


def backward_kernel(size, partners, opens, closes, *refs):
    refs = list(refs)
    (dq, dk, dv, k_feat, v_low, scaled, expo, vec, wq, wk, wv, first_t, att, cot_col, proj,
     angle, seg, tok, cot, d_second, vec_all) = refs[:21]
    came = refs[21 : 21 + partners]
    gates_in, up_bias, bits = refs[21 + partners : 24 + partners]
    refs = refs[24 + partners :]
    if not opens:
        acc_in, small_in = refs[:2]
        refs = refs[2:]
    send, keep, small, acc = refs[:4]
    first = 0 if opens else 2
    mine = bits[0]
    half = first_t.shape[0] // 2
    tile = dq.shape[0]
    here = pl.ds(pl.multiple_of(mine * half, half), half)
    there = pl.ds(pl.multiple_of((1 - mine) * half, half), half)
    columns = pl.ds(pl.multiple_of((first + pl.program_id(0)) * tile, tile), tile)
    count = send.shape[0]
    weight = vec[...].T[:, 7:8]
    step = pl.program_id(0)
    scale = math.sqrt(2.0 / size)
    ids = seg[...]
    length = ids.shape[1]
    last = jnp.where(ids == ids[:, length - 1 :], 1.0, 0.0)
    gates = [None] + [gates_in[m][:1] for m in range(partners)]
    tall = size + EXTRA
    row_s = lax.broadcasted_iota(jnp.int32, (tall, size), 0)
    row_d = lax.broadcasted_iota(jnp.int32, (EXTRA, length), 0)
    ones = jnp.where(row_d < 2, 1.0, 0.0).astype(B16)
    dks, dvs = [], []
    for pair in range(GROUP // 2):
        later = joined(came, gates, pair)
        for h in (2 * pair, 2 * pair + 1):
            rows = slice(h * size, (h + 1) * size)
            g = later[:, (h % 2) * size : (h % 2 + 1) * size]
            n_high, n_low = halves(g[size : size + 1])
            ext = jnp.where(row_s < size, g, jnp.where(row_s == size, n_high, 0.0))
            ext = (ext + jnp.where(row_s == size + 1, n_low, 0.0)).astype(B16)
            v_ext = jnp.concatenate([v_low[rows], ones], axis=0)
            dks.append(dk[rows] + last * dot(ext, v_ext, TN))
            dvs.append(dv[rows] + last * dot(ext[:size], k_feat[rows], NN))
    d_feats = (dq[...], jnp.concatenate(dks, axis=0))
    pieces = []
    total = None
    for side, d_feat in enumerate(d_feats):
        t1 = d_feat * expo[side]
        total = t1 if total is None else total + t1
        d_expo = weight * t1
        d_x = dot(proj[...], d_expo, NN, HIGH) - scaled[side] * head_sums(d_expo, size)
        heads = d_x.shape[0] // size
        d_x = rotate((d_x * scale).reshape(heads, size, length), angle[0], angle[1], True)
        pieces.append(d_x.reshape(heads * size, length).astype(B16))
    pieces.append(jnp.concatenate(dvs, axis=0).astype(B16))

    @pl.when(step == 0)
    def _():
        small[...] = jnp.zeros(small.shape, F32) if opens else small_in[...]
        if opens:
            for r in range(up_bias.shape[1] // first_t.shape[0]):
                part = slice(r * first_t.shape[0], (r + 1) * first_t.shape[0])
                small[9 + r : 10 + r, :] = up_bias[:, part]

    total = jnp.broadcast_to(jnp.sum(total, axis=1, keepdims=True), (tile, 128))
    small[8:9, columns] = total.T[:1]
    one_row = jnp.ones((8, length), B16)
    part = None
    for m, (piece, w) in enumerate(zip(pieces, (wq, wk, wv))):
        g = dot(first_t[there, :], piece, NT)
        send[:, m] = g.reshape(count, TILE, tile)
        g = dot(first_t[here, :], piece, NT)
        keep[:, m] = g.reshape(count, TILE, tile)
        small[5 + m : 6 + m, columns] = dot(one_row, piece, NT)[:1]
        d = dot(w[...], piece, NN)
        part = d if part is None else part + d
    send[:, 3] = dot(att[there, :], cot_col[...], NN).reshape(count, TILE, tile)
    keep[:, 3] = dot(att[here, :], cot_col[...], NN).reshape(count, TILE, tile)

    @pl.when(step == 0)
    def _():
        acc[...] = part if opens else acc_in[...] + part

    @pl.when(step > 0)
    def _():
        acc[...] += part

    if not closes:
        return
    tok_grad = refs[4]

    @pl.when(step == pl.num_programs(0) - 1)
    def _():
        d_first = acc[...].T
        d_sec = d_second[...]
        xhat, rstd = normalise(tok[...])
        cotangent = cot[...].astype(F32)
        for r, x in enumerate((d_first * xhat, d_first, d_sec * xhat, d_sec, cotangent)):
            small[r : r + 1, :] = jnp.sum(x, axis=0, keepdims=True)
        e = d_first * vec_all[0:1] + d_sec * vec_all[2:3]
        mean_e = jnp.mean(e, axis=-1, keepdims=True)
        mean_x = jnp.mean(e * xhat, axis=-1, keepdims=True)
        tok_grad[...] = (cotangent + rstd * (e - mean_e - xhat * mean_x)).astype(B16)


def backward(
    dq, dk, dv, k_feat, v_low, scaled, expo, vec, in_weight, first_t, att, cot, proj, angle,
    seg, tok, d_second, came, gates, up_bias, bits, size, groups, so_far, deps,
):
    width, length = dq.shape
    tile = GROUP * size
    steps = width // tile
    begin, some = groups
    opens, closes = begin == 0, begin + some == steps
    carried = [] if opens else [so_far[3], so_far[2]]
    kept = so_far[:2]
    pairs = GROUP // 2
    partners = len(came)
    rows = pl.BlockSpec((tile, length), lambda g: (begin + g, 0))
    two = pl.BlockSpec((2, tile, length), lambda g: (0, begin + g, 0))
    column = lambda k: pl.BlockSpec((width, tile), lambda g: (0, k * steps + begin + g))
    packed = pl.BlockSpec((pairs, size + EXTRA, 2 * size), lambda g: (begin + g, 0, 0))
    count = width // TILE // 2
    return pl.pallas_call(
        ordered(
            functools.partial(backward_kernel, size, partners, opens, closes),
            24 + partners + len(carried),
            kept + deps,
        ),
        grid=(some,),
        in_specs=[
            rows, rows, rows, rows, rows, two, two,
            pl.BlockSpec((8, tile), lambda g: (0, begin + g)),
            column(0), column(1), column(2),
            full(first_t.shape), full(att.shape),
            pl.BlockSpec((length, tile), lambda g: (0, begin + g)),
            full((tile, tile)),
            full(angle.shape), full(seg.shape),
            full(tok.shape), full(cot.shape), full(d_second.shape), full(vec.shape),
        ]
        + [packed] * partners
        + [full(gates.shape), full(up_bias.shape), pl.BlockSpec(memory_space=pltpu.SMEM)]
        + [full(x.shape) for x in carried]
        + unused(kept + deps),
        out_specs=[
            pl.BlockSpec((count, 4, TILE, tile), lambda g: (0, 0, 0, begin + g)),
            pl.BlockSpec((count, 4, TILE, tile), lambda g: (0, 0, 0, begin + g)),
            full((16, width)),
            full((width, length)),
            full(tok.shape),
        ][: 4 + closes],
        out_shape=[
            jax.ShapeDtypeStruct((count, 4, TILE, width), F32),
            jax.ShapeDtypeStruct((count, 4, TILE, width), F32),
            jax.ShapeDtypeStruct((16, width), F32),
            jax.ShapeDtypeStruct((width, length), F32),
            jax.ShapeDtypeStruct(tok.shape, B16),
        ][: 4 + closes],
        input_output_aliases={24 + partners + len(carried) + k: k for k in range(len(kept))},
        compiler_params=params(),
        cost_estimate=FREE,
        name="backward",
    )(dq, dk, dv, k_feat, v_low, scaled, expo, vec, in_weight, in_weight, in_weight, first_t,
      att, cot, proj, angle, seg, tok, cot, d_second, vec, *came, gates, up_bias, bits, *carried, *kept, *deps)


def per_device(
    tokens,
    segment_ids,
    span_starts,
    first_gain,
    first_shift,
    second_gain,
    second_shift,
    input_weight,
    input_bias,
    feature_freq,
    feature_weight,
    output_weight,
    output_bias,
    up_weight,
    up_bias,
    down_weight,
    down_bias,
    cotangent,
):
    seq_count, length, width = tokens.shape
    assert seq_count == 1
    heads, size = feature_weight.shape
    tok, cot = tokens[0], cotangent[0]
    seqs, batches = lax.axis_size("seq"), lax.axis_size("batch")
    place = lax.axis_index("seq").reshape(1)
    seg = segment_ids.reshape(1, length)
    seg_col = segment_ids.reshape(length, 1)
    start = span_starts[0, :1]
    small = (
        first_gain, first_shift, second_gain, second_shift, input_bias,
        feature_weight.reshape(1, -1), up_bias,
    )
    first_t, second, second_t, proj, proj_t, angle, vec, up_bias_row = norms(
        place * length, tok, small, feature_freq
    )
    active, d_hidden, down_grad, up_bias_grad = mlp_part(
        second, cot, up_weight, up_bias_row, down_weight, 512
    )
    down_sum = lax.psum(down_grad, AXES)
    core = bit_groups()[0][0]
    bits = device_bits()
    up_shapes = [(TILE, up_weight.shape[1])]
    attn_shapes = [(TILE, 3 * width), (TILE, width)]

    def rest(first_t, second_t, active, d_hidden):
        up_send = up_half(bits, core, False, second_t, d_hidden, [])
        up_keep = up_half(bits, core, True, second_t, d_hidden, [up_send])
        up = Reduction(bits, up_send, up_keep)
        q_feat, k_feat, v_low, scaled, expo, summary = features(
            first_t, input_weight, vec, proj_t, angle, seg, start, size, [up_keep]
        )
        states = from_partners(summary)
        mlp_out, d_second = mlp_tail(active, d_hidden, up_weight, down_weight, [summary])
        last = up.scatter(0, [mlp_out] + states)
        groups = heads // GROUP
        att, dq, dk, dv, here, gates = attention(
            place, start, q_feat, k_feat, v_low, output_weight, cot, seg, seg_col, states, size,
            (0, groups), [], last,
        )
        later = from_partners(here)
        result = results(tok, att, output_weight, mlp_out, output_bias, down_bias, [])
        last = up.scatter(1, [result] + later)
        fixed = (
            dq, dk, dv, k_feat, v_low, scaled, expo, vec, input_weight, first_t, att, cot, proj,
            angle, seg, tok, d_second, later, gates, up_bias_grad, bits, size,
        )
        some = list(backward(*fixed, (0, groups - 1), [], last))
        last = up.scatter(2, some[:1])
        send, keep, small, _, tok_grad = backward(*fixed, (groups - 1, 1), some, last)
        attn = Reduction(bits, send, keep, small.reshape(1, 2, 8, width))
        last = up.exchange([tok_grad])
        last = attn.scatter(0, last)
        last = attn.scatter(1, last)
        last = attn.scatter(2, last)
        last = attn.exchange(last)
        last = up.settle(last)
        last = up.gather(2, last)
        last = up.gather(1, last)
        last = attn.settle(last)
        last = up.gather(0, last)
        last = attn.gather(2, last)
        last = up.finish_own(move_up, up_shapes, last)
        last = attn.gather(1, last)
        last = attn.gather(0, last)
        last = attn.finish_own(move_attention, attn_shapes, last)
        (up_sum,) = up.finish(move_up, up_shapes, last)
        in_sum, out_sum = attn.finish(move_attention, attn_shapes, [up_sum])
        return result, tok_grad, up_sum, in_sum, out_sum, attn.small.reshape(16, width)

    def nothing(first_t, second_t, active, d_hidden):
        low = jnp.zeros(tok.shape, B16)
        return (
            low, low, jnp.zeros(up_weight.shape, F32), jnp.zeros(input_weight.shape, F32),
            jnp.zeros(output_weight.shape, F32), jnp.zeros((16, width), F32),
        )

    result, tok_grad, up_sum, in_sum, out_sum, sums = lax.cond(
        start[0] < 2, rest, nothing, first_t, second_t, active, d_hidden
    )
    return (
        result[None],
        tok_grad[None],
        sums[0],
        sums[1],
        sums[2],
        sums[3],
        in_sum,
        sums[5:8].reshape(-1),
        sums[8].reshape(heads, size),
        out_sum,
        sums[4],
        up_sum,
        sums[9 : 9 + up_weight.shape[1] // width].reshape(-1),
        down_sum,
        sums[4],
    )


def solution(mesh):
    in_specs = (
        P("batch", "seq", None),
        P("batch", "seq"),
        P("batch", "seq"),
        P(),
        P(),
        P(),
        P(),
        P(),
        P(),
        P(),
        P(),
        P(),
        P(),
        P(),
        P(),
        P(),
        P(),
        P("batch", "seq", None),
    )
    out_specs = (
        P("batch", "seq", None),
        P("batch", "seq", None),
        P(),
        P(),
        P(),
        P(),
        P(),
        P(),
        P(),
        P(),
        P(),
        P(),
        P(),
        P(),
        P(),
    )
    return jax.shard_map(
        per_device, mesh=mesh, in_specs=in_specs, out_specs=out_specs, check_vma=False
    )
```

profile of v0, /device:TPU:1, one launch (start us, length us, event | category | flops | bytes accessed | tf_op | source)
XLA Modules:
  0.0 376.9 jit_solution(7511556668506383390)
XLA Ops:
  7.2 1.4 reshape.116.feat_weight
  8.6 3.7 norms.1
  14.1 13.1 %mlp.1 = (bf16[512,3072]{1,0:T(8,128)(2,1)}, bf16[512,3072]{1,0:T(8,128)(2,1)S(1)}, f32[3072,768]{1,0:T(8,128)}, f32[1,3072]{1,0:T(1,128)S(1)}) custom-call(bf16[512,768]{1,0:T(8,128)(2,1)S(1)} %copy-done.37, bf16[512,768]{1,0:T(8,128)(2,1)} %bitcast.60, bf16[768,3072]{1,0:T(8,128)(2,1)} %up.1, f32[1,3072]{1,0:T(1,128)S(1)} %copy-done.38, bf16[3072,768]{1,0:T(8,128)(2,1)} %down.1), custom_call_target="tpu_custom_call" | custom-call | tf_op jit(solution)/shard_map/mlp/pallas_call | solution.py:442
  28.4 332.8 %conditional.1 = (f32[768,3072]{1,0:T(8,128)}, f32[768,2304]{1,0:T(8,128)}, f32[768,768]{1,0:T(8,128)}, f32[16,768]{1,0:T(8,128)}, bf16[1,512,768]{2,1,0:T(8,128...) conditional(s32[]{:T(128)} %bitcast.23, () %tuple.27, ...), branch_computations={%region_0.0_spmd, %region_1.0_spmd} | conditional | flops 4620 | bytes 470387456 | solution.py:1058
  29.8 4.3 %up_half.2.refs_3_ = f32[48,8,3072]{2,1,0:T(8,128)S(1)} custom-call(s32[5]{0:T(128)S(1)} %shift-right-arithmetic_and_fusion.refs_0_._.refs_26_.bits, bf16[768,512]{1,0:T(8,128)(2,1)} %get-tuple-element.78.refs_1_, bf16[512,3072]{1,0:T(8,128)(2,1)S(1)} %get-tuple-element.79.refs_2_.refs_1_), custom_call_target="tpu_custom_call" | custom-call | tf_op jit(solution)/shard_map/cond/branch_1_fun/up_half/pallas_call | solution.py:480
  34.3 3.3 up_half.3.refs_9_.refs_0_.refs_2_.refs_4_.refs_3_.refs_6_.refs_8_.refs_5_.refs_10_
  37.6 8.1 %features.1 = (bf16[768,512]{1,0:T(8,128)(2,1)S(1)}, bf16[768,512]{1,0:T(8,128)(2,1)S(1)}, bf16[768,512]{1,0:T(8,128)(2,1)S(1)}, f32[2,768,512]{2,1,0:T(8,128)S(...) custom-call(bf16[768,512]{1,0:T(8,128)(2,1)S(1)} %copy-done.46, bf16[768,2304]{1,0:T(8,128)(2,1)S(1)} %copy-done.39, ...), custom_call_target="tpu_custom_call" | custom-call | tf_op jit(solution)/shard_map/cond/branch_1_fun/features/pallas_call | solution.py:616
  45.7 1.7 copy-done.4
  49.2 3.6 collective-permute-start.3
  53.2 9.1 %mlp_tail.1 = (f32[512,768]{1,0:T(8,128)S(1)}, f32[512,768]{1,0:T(8,128)S(1)}) custom-call(bf16[512,3072]{1,0:T(8,128)(2,1)} %get-tuple-element.80.refs_0_, bf16[512,3072]{1,0:T(8,128)(2,1)S(1)} %copy-done.41, bf16[768,3072]{1,0:T(8,128)(2,1)S(1)} %bitcast.63, bf16[3072,768]{1,0:T(8,128)(2,1)S(1)} %bitcast.65, f32[6,80,128]{2,1,0:T(8,128)S(1)} %get-tuple-element.90.refs_4_), custom_call_target="tpu_custom_call" | custom-call | tf_op jit(solution)/shard_map/cond/branch_1_fun/mlp_tail/pallas_call | solution.py:519
  62.3 1.2 copy-done.17
  63.5 6.5 %collective-permute-done.2.refs_8_.refs_10_ = f32[6,80,128]{2,1,0:T(8,128)S(1)} collective-permute-done((f32[6,80,128]{2,1,0:T(8,128)S(1)}, f32[6,80,128]{2,1,0:T(8,128)S(1)}, u32[]{:S(2)}, u32[]{:S(2)}) %collective-permute-start.2) | collective-permute-done | bytes 245792 | tf_op jit(solution)/shard_map/cond/branch_1_fun/ppermute | solution.py:43
  71.1 3.0 sum_tiles.10
  74.4 1.2 collective-permute-start.6
  75.6 1.4 collective-permute-start.4
  77.2 1.3 copy-done.8
  78.4 1.4 copy-done.12
  83.8 17.6 %attention.1 = (bf16[768,512]{1,0:T(8,128)(2,1)S(1)}, f32[768,512]{1,0:T(8,128)S(1)}, f32[768,512]{1,0:T(8,128)S(1)}, f32[768,512]{1,0:T(8,128)S(1)}, f32[6,80,1...) custom-call(s32[1]{0:T(128)} %get-tuple-element.96.refs_0_, s32[1]{0:T(128)S(1)} %bitcast.76, bf16[768,512]{1,0:T(8,128)(2,1)S(1)} %copy-done.36, ...), custom_call_target="tpu_custom_call" | custom-call | tf_op jit(solution)/shard_map/cond/branch_1_fun/attention/pallas_call | solution.py:769
  101.4 1.2 collective-permute-start.9
  102.7 5.9 %collective-permute-done.9.refs_12_.refs_23_ = f32[6,80,128]{2,1,0:T(8,128)S(1)} collective-permute-done((f32[6,80,128]{2,1,0:T(8,128)S(1)}, f32[6,80,128]{2,1,0:T(8,128)S(1)}, u32[]{:S(2)}, u32[]{:S(2)}) %collective-permute-start.9) | collective-permute-done | bytes 245792 | tf_op jit(solution)/shard_map/cond/branch_1_fun/ppermute | solution.py:43
  108.7 1.4 copy-done.21
  110.1 3.3 results.1.refs_9_
  114.4 1.2 collective-permute-done.8.refs_11_.refs_22_
  115.6 2.8 sum_tiles.11
  118.8 1.5 collective-permute-start.10
  120.4 9.5 %backward.2 = (f32[48,4,8,768]{3,2,1,0:T(8,128)S(1)}, f32[48,4,8,768]{3,2,1,0:T(8,128)S(1)}, f32[16,768]{1,0:T(8,128)S(1)}, f32[768,512]{1,0:T(8,128)S(1)}) custom-call(f32[768,512]{1,0:T(8,128)S(1)} %get-tuple-element.109.refs_0_, f32[768,512]{1,0:T(8,128)S(1)} %get-tuple-element.110.refs_1_, f32[768,512]{1,0:T(8,128)S(1)} %get-tuple-element.111.refs_2_, ...), custom_call_target="tpu_custom_call" | custom-call | tf_op jit(solution)/shard_map/cond/branch_1_fun/backward/pallas_call | solution.py:918
  133.5 2.1 sum_tiles.12
  138.3 1.4 copy-done.28
  139.7 6.9 %backward.3 = (f32[48,4,8,768]{3,2,1,0:T(8,128)S(1)}, f32[48,4,8,768]{3,2,1,0:T(8,128)S(1)}, f32[16,768]{1,0:T(8,128)S(1)}, f32[768,512]{1,0:T(8,128)}, bf16[512,768]{1,0:T(8,128)(2,1)}) custom-call(f32[768,512]{1,0:T(8,128)S(1)} %get-tuple-element.109.refs_0_, ...), custom_call_target="tpu_custom_call", output_to_operand_aliasing={{0}: (29, {}), {1}: (30, {})} | custom-call | tf_op jit(solution)/shard_map/cond/branch_1_fun/backward/pallas_call | solution.py:918
  146.6 1.6 collective-permute-start.17
  151.4 3.3 collective-permute-done.14.refs_9_
  155.5 2.7 copy-done.3
  158.2 2.0 sum_tiles.13.refs_8_.refs_0_.refs_2_.refs_4_
  164.9 16.8 %collective-permute-done.22.refs_10_ = f32[1,2,8,768]{3,2,1,0:T(8,128)S(1)} collective-permute-done((f32[1,2,8,768]{3,2,1,0:T(8,128)S(1)}, f32[1,2,8,768]{3,2,1,0:T(8,128)S(1)}, u32[]{:S(2)}, u32[]{:S(2)}) %collective-permute-start.22) | collective-permute-done | bytes 49184 | tf_op jit(solution)/shard_map/cond/branch_1_fun/ppermute | solution.py:43
  181.7 5.9 %collective-permute-done.21.refs_8_.refs_10_.refs_12_ = f32[8,4,8,768]{3,2,1,0:T(8,128)S(1)} collective-permute-done((f32[8,4,8,768]{3,2,1,0:T(8,128)S(1)}, f32[8,4,8,768]{3,2,1,0:T(8,128)S(1)}, u32[]{:S(2)}, u32[]{:S(2)}) %collective-permute-start.21) | collective-permute-done | bytes 786464 | tf_op jit(solution)/shard_map/cond/branch_1_fun/ppermute | solution.py:43
  188.3 1.8 collective-permute-start.24
  191.6 1.5 collective-permute-start.26
  193.1 11.8 %collective-permute-done.26.refs_13_ = f32[1,2,8,768]{3,2,1,0:T(8,128)S(1)} collective-permute-done((f32[1,2,8,768]{3,2,1,0:T(8,128)S(1)}, f32[1,2,8,768]{3,2,1,0:T(8,128)S(1)}, u32[]{:S(2)}, u32[]{:S(2)}) %collective-permute-start.26) | collective-permute-done | bytes 49184 | tf_op jit(solution)/shard_map/cond/branch_1_fun/ppermute | solution.py:43
  204.9 11.8 %collective-permute-done.24.refs_7_.refs_8_ = f32[4,4,8,768]{3,2,1,0:T(8,128)S(1)} collective-permute-done((f32[4,4,8,768]{3,2,1,0:T(8,128)S(1)}, f32[4,4,8,768]{3,2,1,0:T(8,128)S(1)}, u32[]{:S(2)}, u32[]{:S(2)}) %collective-permute-start.24) | collective-permute-done | bytes 393248 | tf_op jit(solution)/shard_map/cond/branch_1_fun/ppermute | solution.py:43
  217.6 1.5 collective-permute-start.30
  219.1 21.0 %collective-permute-done.30.refs_16_ = f32[1,2,8,768]{3,2,1,0:T(8,128)S(1)} collective-permute-done((f32[1,2,8,768]{3,2,1,0:T(8,128)S(1)}, f32[1,2,8,768]{3,2,1,0:T(8,128)S(1)}, u32[]{:S(2)}, u32[]{:S(2)}) %collective-permute-start.30) | collective-permute-done | bytes 49184 | tf_op jit(solution)/shard_map/cond/branch_1_fun/ppermute | solution.py:43
  241.6 2.4 collective-permute-start.31
  244.0 2.0 collective-permute-start.33
  246.0 6.8 %collective-permute-done.31.refs_1_ = f32[2,8,3072]{2,1,0:T(8,128)S(1)} collective-permute-done((f32[2,8,3072]{2,1,0:T(8,128)S(1)}, f32[2,8,3072]{2,1,0:T(8,128)S(1)}, u32[]{:S(2)}, u32[]{:S(2)}) %collective-permute-start.31) | collective-permute-done | bytes 196640 | tf_op jit(solution)/shard_map/cond/branch_1_fun/ppermute | solution.py:43
  253.5 1.4 collective-permute-start.35
  255.0 2.0 collective-permute-start.36
  256.9 11.7 %collective-permute-done.35.refs_3_ = f32[4,8,3072]{2,1,0:T(8,128)S(1)} collective-permute-done((f32[4,8,3072]{2,1,0:T(8,128)S(1)}, f32[4,8,3072]{2,1,0:T(8,128)S(1)}, u32[]{:S(2)}, u32[]{:S(2)}) %collective-permute-start.35) | collective-permute-done | bytes 393248 | tf_op jit(solution)/shard_map/cond/branch_1_fun/ppermute | solution.py:43
  268.6 1.2 interleave.7
  270.0 1.7 collective-permute-start.40
  274.2 25.9 %collective-permute-done.41.refs_7_ = f32[1,2,8,768]{3,2,1,0:T(8,128)S(1)} collective-permute-done((f32[1,2,8,768]{3,2,1,0:T(8,128)S(1)}, f32[1,2,8,768]{3,2,1,0:T(8,128)S(1)}, u32[]{:S(2)}, u32[]{:S(2)}) %collective-permute-start.41) | collective-permute-done | bytes 49184 | tf_op jit(solution)/shard_map/cond/branch_1_fun/ppermute | solution.py:43
  302.5 1.5 collective-permute-start.43
  304.1 3.2 interleave.8
  309.4 1.3 collective-permute-start.46
  311.0 4.5 %put_half.4.refs_6_.refs_0_ = f32[2,48,8,3072]{3,2,1,0:T(8,128)} custom-call(s32[5]{0:T(128)S(1)} %shift-right-arithmetic_and_fusion.refs_0_._.refs_26_.bits, f32[48,8,3072]{2,1,0:T(8,128)} %bitcast.9.refs_6_.part, f32[4,4,8,768]{3,2,1,0:T(8,128)S(1)} %bitcast.37), custom_call_target="tpu_custom_call" | custom-call | tf_op jit(solution)/shard_map/cond/branch_1_fun/put_half/pallas_call | solution.py:201
  316.0 1.6 collective-permute-done.48.refs_5_
  318.7 1.5 collective-permute-start.49
  320.2 10.9 %collective-permute-start.42 = (f32[48,8,3072]{2,1,0:T(8,128)}, f32[48,8,3072]{2,1,0:T(8,128)}, u32[]{:S(2)}, u32[]{:S(2)}) collective-permute-start(f32[48,8,3072]{2,1,0:T(8,128)} %bitcast.9.refs_6_.part), channel_id=1, source_target_pairs={{0,1},{1,0},{2,3},{3,2},{4,5},{5,4},{6,7},{7,6},{8,9},{9,8},{10,11... | collective-permute-start | bytes 14155784 | tf_op jit(solution)/shard_map/cond/branch_1_fun/ppermute | solution.py:43
  331.3 2.4 collective-permute-done.49.refs_1_
  333.6 3.2 interleave.11
  336.8 9.4 %collective-permute-start.52 = (f32[48,4,8,768]{3,2,1,0:T(8,128)}, f32[48,4,8,768]{3,2,1,0:T(8,128)}, u32[]{:S(2)}, u32[]{:S(2)}) collective-permute-start(f32[48,4,8,768]{3,2,1,0:T(8,128)} %bitcast.16.part.refs_0_), channel_id=1, source_target_pairs={{0,1},{1,0},{2,3},{3,2},{4,5},{5,4},{6,7},{7,6},{8,9},{9,8},{10,11... | collective-permute-start | bytes 14155784 | tf_op jit(solution)/shard_map/cond/branch_1_fun/ppermute | solution.py:43
  347.0 4.6 %put_half.5 = (f32[2,48,8,2304]{3,2,1,0:T(8,128)}, f32[2,48,8,768]{3,2,1,0:T(8,128)}) custom-call(s32[5]{0:T(128)S(1)} %shift-right-arithmetic_and_fusion.refs_0_._.refs_26_.bits, f32[48,4,8,768]{3,2,1,0:T(8,128)} %bitcast.16.part.refs_0_, f32[48,4,8,768]{3,2,1,0:T(8,128)} %bitcast.16.part.refs_0_), custom_call_target="tpu_custom_call" | custom-call | tf_op jit(solution)/shard_map/cond/branch_1_fun/put_half/pallas_call | solution.py:201
  351.7 4.5 %put_half.6 = f32[2,48,8,3072]{3,2,1,0:T(8,128)} custom-call(s32[5]{0:T(128)S(1)} %shift-right-arithmetic_and_fusion.refs_0_._.refs_26_.bits, f32[48,8,3072]{2,1,0:T(8,128)} %collective-permute-done.42.part, f32[2,48,8,3072]{3,2,1,0:T(8,128)} %put_half.4.refs_6_.refs_0_, ...), custom_call_target="tpu_custom_call", output_to_operand_aliasing={{}: (2, {})} | custom-call | tf_op jit(solution)/shard_map/cond/branch_1_fun/put_half/pallas_call | solution.py:201
  356.2 4.7 %put_half.7 = (f32[2,48,8,2304]{3,2,1,0:T(8,128)}, f32[2,48,8,768]{3,2,1,0:T(8,128)}) custom-call(s32[5]{0:T(128)S(1)} %shift-right-arithmetic_and_fusion.refs_0_._.refs_26_.bits, f32[48,4,8,768]{3,2,1,0:T(8,128)} %collective-permute-done.52.part, ...), custom_call_target="tpu_custom_call", output_to_operand_aliasing={{0}: (2, {}), {1}: (3, {})} | custom-call | tf_op jit(solution)/shard_map/cond/branch_1_fun/put_half/pallas_call | solution.py:201
  361.9 8.1 %copy.98 = f32[3072,768]{1,0:T(8,128)} copy(f32[3072,768]{1,0:T(8,128)} %all-reduce.2.cloned.1.call-done) | data formatting | bytes 18874368
  (239 shorter events, 44.1 us)
Async XLA Ops:
  7.2 354.1 %all-reduce.2.cloned.1.call-start = ((), (), s32[]{:S(2)}) async-start(), calls=%async_computation | async-start | bytes 18874368 | tf_op jit(solution)/shard_map/psum | solution.py:1000
  34.1 37.0 %collective-permute-start = (f32[48,8,3072]{2,1,0:T(8,128)S(1)}, f32[48,8,3072]{2,1,0:T(8,128)S(1)}, u32[]{:S(2)}, u32[]{:S(2)}) collective-permute-start(f32[48,8,3072]{2,1,0:T(8,128)S(1)} %up_half.2.refs_3_), channel_id=1, source_target_pairs={{0,1},{1,0},{2,3},{3,2},{4,5},{5,4},{6,7},{7,6},{8,9},{9,8},{10,11... | collective-permute-start | bytes 14155784 | tf_op jit(solution)/shard_map/cond/branch_1_fun/ppermute | solution.py:43
  34.3 18.9 %slice-start.2 = ((s8[4718592]{0:T(1024)(128)(4,1)}), s8[4194304]{0:T(1024)(128)(4,1)S(1)}, s32[]{:S(2)}) async-start(s8[4718592]{0:T(1024)(128)(4,1)} %bitcast.62), calls=%async_computation.3 | async-start | bytes 8388608 | tf_op jit(solution)/shard_map/cond
  34.3 18.9 %slice-start.4 = ((s8[4718592]{0:T(1024)(128)(4,1)}), s8[4194304]{0:T(1024)(128)(4,1)S(1)}, s32[]{:S(2)}) async-start(s8[4718592]{0:T(1024)(128)(4,1)} %bitcast.64), calls=%async_computation.5 | async-start | bytes 8388608 | tf_op jit(solution)/shard_map/cond
  37.6 33.6 %copy-start = (f32[48,8,3072]{2,1,0:T(8,128)}, f32[48,8,3072]{2,1,0:T(8,128)S(1)}, u32[]{:S(2)}) copy-start(f32[48,8,3072]{2,1,0:T(8,128)S(1)} %up_half.3.refs_9_.refs_0_.refs_2_.refs_4_.refs_3_.refs_6_.refs_8_.refs_5_.refs_10_) | copy-start | bytes 14155780 | tf_op jit(solution)/shard_map/cond
  37.6 15.5 %copy-start.41 = (bf16[512,3072]{1,0:T(8,128)(2,1)S(1)}, bf16[512,3072]{1,0:T(8,128)(2,1)}, u32[]{:S(2)}) copy-start(bf16[512,3072]{1,0:T(8,128)(2,1)} %copy-done.40) | copy-start | bytes 9437188 | tf_op jit(solution)/shard_map/cond
  49.2 14.3 %collective-permute-start.3 = (f32[6,80,128]{2,1,0:T(8,128)S(1)}, f32[6,80,128]{2,1,0:T(8,128)S(1)}, u32[]{:S(2)}, u32[]{:S(2)}) collective-permute-start(f32[6,80,128]{2,1,0:T(8,128)S(1)} %get-tuple-element.90.refs_4_), channel_id=1, source_target_pairs={{0,24},{1,25},{2,26},{3,27},{4,28},{5,29},{6,30},{7,31},{8,16},{9,... | collective-permute-start | bytes 737288 | tf_op jit(solution)/shard_map/cond/branch_1_fun/ppermute | solution.py:43
  52.9 17.2 %collective-permute-start.2 = (f32[6,80,128]{2,1,0:T(8,128)S(1)}, f32[6,80,128]{2,1,0:T(8,128)S(1)}, u32[]{:S(2)}, u32[]{:S(2)}) collective-permute-start(f32[6,80,128]{2,1,0:T(8,128)S(1)} %get-tuple-element.90.refs_4_), channel_id=1, source_target_pairs={{0,16},{1,17},{2,18},{3,19},{4,20},{5,21},{6,22},{7,23},{8,24},{9,... | collective-permute-start | bytes 737288 | tf_op jit(solution)/shard_map/cond/branch_1_fun/ppermute | solution.py:43
  53.1 18.0 %collective-permute-start.1 = (f32[6,80,128]{2,1,0:T(8,128)S(1)}, f32[6,80,128]{2,1,0:T(8,128)S(1)}, u32[]{:S(2)}, u32[]{:S(2)}) collective-permute-start(f32[6,80,128]{2,1,0:T(8,128)S(1)} %get-tuple-element.90.refs_4_), channel_id=1, source_target_pairs={{0,8},{1,9},{2,10},{3,11},{4,12},{5,13},{6,14},{7,15},{8,0},{9,1},... | collective-permute-start | bytes 737288 | tf_op jit(solution)/shard_map/cond/branch_1_fun/ppermute | solution.py:43
  74.2 41.4 %collective-permute-start.5 = (f32[8,8,3072]{2,1,0:T(8,128)}, f32[8,8,3072]{2,1,0:T(8,128)}, u32[]{:S(2)}, u32[]{:S(2)}) collective-permute-start(f32[8,8,3072]{2,1,0:T(8,128)} %get-tuple-element.93), channel_id=1, source_target_pairs={{0,16},{1,17},{2,18},{3,19},{4,20},{5,21},{6,22},{7,23},{8,24},{9,... | collective-permute-start | bytes 2359304 | tf_op jit(solution)/shard_map/cond/branch_1_fun/ppermute | solution.py:43
  74.4 41.2 %collective-permute-start.6 = (f32[8,8,3072]{2,1,0:T(8,128)}, f32[8,8,3072]{2,1,0:T(8,128)}, u32[]{:S(2)}, u32[]{:S(2)}) collective-permute-start(f32[8,8,3072]{2,1,0:T(8,128)} %get-tuple-element.94), channel_id=1, source_target_pairs={{0,2},{1,3},{2,0},{3,1},{4,6},{5,7},{6,4},{7,5},{8,10},{9,11},{10,... | collective-permute-start | bytes 2359304 | tf_op jit(solution)/shard_map/cond/branch_1_fun/ppermute | solution.py:43
  75.6 39.9 %collective-permute-start.4 = (f32[8,8,3072]{2,1,0:T(8,128)}, f32[8,8,3072]{2,1,0:T(8,128)}, u32[]{:S(2)}, u32[]{:S(2)}) collective-permute-start(f32[8,8,3072]{2,1,0:T(8,128)} %get-tuple-element.92.refs_12_), channel_id=1, source_target_pairs={{0,8},{1,9},{2,10},{3,11},{4,12},{5,13},{6,14},{7,15},{8,0},{9,1},... | collective-permute-start | bytes 2359304 | tf_op jit(solution)/shard_map/cond/branch_1_fun/ppermute | solution.py:43
  77.1 38.4 %slice-start = ((s8[4718592]{0:T(1024)(128)(4,1)}), s8[4194304]{0:T(1024)(128)(4,1)S(1)}, s32[]{:S(2)}) async-start(s8[4718592]{0:T(1024)(128)(4,1)} %bitcast.28), calls=%async_computation.1 | async-start | bytes 8388608 | tf_op jit(solution)/shard_map/cond
  83.8 31.8 %slice-start.1 = ((s8[4718592]{0:T(1024)(128)(4,1)}), s8[524288]{0:T(1024)(128)(4,1)S(1)}, s32[]{:S(2)}) async-start(s8[4718592]{0:T(1024)(128)(4,1)} %bitcast.28), calls=%async_computation.2 | async-start | bytes 1048576 | tf_op jit(solution)/shard_map/cond
  83.8 31.8 %copy-start.2 = (f32[48,8,3072]{2,1,0:T(8,128)S(1)}, f32[48,8,3072]{2,1,0:T(8,128)}, u32[]{:S(2)}) copy-start(f32[48,8,3072]{2,1,0:T(8,128)} %copy-done.1) | copy-start | bytes 14155780 | tf_op jit(solution)/shard_map/cond
  101.4 7.3 %collective-permute-start.9 = (f32[6,80,128]{2,1,0:T(8,128)S(1)}, f32[6,80,128]{2,1,0:T(8,128)S(1)}, u32[]{:S(2)}, u32[]{:S(2)}) collective-permute-start(f32[6,80,128]{2,1,0:T(8,128)S(1)} %get-tuple-element.105), channel_id=1, source_target_pairs={{0,24},{1,25},{2,26},{3,27},{4,28},{5,29},{6,30},{7,31},{8,16},{9,... | collective-permute-start | bytes 737288 | tf_op jit(solution)/shard_map/cond/branch_1_fun/ppermute | solution.py:43
  102.6 12.9 %collective-permute-start.8 = (f32[6,80,128]{2,1,0:T(8,128)S(1)}, f32[6,80,128]{2,1,0:T(8,128)S(1)}, u32[]{:S(2)}, u32[]{:S(2)}) collective-permute-start(f32[6,80,128]{2,1,0:T(8,128)S(1)} %get-tuple-element.105), channel_id=1, source_target_pairs={{0,16},{1,17},{2,18},{3,19},{4,20},{5,21},{6,22},{7,23},{8,24},{9,... | collective-permute-start | bytes 737288 | tf_op jit(solution)/shard_map/cond/branch_1_fun/ppermute | solution.py:43
  108.7 6.8 %collective-permute-start.7 = (f32[6,80,128]{2,1,0:T(8,128)S(1)}, f32[6,80,128]{2,1,0:T(8,128)S(1)}, u32[]{:S(2)}, u32[]{:S(2)}) collective-permute-start(f32[6,80,128]{2,1,0:T(8,128)S(1)} %get-tuple-element.105), channel_id=1, source_target_pairs={{0,8},{1,9},{2,10},{3,11},{4,12},{5,13},{6,14},{7,15},{8,0},{9,1},... | collective-permute-start | bytes 737288 | tf_op jit(solution)/shard_map/cond/branch_1_fun/ppermute | solution.py:43
  118.4 13.2 %collective-permute-start.11 = (f32[4,8,3072]{2,1,0:T(8,128)S(1)}, f32[4,8,3072]{2,1,0:T(8,128)S(1)}, u32[]{:S(2)}, u32[]{:S(2)}) collective-permute-start(f32[4,8,3072]{2,1,0:T(8,128)S(1)} %get-tuple-element.107), channel_id=1, source_target_pairs={{0,2},{1,3},{2,0},{3,1},{4,6},{5,7},{6,4},{7,5},{8,10},{9,11},{10,... | collective-permute-start | bytes 1179656 | tf_op jit(solution)/shard_map/cond/branch_1_fun/ppermute | solution.py:43
  118.8 12.9 %collective-permute-start.12 = (f32[4,8,3072]{2,1,0:T(8,128)S(1)}, f32[4,8,3072]{2,1,0:T(8,128)S(1)}, u32[]{:S(2)}, u32[]{:S(2)}) collective-permute-start(f32[4,8,3072]{2,1,0:T(8,128)S(1)} %get-tuple-element.108), channel_id=1, source_target_pairs={{0,8},{1,9},{2,10},{3,11},{4,12},{5,13},{6,14},{7,15},{8,0},{9,1},... | collective-permute-start | bytes 1179656 | tf_op jit(solution)/shard_map/cond/branch_1_fun/ppermute | solution.py:43
  118.8 12.9 %collective-permute-start.10 = (f32[4,8,3072]{2,1,0:T(8,128)S(1)}, f32[4,8,3072]{2,1,0:T(8,128)S(1)}, u32[]{:S(2)}, u32[]{:S(2)}) collective-permute-start(f32[4,8,3072]{2,1,0:T(8,128)S(1)} %get-tuple-element.106.refs_27_), channel_id=1, source_target_pairs={{0,16},{1,17},{2,18},{3,19},{4,20},{5,21},{6,22},{7,23},{8,24},{9,... | collective-permute-start | bytes 1179656 | tf_op jit(solution)/shard_map/cond/branch_1_fun/ppermute | solution.py:43
  139.7 15.8 %copy-start.23 = (f32[4,8,3072]{2,1,0:T(8,128)S(1)}, f32[4,8,3072]{2,1,0:T(8,128)}, u32[]{:S(2)}) copy-start(f32[4,8,3072]{2,1,0:T(8,128)} %copy-done.22) | copy-start | bytes 1179652 | tf_op jit(solution)/shard_map/cond
  139.7 15.8 %copy-start.26 = (f32[4,8,3072]{2,1,0:T(8,128)S(1)}, f32[4,8,3072]{2,1,0:T(8,128)}, u32[]{:S(2)}) copy-start(f32[4,8,3072]{2,1,0:T(8,128)} %copy-done.24) | copy-start | bytes 1179652 | tf_op jit(solution)/shard_map/cond
  146.6 13.6 %collective-permute-start.17 = (f32[48,4,8,768]{3,2,1,0:T(8,128)S(1)}, f32[48,4,8,768]{3,2,1,0:T(8,128)S(1)}, u32[]{:S(2)}, u32[]{:S(2)}) collective-permute-start(f32[48,4,8,768]{3,2,1,0:T(8,128)S(1)} %get-tuple-element.127), channel_id=1, source_target_pairs={{0,1},{1,0},{2,3},{3,2},{4,5},{5,4},{6,7},{7,6},{8,9},{9,8},{10,11... | collective-permute-start | bytes 14155784 | tf_op jit(solution)/shard_map/cond/branch_1_fun/ppermute | solution.py:43
  148.2 6.5 %collective-permute-start.14 = (f32[2,8,3072]{2,1,0:T(8,128)S(1)}, f32[2,8,3072]{2,1,0:T(8,128)S(1)}, u32[]{:S(2)}, u32[]{:S(2)}) collective-permute-start(f32[2,8,3072]{2,1,0:T(8,128)S(1)} %get-tuple-element.120), channel_id=1, source_target_pairs={{0,8},{1,9},{2,10},{3,11},{4,12},{5,13},{6,14},{7,15},{8,0},{9,1},... | collective-permute-start | bytes 589832 | tf_op jit(solution)/shard_map/cond/branch_1_fun/ppermute | solution.py:43
  149.1 6.2 %collective-permute-start.15 = (f32[2,8,3072]{2,1,0:T(8,128)S(1)}, f32[2,8,3072]{2,1,0:T(8,128)S(1)}, u32[]{:S(2)}, u32[]{:S(2)}) collective-permute-start(f32[2,8,3072]{2,1,0:T(8,128)S(1)} %get-tuple-element.121), channel_id=1, source_target_pairs={{0,16},{1,17},{2,18},{3,19},{4,20},{5,21},{6,22},{7,23},{8,24},{9,... | collective-permute-start | bytes 589832 | tf_op jit(solution)/shard_map/cond/branch_1_fun/ppermute | solution.py:43
  149.6 5.9 %collective-permute-start.13 = (f32[2,8,3072]{2,1,0:T(8,128)S(1)}, f32[2,8,3072]{2,1,0:T(8,128)S(1)}, u32[]{:S(2)}, u32[]{:S(2)}) collective-permute-start(f32[2,8,3072]{2,1,0:T(8,128)S(1)} %get-tuple-element.119.refs_31_), channel_id=1, source_target_pairs={{0,2},{1,3},{2,0},{3,1},{4,6},{5,7},{6,4},{7,5},{8,10},{9,11},{10,... | collective-permute-start | bytes 589832 | tf_op jit(solution)/shard_map/cond/branch_1_fun/ppermute | solution.py:43
  150.6 9.7 %collective-permute-start.18 = (f32[1,2,8,768]{3,2,1,0:T(8,128)S(1)}, f32[1,2,8,768]{3,2,1,0:T(8,128)S(1)}, u32[]{:S(2)}, u32[]{:S(2)}) collective-permute-start(f32[1,2,8,768]{3,2,1,0:T(8,128)S(1)} %bitcast.58), channel_id=1, source_target_pairs={{0,1},{1,0},{2,3},{3,2},{4,5},{5,4},{6,7},{7,6},{8,9},{9,8},{10,11... | collective-permute-start | bytes 147464 | tf_op jit(solution)/shard_map/cond/branch_1_fun/ppermute | solution.py:43
  161.2 20.5 %collective-permute-start.20 = (f32[8,4,8,768]{3,2,1,0:T(8,128)S(1)}, f32[8,4,8,768]{3,2,1,0:T(8,128)S(1)}, u32[]{:S(2)}, u32[]{:S(2)}) collective-permute-start(f32[8,4,8,768]{3,2,1,0:T(8,128)S(1)} %get-tuple-element.130), channel_id=1, source_target_pairs={{0,16},{1,17},{2,18},{3,19},{4,20},{5,21},{6,22},{7,23},{8,24},{9,... | collective-permute-start | bytes 2359304 | tf_op jit(solution)/shard_map/cond/branch_1_fun/ppermute | solution.py:43
  162.3 25.3 %collective-permute-start.21 = (f32[8,4,8,768]{3,2,1,0:T(8,128)S(1)}, f32[8,4,8,768]{3,2,1,0:T(8,128)S(1)}, u32[]{:S(2)}, u32[]{:S(2)}) collective-permute-start(f32[8,4,8,768]{3,2,1,0:T(8,128)S(1)} %get-tuple-element.131), channel_id=1, source_target_pairs={{0,2},{1,3},{2,0},{3,1},{4,6},{5,7},{6,4},{7,5},{8,10},{9,11},{10,... | collective-permute-start | bytes 2359304 | tf_op jit(solution)/shard_map/cond/branch_1_fun/ppermute | solution.py:43
  163.4 24.1 %collective-permute-start.19 = (f32[8,4,8,768]{3,2,1,0:T(8,128)S(1)}, f32[8,4,8,768]{3,2,1,0:T(8,128)S(1)}, u32[]{:S(2)}, u32[]{:S(2)}) collective-permute-start(f32[8,4,8,768]{3,2,1,0:T(8,128)S(1)} %get-tuple-element.129.refs_11_), channel_id=1, source_target_pairs={{0,8},{1,9},{2,10},{3,11},{4,12},{5,13},{6,14},{7,15},{8,0},{9,1},... | collective-permute-start | bytes 2359304 | tf_op jit(solution)/shard_map/cond/branch_1_fun/ppermute | solution.py:43
  164.0 17.7 %collective-permute-start.22 = (f32[1,2,8,768]{3,2,1,0:T(8,128)S(1)}, f32[1,2,8,768]{3,2,1,0:T(8,128)S(1)}, u32[]{:S(2)}, u32[]{:S(2)}) collective-permute-start(f32[1,2,8,768]{3,2,1,0:T(8,128)S(1)} %get-tuple-element.132.refs_9_), channel_id=1, source_target_pairs={{0,8},{1,9},{2,10},{3,11},{4,12},{5,13},{6,14},{7,15},{8,0},{9,1},... | collective-permute-start | bytes 147464 | tf_op jit(solution)/shard_map/cond/branch_1_fun/ppermute | solution.py:43
  188.3 28.3 %collective-permute-start.24 = (f32[4,4,8,768]{3,2,1,0:T(8,128)S(1)}, f32[4,4,8,768]{3,2,1,0:T(8,128)S(1)}, u32[]{:S(2)}, u32[]{:S(2)}) collective-permute-start(f32[4,4,8,768]{3,2,1,0:T(8,128)S(1)} %get-tuple-element.134), channel_id=1, source_target_pairs={{0,2},{1,3},{2,0},{3,1},{4,6},{5,7},{6,4},{7,5},{8,10},{9,11},{10,... | collective-permute-start | bytes 1179656 | tf_op jit(solution)/shard_map/cond/branch_1_fun/ppermute | solution.py:43
  190.2 26.5 %collective-permute-start.25 = (f32[4,4,8,768]{3,2,1,0:T(8,128)S(1)}, f32[4,4,8,768]{3,2,1,0:T(8,128)S(1)}, u32[]{:S(2)}, u32[]{:S(2)}) collective-permute-start(f32[4,4,8,768]{3,2,1,0:T(8,128)S(1)} %get-tuple-element.135), channel_id=1, source_target_pairs={{0,8},{1,9},{2,10},{3,11},{4,12},{5,13},{6,14},{7,15},{8,0},{9,1},... | collective-permute-start | bytes 1179656 | tf_op jit(solution)/shard_map/cond/branch_1_fun/ppermute | solution.py:43
  190.2 26.5 %collective-permute-start.23 = (f32[4,4,8,768]{3,2,1,0:T(8,128)S(1)}, f32[4,4,8,768]{3,2,1,0:T(8,128)S(1)}, u32[]{:S(2)}, u32[]{:S(2)}) collective-permute-start(f32[4,4,8,768]{3,2,1,0:T(8,128)S(1)} %get-tuple-element.133.refs_14_), channel_id=1, source_target_pairs={{0,16},{1,17},{2,18},{3,19},{4,20},{5,21},{6,22},{7,23},{8,24},{9,... | collective-permute-start | bytes 1179656 | tf_op jit(solution)/shard_map/cond/branch_1_fun/ppermute | solution.py:43
  190.4 50.6 %collective-permute-start.16 = (f32[6,8,3072]{2,1,0:T(8,128)S(1)}, f32[6,8,3072]{2,1,0:T(8,128)S(1)}, u32[]{:S(2)}, u32[]{:S(2)}) collective-permute-start(f32[6,8,3072]{2,1,0:T(8,128)S(1)} %sum_tiles.13.refs_8_.refs_0_.refs_2_.refs_4_), channel_id=1, source_target_pairs={{0,4},{1,5},{2,6},{3,7},{4,0},{5,1},{6,2},{7,3},{8,12},{9,13},{10,... | collective-permute-start | bytes 1769480 | tf_op jit(solution)/shard_map/cond/branch_1_fun/ppermute | solution.py:43
  191.6 13.3 %collective-permute-start.26 = (f32[1,2,8,768]{3,2,1,0:T(8,128)S(1)}, f32[1,2,8,768]{3,2,1,0:T(8,128)S(1)}, u32[]{:S(2)}, u32[]{:S(2)}) collective-permute-start(f32[1,2,8,768]{3,2,1,0:T(8,128)S(1)} %get-tuple-element.136.refs_12_), channel_id=1, source_target_pairs={{0,16},{1,17},{2,18},{3,19},{4,20},{5,21},{6,22},{7,23},{8,24},{9,... | collective-permute-start | bytes 147464 | tf_op jit(solution)/shard_map/cond/branch_1_fun/ppermute | solution.py:43
  217.4 22.7 %collective-permute-start.28 = (f32[2,4,8,768]{3,2,1,0:T(8,128)S(1)}, f32[2,4,8,768]{3,2,1,0:T(8,128)S(1)}, u32[]{:S(2)}, u32[]{:S(2)}) collective-permute-start(f32[2,4,8,768]{3,2,1,0:T(8,128)S(1)} %get-tuple-element.138), channel_id=1, source_target_pairs={{0,8},{1,9},{2,10},{3,11},{4,12},{5,13},{6,14},{7,15},{8,0},{9,1},... | collective-permute-start | bytes 589832 | tf_op jit(solution)/shard_map/cond/branch_1_fun/ppermute | solution.py:43
  217.5 22.6 %collective-permute-start.29 = (f32[2,4,8,768]{3,2,1,0:T(8,128)S(1)}, f32[2,4,8,768]{3,2,1,0:T(8,128)S(1)}, u32[]{:S(2)}, u32[]{:S(2)}) collective-permute-start(f32[2,4,8,768]{3,2,1,0:T(8,128)S(1)} %get-tuple-element.139), channel_id=1, source_target_pairs={{0,16},{1,17},{2,18},{3,19},{4,20},{5,21},{6,22},{7,23},{8,24},{9,... | collective-permute-start | bytes 589832 | tf_op jit(solution)/shard_map/cond/branch_1_fun/ppermute | solution.py:43
  217.5 22.6 %collective-permute-start.27 = (f32[2,4,8,768]{3,2,1,0:T(8,128)S(1)}, f32[2,4,8,768]{3,2,1,0:T(8,128)S(1)}, u32[]{:S(2)}, u32[]{:S(2)}) collective-permute-start(f32[2,4,8,768]{3,2,1,0:T(8,128)S(1)} %get-tuple-element.137.refs_17_), channel_id=1, source_target_pairs={{0,2},{1,3},{2,0},{3,1},{4,6},{5,7},{6,4},{7,5},{8,10},{9,11},{10,... | collective-permute-start | bytes 589832 | tf_op jit(solution)/shard_map/cond/branch_1_fun/ppermute | solution.py:43
  217.6 22.5 %collective-permute-start.30 = (f32[1,2,8,768]{3,2,1,0:T(8,128)S(1)}, f32[1,2,8,768]{3,2,1,0:T(8,128)S(1)}, u32[]{:S(2)}, u32[]{:S(2)}) collective-permute-start(f32[1,2,8,768]{3,2,1,0:T(8,128)S(1)} %get-tuple-element.140.refs_15_), channel_id=1, source_target_pairs={{0,2},{1,3},{2,0},{3,1},{4,6},{5,7},{6,4},{7,5},{8,10},{9,11},{10,... | collective-permute-start | bytes 147464 | tf_op jit(solution)/shard_map/cond/branch_1_fun/ppermute | solution.py:43
  241.6 11.1 %collective-permute-start.31 = (f32[2,8,3072]{2,1,0:T(8,128)S(1)}, f32[2,8,3072]{2,1,0:T(8,128)S(1)}, u32[]{:S(2)}, u32[]{:S(2)}) collective-permute-start(f32[2,8,3072]{2,1,0:T(8,128)S(1)} %get-tuple-element.142.refs_0_.refs_6_), channel_id=1, source_target_pairs={{0,2},{1,3},{2,0},{3,1},{4,6},{5,7},{6,4},{7,5},{8,10},{9,11},{10,... | collective-permute-start | bytes 589832 | tf_op jit(solution)/shard_map/cond/branch_1_fun/ppermute | solution.py:43
  244.0 8.7 %collective-permute-start.32 = (f32[2,8,3072]{2,1,0:T(8,128)S(1)}, f32[2,8,3072]{2,1,0:T(8,128)S(1)}, u32[]{:S(2)}, u32[]{:S(2)}) collective-permute-start(f32[2,8,3072]{2,1,0:T(8,128)S(1)} %get-tuple-element.143.refs_2_), channel_id=1, source_target_pairs={{0,8},{1,9},{2,10},{3,11},{4,12},{5,13},{6,14},{7,15},{8,0},{9,1},... | collective-permute-start | bytes 589832 | tf_op jit(solution)/shard_map/cond/branch_1_fun/ppermute | solution.py:43
  244.0 8.7 %collective-permute-start.33 = (f32[2,8,3072]{2,1,0:T(8,128)S(1)}, f32[2,8,3072]{2,1,0:T(8,128)S(1)}, u32[]{:S(2)}, u32[]{:S(2)}) collective-permute-start(f32[2,8,3072]{2,1,0:T(8,128)S(1)} %get-tuple-element.144.refs_4_), channel_id=1, source_target_pairs={{0,16},{1,17},{2,18},{3,19},{4,20},{5,21},{6,22},{7,23},{8,24},{9,... | collective-permute-start | bytes 589832 | tf_op jit(solution)/shard_map/cond/branch_1_fun/ppermute | solution.py:43
  253.5 15.1 %collective-permute-start.35 = (f32[4,8,3072]{2,1,0:T(8,128)S(1)}, f32[4,8,3072]{2,1,0:T(8,128)S(1)}, u32[]{:S(2)}, u32[]{:S(2)}) collective-permute-start(f32[4,8,3072]{2,1,0:T(8,128)S(1)} %bitcast.54), channel_id=1, source_target_pairs={{0,2},{1,3},{2,0},{3,1},{4,6},{5,7},{6,4},{7,5},{8,10},{9,11},{10,... | collective-permute-start | bytes 1179656 | tf_op jit(solution)/shard_map/cond/branch_1_fun/ppermute | solution.py:43
  255.0 13.7 %collective-permute-start.34 = (f32[4,8,3072]{2,1,0:T(8,128)S(1)}, f32[4,8,3072]{2,1,0:T(8,128)S(1)}, u32[]{:S(2)}, u32[]{:S(2)}) collective-permute-start(f32[4,8,3072]{2,1,0:T(8,128)S(1)} %bitcast.39), channel_id=1, source_target_pairs={{0,16},{1,17},{2,18},{3,19},{4,20},{5,21},{6,22},{7,23},{8,24},{9,... | collective-permute-start | bytes 1179656 | tf_op jit(solution)/shard_map/cond/branch_1_fun/ppermute | solution.py:43
  255.0 13.7 %collective-permute-start.36 = (f32[4,8,3072]{2,1,0:T(8,128)S(1)}, f32[4,8,3072]{2,1,0:T(8,128)S(1)}, u32[]{:S(2)}, u32[]{:S(2)}) collective-permute-start(f32[4,8,3072]{2,1,0:T(8,128)S(1)} %bitcast.56), channel_id=1, source_target_pairs={{0,8},{1,9},{2,10},{3,11},{4,12},{5,13},{6,14},{7,15},{8,0},{9,1},... | collective-permute-start | bytes 1179656 | tf_op jit(solution)/shard_map/cond/branch_1_fun/ppermute | solution.py:43
  269.8 32.7 %collective-permute-start.38 = (f32[8,8,3072]{2,1,0:T(8,128)S(1)}, f32[8,8,3072]{2,1,0:T(8,128)S(1)}, u32[]{:S(2)}, u32[]{:S(2)}) collective-permute-start(f32[8,8,3072]{2,1,0:T(8,128)S(1)} %bitcast.42), channel_id=1, source_target_pairs={{0,16},{1,17},{2,18},{3,19},{4,20},{5,21},{6,22},{7,23},{8,24},{9,... | collective-permute-start | bytes 2359304 | tf_op jit(solution)/shard_map/cond/branch_1_fun/ppermute | solution.py:43
  270.0 30.1 %collective-permute-start.40 = (f32[6,4,8,768]{3,2,1,0:T(8,128)S(1)}, f32[6,4,8,768]{3,2,1,0:T(8,128)S(1)}, u32[]{:S(2)}, u32[]{:S(2)}) collective-permute-start(f32[6,4,8,768]{3,2,1,0:T(8,128)S(1)} %get-tuple-element.141.refs_6_.refs_0_.refs_2_.refs_4_), channel_id=1, source_target_pairs={{0,4},{1,5},{2,6},{3,7},{4,0},{5,1},{6,2},{7,3},{8,12},{9,13},{10,... | collective-permute-start | bytes 1769480 | tf_op jit(solution)/shard_map/cond/branch_1_fun/ppermute | solution.py:43
  271.8 32.3 %collective-permute-start.37 = (f32[8,8,3072]{2,1,0:T(8,128)S(1)}, f32[8,8,3072]{2,1,0:T(8,128)S(1)}, u32[]{:S(2)}, u32[]{:S(2)}) collective-permute-start(f32[8,8,3072]{2,1,0:T(8,128)S(1)} %bitcast.30), channel_id=1, source_target_pairs={{0,8},{1,9},{2,10},{3,11},{4,12},{5,13},{6,14},{7,15},{8,0},{9,1},... | collective-permute-start | bytes 2359304 | tf_op jit(solution)/shard_map/cond/branch_1_fun/ppermute | solution.py:43
  272.9 31.2 %collective-permute-start.39 = (f32[8,8,3072]{2,1,0:T(8,128)S(1)}, f32[8,8,3072]{2,1,0:T(8,128)S(1)}, u32[]{:S(2)}, u32[]{:S(2)}) collective-permute-start(f32[8,8,3072]{2,1,0:T(8,128)S(1)} %bitcast.44), channel_id=1, source_target_pairs={{0,2},{1,3},{2,0},{3,1},{4,6},{5,7},{6,4},{7,5},{8,10},{9,11},{10,... | collective-permute-start | bytes 2359304 | tf_op jit(solution)/shard_map/cond/branch_1_fun/ppermute | solution.py:43
  273.2 26.9 %collective-permute-start.41 = (f32[1,2,8,768]{3,2,1,0:T(8,128)S(1)}, f32[1,2,8,768]{3,2,1,0:T(8,128)S(1)}, u32[]{:S(2)}, u32[]{:S(2)}) collective-permute-start(f32[1,2,8,768]{3,2,1,0:T(8,128)S(1)} %get-tuple-element.151.refs_6_), channel_id=1, source_target_pairs={{0,4},{1,5},{2,6},{3,7},{4,0},{5,1},{6,2},{7,3},{8,12},{9,13},{10,... | collective-permute-start | bytes 147464 | tf_op jit(solution)/shard_map/cond/branch_1_fun/ppermute | solution.py:43
  300.8 45.6 %copy-start.51 = (f32[1,2,8,768]{3,2,1,0:T(8,128)}, f32[1,2,8,768]{3,2,1,0:T(8,128)S(1)}, u32[]{:S(2)}) copy-start(f32[1,2,8,768]{3,2,1,0:T(8,128)S(1)} %get-tuple-element.165) | copy-start | bytes 147460 | tf_op jit(solution)/shard_map/cond
  300.8 6.5 %collective-permute-start.44 = (f32[2,4,8,768]{3,2,1,0:T(8,128)S(1)}, f32[2,4,8,768]{3,2,1,0:T(8,128)S(1)}, u32[]{:S(2)}, u32[]{:S(2)}) collective-permute-start(f32[2,4,8,768]{3,2,1,0:T(8,128)S(1)} %get-tuple-element.153.refs_2_), channel_id=1, source_target_pairs={{0,8},{1,9},{2,10},{3,11},{4,12},{5,13},{6,14},{7,15},{8,0},{9,1},... | collective-permute-start | bytes 589832 | tf_op jit(solution)/shard_map/cond/branch_1_fun/ppermute | solution.py:43
  301.9 5.4 %collective-permute-start.45 = (f32[2,4,8,768]{3,2,1,0:T(8,128)S(1)}, f32[2,4,8,768]{3,2,1,0:T(8,128)S(1)}, u32[]{:S(2)}, u32[]{:S(2)}) collective-permute-start(f32[2,4,8,768]{3,2,1,0:T(8,128)S(1)} %get-tuple-element.154.refs_4_), channel_id=1, source_target_pairs={{0,16},{1,17},{2,18},{3,19},{4,20},{5,21},{6,22},{7,23},{8,24},{9,... | collective-permute-start | bytes 589832 | tf_op jit(solution)/shard_map/cond/branch_1_fun/ppermute | solution.py:43
  302.5 5.5 %collective-permute-start.43 = (f32[2,4,8,768]{3,2,1,0:T(8,128)S(1)}, f32[2,4,8,768]{3,2,1,0:T(8,128)S(1)}, u32[]{:S(2)}, u32[]{:S(2)}) collective-permute-start(f32[2,4,8,768]{3,2,1,0:T(8,128)S(1)} %get-tuple-element.152.refs_6_.refs_0_), channel_id=1, source_target_pairs={{0,2},{1,3},{2,0},{3,1},{4,6},{5,7},{6,4},{7,5},{8,10},{9,11},{10,... | collective-permute-start | bytes 589832 | tf_op jit(solution)/shard_map/cond/branch_1_fun/ppermute | solution.py:43
  308.7 6.9 %collective-permute-start.47 = (f32[4,4,8,768]{3,2,1,0:T(8,128)S(1)}, f32[4,4,8,768]{3,2,1,0:T(8,128)S(1)}, u32[]{:S(2)}, u32[]{:S(2)}) collective-permute-start(f32[4,4,8,768]{3,2,1,0:T(8,128)S(1)} %bitcast.50), channel_id=1, source_target_pairs={{0,2},{1,3},{2,0},{3,1},{4,6},{5,7},{6,4},{7,5},{8,10},{9,11},{10,... | collective-permute-start | bytes 1179656 | tf_op jit(solution)/shard_map/cond/branch_1_fun/ppermute | solution.py:43
  309.4 6.6 %collective-permute-start.46 = (f32[4,4,8,768]{3,2,1,0:T(8,128)S(1)}, f32[4,4,8,768]{3,2,1,0:T(8,128)S(1)}, u32[]{:S(2)}, u32[]{:S(2)}) collective-permute-start(f32[4,4,8,768]{3,2,1,0:T(8,128)S(1)} %bitcast.36), channel_id=1, source_target_pairs={{0,16},{1,17},{2,18},{3,19},{4,20},{5,21},{6,22},{7,23},{8,24},{9,... | collective-permute-start | bytes 1179656 | tf_op jit(solution)/shard_map/cond/branch_1_fun/ppermute | solution.py:43
  310.8 6.9 %collective-permute-start.48 = (f32[4,4,8,768]{3,2,1,0:T(8,128)S(1)}, f32[4,4,8,768]{3,2,1,0:T(8,128)S(1)}, u32[]{:S(2)}, u32[]{:S(2)}) collective-permute-start(f32[4,4,8,768]{3,2,1,0:T(8,128)S(1)} %bitcast.52), channel_id=1, source_target_pairs={{0,8},{1,9},{2,10},{3,11},{4,12},{5,13},{6,14},{7,15},{8,0},{9,1},... | collective-permute-start | bytes 1179656 | tf_op jit(solution)/shard_map/cond/branch_1_fun/ppermute | solution.py:43
  318.6 12.7 %collective-permute-start.50 = (f32[8,4,8,768]{3,2,1,0:T(8,128)S(1)}, f32[8,4,8,768]{3,2,1,0:T(8,128)S(1)}, u32[]{:S(2)}, u32[]{:S(2)}) collective-permute-start(f32[8,4,8,768]{3,2,1,0:T(8,128)S(1)} %bitcast.46), channel_id=1, source_target_pairs={{0,16},{1,17},{2,18},{3,19},{4,20},{5,21},{6,22},{7,23},{8,24},{9,... | collective-permute-start | bytes 2359304 | tf_op jit(solution)/shard_map/cond/branch_1_fun/ppermute | solution.py:43
  318.7 14.9 %collective-permute-start.49 = (f32[8,4,8,768]{3,2,1,0:T(8,128)S(1)}, f32[8,4,8,768]{3,2,1,0:T(8,128)S(1)}, u32[]{:S(2)}, u32[]{:S(2)}) collective-permute-start(f32[8,4,8,768]{3,2,1,0:T(8,128)S(1)} %bitcast.33), channel_id=1, source_target_pairs={{0,8},{1,9},{2,10},{3,11},{4,12},{5,13},{6,14},{7,15},{8,0},{9,1},... | collective-permute-start | bytes 2359304 | tf_op jit(solution)/shard_map/cond/branch_1_fun/ppermute | solution.py:43
  320.2 13.5 %collective-permute-start.51 = (f32[8,4,8,768]{3,2,1,0:T(8,128)S(1)}, f32[8,4,8,768]{3,2,1,0:T(8,128)S(1)}, u32[]{:S(2)}, u32[]{:S(2)}) collective-permute-start(f32[8,4,8,768]{3,2,1,0:T(8,128)S(1)} %bitcast.48), channel_id=1, source_target_pairs={{0,2},{1,3},{2,0},{3,1},{4,6},{5,7},{6,4},{7,5},{8,10},{9,11},{10,... | collective-permute-start | bytes 2359304 | tf_op jit(solution)/shard_map/cond/branch_1_fun/ppermute | solution.py:43
  320.2 31.5 %collective-permute-start.42 = (f32[48,8,3072]{2,1,0:T(8,128)}, f32[48,8,3072]{2,1,0:T(8,128)}, u32[]{:S(2)}, u32[]{:S(2)}) collective-permute-start(f32[48,8,3072]{2,1,0:T(8,128)} %bitcast.9.refs_6_.part), channel_id=1, source_target_pairs={{0,1},{1,0},{2,3},{3,2},{4,5},{5,4},{6,7},{7,6},{8,9},{9,8},{10,11... | collective-permute-start | bytes 14155784 | tf_op jit(solution)/shard_map/cond/branch_1_fun/ppermute | solution.py:43
  336.8 19.4 %collective-permute-start.52 = (f32[48,4,8,768]{3,2,1,0:T(8,128)}, f32[48,4,8,768]{3,2,1,0:T(8,128)}, u32[]{:S(2)}, u32[]{:S(2)}) collective-permute-start(f32[48,4,8,768]{3,2,1,0:T(8,128)} %bitcast.16.part.refs_0_), channel_id=1, source_target_pairs={{0,1},{1,0},{2,3},{3,2},{4,5},{5,4},{6,7},{7,6},{8,9},{9,8},{10,11... | collective-permute-start | bytes 14155784 | tf_op jit(solution)/shard_map/cond/branch_1_fun/ppermute | solution.py:43
  (64 other events, 284.5 us)
Sparse Core Ops, SparseCore 0:
  27.4 238.9 all-reduce.1
where the time goes:
time: 378 us; the launch traced here: 377 us
  waiting for transfers between devices  137 us (36%)
  Pallas kernels  122 us (32%)
  starting transfers between devices  64.6 us (17%)
  local copies, waits for them, and re-layouts  37.2 us (10%)
  between operations  14.2 us (4%)
    ppermute x53, waiting for transfers between devices, swap(): return lax.ppermute(array, AXES, [(i, i ^ bit) for i in range(count)])  137 us
    ppermute x53, starting transfers between devices, swap(): return lax.ppermute(array, AXES, [(i, i ^ bit) for i in range(count)])  64.6 us
    cond x120, local copies, waits for them, and re-layouts  23.9 us
    pallas_call x4, Pallas kernels, put_half(): pl.pallas_call(kernel, grid_spec=pltpu.PrefetchScalarGridSpec(num_scalar_...  18.3 us
    pallas_call x1, Pallas kernels, attention(): pl.pallas_call(ordered(functools.partial(attention_kernel, size, partners...  17.6 us
    pallas_call x2, Pallas kernels, backward(): pl.pallas_call(ordered(functools.partial(backward_kernel, size, partners,...  16.4 us
    pallas_call x10, Pallas kernels, sum_tiles(): pl.pallas_call(kernel, grid_spec=pltpu.PrefetchScalarGridSpec(num_scalar_...  14.5 us
    pallas_call x1, Pallas kernels, mlp_part(): pl.pallas_call(mlp_kernel, grid=(hidden // tile,), in_specs=[full((rows,...  13.1 us
  transfers between devices with their start and end apart: 54, of which 22 were waited for; matrix products, arithmetic and copies ran while one was open for 1% of the time, Pallas kernels for 28%

commit v1 on v0

--- a/solution.py
+++ b/solution.py
@@ -19,9 +19,9 @@
 EXTRA = 16
 NN, NT, TN = ((1,), (0,)), ((1,), (1,)), ((0,), (0,))
 TILE = 8
-VMEM_LIMIT = 24 * 1024 * 1024
-STEP_LIMIT = 14 * 1024 * 1024
-BIG_LIMIT = 60 * 1024 * 1024
+MIB = 1024 * 1024
+STEP_LIMIT = 10 * MIB
+BIG_LIMIT = 60 * MIB
 FREE = pl.CostEstimate(flops=0, bytes_accessed=0, transcendentals=0)
 
 AXES = ("seq", "batch")
@@ -127,8 +127,8 @@
     return list(got)
 
 
-def interleave(bits, pairs, order, merge, block, deps):
-    count, shape = pairs[0][0].shape[0], pairs[0][0].shape[1:]
+def interleave(bits, pairs, count, order, merge, block, deps):
+    shape = pairs[0][0][0].shape[1:]
     groups = len(pairs)
     tail = (0,) * len(shape)
     flat = [x for pair in pairs for x in pair]
@@ -154,14 +154,17 @@
         grid_spec=pltpu.PrefetchScalarGridSpec(
             num_scalar_prefetch=1,
             grid=(count // block,),
-            in_specs=[block_spec(x.shape, block, lambda i, bits: i) for x in flat] + unused(deps),
+            in_specs=[
+                block_spec(x.shape, block, lambda i, bits, at=at: at // block + i) for x, at in flat
+            ]
+            + unused(deps),
             out_specs=out_specs,
         ),
         out_shape=out_shape,
         compiler_params=params(STEP_LIMIT),
         cost_estimate=FREE,
         name="interleave",
-    )(bits, *flat, *deps)
+    )(bits, *[x for x, _ in flat], *deps)
     if merge:
         return got[0].reshape((groups * 2 * count,) + shape)
     return [x.reshape((2 * count,) + shape) for x in got]
@@ -231,19 +234,27 @@
     return [(part.at[rows, m], piece) for m, piece in enumerate(pieces)]
 
 
+def block_of(count, most):
+    return max(b for b in range(1, most + 1) if count % b == 0)
+
+
 class Reduction:
-    def __init__(self, bits, send, keep, small=None):
+    def __init__(self, bits, send, keep, groups, small=None):
         core, seqs, rest = bit_groups()
-        ring = seqs + rest[:1]
+        ring = seqs + rest[:1] if groups == 3 else seqs
         self.bits = bits
         self.core, self.tail = core[0], rest[1:]
-        self.orders = [ring[k:] + ring[:k] for k in range(3)]
-        self.left = keep.shape[0] // 3
+        self.merged = None if groups == 3 else rest[0]
+        self.orders = [ring[k:] + ring[:k] for k in range(groups)]
+        self.last = len(ring) - 1
+        self.left = keep.shape[0] // groups
         came = swap(send, self.core)
-        self.terms = [[(keep, {0: g * self.left}), (came, {0: g * self.left})] for g in range(3)]
+        self.terms = [
+            [(keep, {0: g * self.left}), (came, {0: g * self.left})] for g in range(groups)
+        ]
         self.small = small
         if small is not None:
-            self.small_bits = ring + self.tail
+            self.small_bits = seqs + rest
             self.small_came = swap(small, self.core)
 
     def small_output(self):
@@ -258,21 +269,36 @@
 
     def scatter(self, step, deps):
         self.left //= 2
+        block = block_of(self.left, max(min(3, self.left // 2), 1))
         outputs = []
         for g, order in enumerate(self.orders):
             bit = order[step]
             terms = [
                 (t, shifted(shifted(at, 0, self.left), bit, -self.left)) for t, at in self.terms[g]
             ]
-            outputs.append((min(2, max(self.left // 2, 1)), [(self.left, terms)]))
+            outputs.append((block, [(self.left, terms)]))
         sends = sum_tiles(self.bits, outputs + self.small_output(), deps)
         for g, order in enumerate(self.orders):
             bit = order[step]
             came = swap(sends[g], bit)
             self.terms[g] = [(t, shifted(at, bit, self.left)) for t, at in self.terms[g]]
             self.terms[g].append((came, {}))
-        self.small_next(sends[3:])
+        self.small_next(sends[len(self.orders) :])
         return sends[:1]
+
+    def merge(self, deps):
+        self.left //= 2
+        bit, segments = self.merged, []
+        for terms in self.terms:
+            terms = [(t, shifted(shifted(at, 0, self.left), bit, -self.left)) for t, at in terms]
+            segments.append((self.left, terms))
+        send, *small = sum_tiles(self.bits, [(self.left, segments)] + self.small_output(), deps)
+        self.small_next(small)
+        came = swap(send, bit)
+        for g, terms in enumerate(self.terms):
+            self.terms[g] = [(t, shifted(at, bit, self.left)) for t, at in terms]
+            self.terms[g].append((came, {0: g * self.left}))
+        return [send]
 
     def exchange(self, deps):
         segments = [(self.left, terms) for terms in self.terms]
@@ -287,24 +313,44 @@
         return [first]
 
     def settle(self, deps):
-        outputs = [
-            (self.left, [(self.left, [(x, {0: g * self.left}) for x in self.both])])
-            for g in range(3)
-        ]
-        self.pieces = sum_tiles(self.bits, outputs + self.small_output(), deps)
-        self.small_next(self.pieces[3:])
-        self.pieces = self.pieces[:3]
-        self.next_swap(2)
+        groups = len(self.orders)
+        if self.merged:
+            count = groups * self.left
+            outputs = [(self.left, [(count, [(x, {}) for x in self.both])])]
+        else:
+            outputs = [
+                (self.left, [(self.left, [(x, {0: g * self.left}) for x in self.both])])
+                for g in range(groups)
+            ]
+        got = sum_tiles(self.bits, outputs + self.small_output(), deps)
+        self.pieces = got[: len(outputs)]
+        self.small_next(got[len(outputs) :])
+        if self.merged:
+            self.came = [swap(self.pieces[0], self.merged)]
+        else:
+            self.next_swap(self.last)
         return self.pieces[:1]
 
     def next_swap(self, step):
         self.came = [swap(p, order[step]) for p, order in zip(self.pieces, self.orders)]
 
+    def unmerge(self, deps):
+        groups = len(self.orders)
+        pairs = [
+            ((self.pieces[0], g * self.left), (self.came[0], g * self.left)) for g in range(groups)
+        ]
+        self.pieces = interleave(
+            self.bits, pairs, self.left, [self.merged] * groups, False, self.left, deps
+        )
+        self.next_swap(self.last)
+        return self.pieces[:1]
+
     def gather(self, step, deps):
-        pairs = list(zip(self.pieces, self.came))
+        pairs = [((a, 0), (b, 0)) for a, b in zip(self.pieces, self.came)]
+        count = self.pieces[0].shape[0]
         order = [o[step] for o in self.orders]
-        block = max(pairs[0][0].shape[0] // 4, 1) if step == 0 else max(pairs[0][0].shape[0] // 2, 1)
-        self.pieces = interleave(self.bits, pairs, order, step == 0, block, deps)
+        block = block_of(count, max(min(3, count // 2), 1))
+        self.pieces = interleave(self.bits, pairs, count, order, step == 0, block, deps)
         if step:
             self.next_swap(step - 1)
             return self.pieces[:1]
@@ -340,8 +386,8 @@
     return lax.dot_general(a, b, (dims, ((), ())), preferred_element_type=F32, precision=precision)
 
 
-def params(limit=None):
-    return pltpu.CompilerParams(vmem_limit_bytes=limit or VMEM_LIMIT)
+def params(limit):
+    return pltpu.CompilerParams(vmem_limit_bytes=limit)
 
 
 def ordered(kernel, count, deps):
@@ -461,7 +507,7 @@
             pltpu.HBM((hidden, width), F32),
             jax.ShapeDtypeStruct((1, hidden), F32),
         ),
-        compiler_params=params(),
+        compiler_params=params(18 * MIB),
         name="mlp",
     )(second, cot, up, up_bias, down)
 
@@ -490,7 +536,7 @@
             out_specs=pl.BlockSpec((half // TILE, TILE, tile), lambda j, bits: (0, 0, j)),
         ),
         out_shape=jax.ShapeDtypeStruct((half // TILE, TILE, hidden), F32),
-        compiler_params=params(),
+        compiler_params=params(10 * MIB),
         cost_estimate=FREE,
         name="up_half",
     )(bits, second_t, d_hidden, *deps)
@@ -528,7 +574,7 @@
         + unused(deps),
         out_specs=[full((rows, width)), full((rows, width))],
         out_shape=(wide, wide),
-        compiler_params=params(),
+        compiler_params=params(14 * MIB),
         cost_estimate=FREE,
         name="mlp_tail",
     )(active, d_hidden, up, down, *deps)
@@ -544,7 +590,7 @@
         ordered(result_kernel, 6, deps),
         in_specs=[pl.BlockSpec()] * 6 + unused(deps),
         out_shape=jax.ShapeDtypeStruct(tok.shape, B16),
-        compiler_params=params(),
+        compiler_params=params(10 * MIB),
         cost_estimate=FREE,
         name="results",
     )(tok, att, w_out, mlp_out, out_bias, down_bias, *deps)
@@ -633,7 +679,7 @@
             low, low, low, wide, wide,
             jax.ShapeDtypeStruct((steps * pairs, size + EXTRA, 2 * size), F32),
         ),
-        compiler_params=params(),
+        compiler_params=params(14 * MIB),
         cost_estimate=FREE,
         name="features",
     )(first_t, in_weight, in_weight, in_weight, vec, proj_t, angle, seg, start, *deps)
@@ -787,7 +833,7 @@
         ),
         scratch_shapes=[pltpu.VMEM((length, length), F32)],
         input_output_aliases={9 + partners + k: k for k in range(len(so_far))},
-        compiler_params=params(),
+        compiler_params=params(16 * MIB),
         cost_estimate=FREE,
         name="attention",
     )(place, start, q_feat, k_feat, v_low, w_out, cot, seg, seg_col, *came, *so_far, *deps)
@@ -951,7 +997,7 @@
             jax.ShapeDtypeStruct(tok.shape, B16),
         ][: 4 + closes],
         input_output_aliases={24 + partners + len(carried) + k: k for k in range(len(kept))},
-        compiler_params=params(),
+        compiler_params=params(20 * MIB),
         cost_estimate=FREE,
         name="backward",
     )(dq, dk, dv, k_feat, v_low, scaled, expo, vec, in_weight, in_weight, in_weight, first_t,
@@ -1006,7 +1052,7 @@
     def rest(first_t, second_t, active, d_hidden):
         up_send = up_half(bits, core, False, second_t, d_hidden, [])
         up_keep = up_half(bits, core, True, second_t, d_hidden, [up_send])
-        up = Reduction(bits, up_send, up_keep)
+        up = Reduction(bits, up_send, up_keep, 3)
         q_feat, k_feat, v_low, scaled, expo, summary = features(
             first_t, input_weight, vec, proj_t, angle, seg, start, size, [up_keep]
         )
@@ -1028,7 +1074,7 @@
         some = list(backward(*fixed, (0, groups - 1), [], last))
         last = up.scatter(2, some[:1])
         send, keep, small, _, tok_grad = backward(*fixed, (groups - 1, 1), some, last)
-        attn = Reduction(bits, send, keep, small.reshape(1, 2, 8, width))
+        attn = Reduction(bits, send, keep, 3, small.reshape(1, 2, 8, width))
         last = up.exchange([tok_grad])
         last = attn.scatter(0, last)
         last = attn.scatter(1, last)
@@ -1036,12 +1082,12 @@
         last = attn.exchange(last)
         last = up.settle(last)
         last = up.gather(2, last)
+        last = attn.settle(last)
         last = up.gather(1, last)
-        last = attn.settle(last)
+        last = attn.gather(2, last)
         last = up.gather(0, last)
-        last = attn.gather(2, last)
+        last = attn.gather(1, last)
         last = up.finish_own(move_up, up_shapes, last)
-        last = attn.gather(1, last)
         last = attn.gather(0, last)
         last = attn.finish_own(move_attention, attn_shapes, last)
         (up_sum,) = up.finish(move_up, up_shapes, last)

time: 378 us -> 372 us (0.984)
  local copies, waits for them, and re-layouts: 37.2 us -> 27.6 us
  waiting for transfers between devices: 137 us -> 142 us
    cond x120 -> x96, local copies, waits for them, and re-layouts: 23.9 us -> 13.5 us
    ppermute x53, waiting for transfers between devices: 137 us -> 142 us  [swap(): return lax.ppermute(array, AXES, [(i, i ^ bit) for i in range(count)])]
  transfers between devices with their start and end apart: 54 -> 54, of which waited for: 22 -> 21; matrix products, arithmetic and copies ran while one was open for 1% -> 1% of each run, Pallas kernels for 28% -> 28%
where the time goes in v1:
time: 372 us
  waiting for transfers between devices  142 us (38%)
  Pallas kernels  120 us (32%)
  starting transfers between devices  64.9 us (17%)
  local copies, waits for them, and re-layouts  27.6 us (7%)
  between operations  14.2 us (4%)
    ppermute x53, waiting for transfers between devices, swap(): return lax.ppermute(array, AXES, [(i, i ^ bit) for i in range(count)])  142 us
    ppermute x53, starting transfers between devices, swap(): return lax.ppermute(array, AXES, [(i, i ^ bit) for i in range(count)])  64.9 us
    pallas_call x4, Pallas kernels, put_half(): pl.pallas_call(kernel, grid_spec=pltpu.PrefetchScalarGridSpec(num_scalar_...  18.3 us
    pallas_call x1, Pallas kernels, attention(): pl.pallas_call(ordered(functools.partial(attention_kernel, size, partners...  17.6 us
    pallas_call x2, Pallas kernels, backward(): pl.pallas_call(ordered(functools.partial(backward_kernel, size, partners,...  16.1 us
    pallas_call x10, Pallas kernels, sum_tiles(): pl.pallas_call(kernel, grid_spec=pltpu.PrefetchScalarGridSpec(num_scalar_...  14.2 us
    cond x96, local copies, waits for them, and re-layouts  13.5 us
    pallas_call x1, Pallas kernels, mlp_part(): pl.pallas_call(mlp_kernel, grid=(hidden // tile,), in_specs=[full((rows,...  13.1 us
  transfers between devices with their start and end apart: 54, of which 21 were waited for; matrix products, arithmetic and copies ran while one was open for 1% of the time, Pallas kernels for 28%

profile of v1, /device:TPU:1, one launch (start us, length us, event | category | flops | bytes accessed | tf_op | source)
XLA Modules:
  0.0 371.6 jit_solution(17011499513039608990)
XLA Ops:
  7.2 1.4 reshape.116.feat_weight
  8.6 3.5 norms.1
  13.9 13.1 %mlp.1 = (bf16[512,3072]{1,0:T(8,128)(2,1)}, bf16[512,3072]{1,0:T(8,128)(2,1)S(1)}, f32[3072,768]{1,0:T(8,128)}, f32[1,3072]{1,0:T(1,128)S(1)}) custom-call(bf16[512,768]{1,0:T(8,128)(2,1)S(1)} %copy-done.26, bf16[512,768]{1,0:T(8,128)(2,1)} %bitcast.60, bf16[768,3072]{1,0:T(8,128)(2,1)} %up.1, f32[1,3072]{1,0:T(1,128)S(1)} %copy-done.27, bf16[3072,768]{1,0:T(8,128)(2,1)} %down.1), custom_call_target="tpu_custom_call" | custom-call | tf_op jit(solution)/shard_map/mlp/pallas_call | solution.py:488
  28.3 327.5 %conditional.1 = (f32[768,3072]{1,0:T(8,128)}, f32[768,2304]{1,0:T(8,128)}, f32[768,768]{1,0:T(8,128)}, f32[16,768]{1,0:T(8,128)}, bf16[1,512,768]{2,1,0:T(8,128...) conditional(s32[]{:T(128)} %bitcast.23, () %tuple.27, ...), branch_computations={%region_0.0_spmd, %region_1.0_spmd} | conditional | flops 4620 | bytes 423209344 | solution.py:1104
  29.8 4.3 %up_half.2.refs_3_ = f32[48,8,3072]{2,1,0:T(8,128)S(1)} custom-call(s32[5]{0:T(128)S(1)} %shift-right-arithmetic_and_fusion.refs_0_._.refs_26_.bits, bf16[768,512]{1,0:T(8,128)(2,1)} %get-tuple-element.78.refs_1_, bf16[512,3072]{1,0:T(8,128)(2,1)S(1)} %get-tuple-element.79.refs_2_.refs_1_), custom_call_target="tpu_custom_call" | custom-call | tf_op jit(solution)/shard_map/cond/branch_1_fun/up_half/pallas_call | solution.py:526
  34.3 3.3 up_half.3.refs_9_.refs_0_.refs_2_.refs_4_.refs_3_.refs_6_.refs_8_.refs_5_.refs_10_
  37.7 8.1 %features.1 = (bf16[768,512]{1,0:T(8,128)(2,1)S(1)}, bf16[768,512]{1,0:T(8,128)(2,1)S(1)}, bf16[768,512]{1,0:T(8,128)(2,1)S(1)}, f32[2,768,512]{2,1,0:T(8,128)S(...) custom-call(bf16[768,512]{1,0:T(8,128)(2,1)S(1)} %copy-done.34, bf16[768,2304]{1,0:T(8,128)(2,1)S(1)} %copy-done.28, ...), custom_call_target="tpu_custom_call" | custom-call | tf_op jit(solution)/shard_map/cond/branch_1_fun/features/pallas_call | solution.py:662
  45.7 1.7 copy-done.3
  48.4 3.6 collective-permute-start.3
  52.4 8.5 %mlp_tail.1 = (f32[512,768]{1,0:T(8,128)S(1)}, f32[512,768]{1,0:T(8,128)S(1)}) custom-call(bf16[512,3072]{1,0:T(8,128)(2,1)S(1)} %copy-done.36, bf16[512,3072]{1,0:T(8,128)(2,1)S(1)} %copy-done.31, bf16[768,3072]{1,0:T(8,128)(2,1)S(1)} %bitcast.63, bf16[3072,768]{1,0:T(8,128)(2,1)S(1)} %bitcast.65, f32[6,80,128]{2,1,0:T(8,128)S(1)} %get-tuple-element.90.refs_4_), custom_call_target="tpu_custom_call" | custom-call | tf_op jit(solution)/shard_map/cond/branch_1_fun/mlp_tail/pallas_call | solution.py:565
  60.8 1.2 copy-done.13
  62.3 6.8 %collective-permute-done.2.refs_8_.refs_10_ = f32[6,80,128]{2,1,0:T(8,128)S(1)} collective-permute-done((f32[6,80,128]{2,1,0:T(8,128)S(1)}, f32[6,80,128]{2,1,0:T(8,128)S(1)}, u32[]{:S(2)}, u32[]{:S(2)}) %collective-permute-start.2) | collective-permute-done | bytes 245792 | tf_op jit(solution)/shard_map/cond/branch_1_fun/ppermute | solution.py:43
  70.1 3.0 sum_tiles.10
  73.8 1.3 collective-permute-start.6
  76.8 1.3 copy-done.6
  78.1 1.4 copy-done.9
  84.4 17.6 %attention.1 = (bf16[768,512]{1,0:T(8,128)(2,1)S(1)}, f32[768,512]{1,0:T(8,128)S(1)}, f32[768,512]{1,0:T(8,128)S(1)}, f32[768,512]{1,0:T(8,128)S(1)}, f32[6,80,1...) custom-call(s32[1]{0:T(128)} %get-tuple-element.96.refs_0_, s32[1]{0:T(128)S(1)} %bitcast.76, bf16[768,512]{1,0:T(8,128)(2,1)S(1)} %copy-done.25, ...), custom_call_target="tpu_custom_call" | custom-call | tf_op jit(solution)/shard_map/cond/branch_1_fun/attention/pallas_call | solution.py:815
  102.0 1.3 collective-permute-start.9
  103.9 5.1 %collective-permute-done.9.refs_12_.refs_23_ = f32[6,80,128]{2,1,0:T(8,128)S(1)} collective-permute-done((f32[6,80,128]{2,1,0:T(8,128)S(1)}, f32[6,80,128]{2,1,0:T(8,128)S(1)}, u32[]{:S(2)}, u32[]{:S(2)}) %collective-permute-start.9) | collective-permute-done | bytes 245792 | tf_op jit(solution)/shard_map/cond/branch_1_fun/ppermute | solution.py:43
  109.8 1.4 copy-done.16
  111.2 3.3 results.1.refs_9_
  114.6 1.5 collective-permute-done.8.refs_11_.refs_22_
  116.1 2.8 sum_tiles.11
  121.0 8.8 %backward.2 = (f32[48,4,8,768]{3,2,1,0:T(8,128)S(1)}, f32[48,4,8,768]{3,2,1,0:T(8,128)S(1)}, f32[16,768]{1,0:T(8,128)S(1)}, f32[768,512]{1,0:T(8,128)S(1)}) custom-call(f32[768,512]{1,0:T(8,128)S(1)} %get-tuple-element.109.refs_0_, f32[768,512]{1,0:T(8,128)S(1)} %get-tuple-element.110.refs_1_, f32[768,512]{1,0:T(8,128)S(1)} %get-tuple-element.111.refs_2_, ...), custom_call_target="tpu_custom_call" | custom-call | tf_op jit(solution)/shard_map/cond/branch_1_fun/backward/pallas_call | solution.py:964
  129.9 2.2 collective-permute-done.11.refs_7_.refs_8_
  132.0 1.8 sum_tiles.12
  133.9 7.3 %backward.3 = (f32[48,4,8,768]{3,2,1,0:T(8,128)S(1)}, f32[48,4,8,768]{3,2,1,0:T(8,128)S(1)}, f32[16,768]{1,0:T(8,128)S(1)}, f32[768,512]{1,0:T(8,128)}, bf16[512,768]{1,0:T(8,128)(2,1)}) custom-call(f32[768,512]{1,0:T(8,128)S(1)} %get-tuple-element.109.refs_0_, ...), custom_call_target="tpu_custom_call", output_to_operand_aliasing={{0}: (29, {}), {1}: (30, {})} | custom-call | tf_op jit(solution)/shard_map/cond/branch_1_fun/backward/pallas_call | solution.py:964
  141.1 1.5 collective-permute-start.17
  145.6 3.5 collective-permute-done.14.refs_9_
  149.6 1.3 collective-permute-done.13.refs_4_
  150.9 2.0 sum_tiles.13.refs_8_.refs_0_.refs_2_.refs_4_
  155.4 1.2 collective-permute-start.19
  156.9 24.3 %collective-permute-done.22.refs_10_ = f32[1,2,8,768]{3,2,1,0:T(8,128)S(1)} collective-permute-done((f32[1,2,8,768]{3,2,1,0:T(8,128)S(1)}, f32[1,2,8,768]{3,2,1,0:T(8,128)S(1)}, u32[]{:S(2)}, u32[]{:S(2)}) %collective-permute-start.22) | collective-permute-done | bytes 49184 | tf_op jit(solution)/shard_map/cond/branch_1_fun/ppermute | solution.py:43
  181.2 2.0 collective-permute-done.21.refs_8_.refs_10_.refs_12_
  184.1 1.6 collective-permute-start.25
  185.7 1.4 collective-permute-start.16
  187.1 1.2 collective-permute-start.26
  188.4 14.8 %collective-permute-done.26.refs_13_ = f32[1,2,8,768]{3,2,1,0:T(8,128)S(1)} collective-permute-done((f32[1,2,8,768]{3,2,1,0:T(8,128)S(1)}, f32[1,2,8,768]{3,2,1,0:T(8,128)S(1)}, u32[]{:S(2)}, u32[]{:S(2)}) %collective-permute-start.26) | collective-permute-done | bytes 49184 | tf_op jit(solution)/shard_map/cond/branch_1_fun/ppermute | solution.py:43
  203.2 1.9 collective-permute-done.24.refs_7_.refs_8_
  205.8 1.6 collective-permute-start.28
  207.5 1.5 collective-permute-start.30
  208.9 21.5 %collective-permute-done.30.refs_16_ = f32[1,2,8,768]{3,2,1,0:T(8,128)S(1)} collective-permute-done((f32[1,2,8,768]{3,2,1,0:T(8,128)S(1)}, f32[1,2,8,768]{3,2,1,0:T(8,128)S(1)}, u32[]{:S(2)}, u32[]{:S(2)}) %collective-permute-start.30) | collective-permute-done | bytes 49184 | tf_op jit(solution)/shard_map/cond/branch_1_fun/ppermute | solution.py:43
  232.0 2.4 collective-permute-start.31
  234.4 2.0 collective-permute-start.32
  236.4 7.2 %collective-permute-done.31.refs_1_ = f32[2,8,3072]{2,1,0:T(8,128)S(1)} collective-permute-done((f32[2,8,3072]{2,1,0:T(8,128)S(1)}, f32[2,8,3072]{2,1,0:T(8,128)S(1)}, u32[]{:S(2)}, u32[]{:S(2)}) %collective-permute-start.31) | collective-permute-done | bytes 196640 | tf_op jit(solution)/shard_map/cond/branch_1_fun/ppermute | solution.py:43
  244.7 3.2 collective-permute-start.36
  247.9 31.8 %collective-permute-done.38.refs_7_ = f32[1,2,8,768]{3,2,1,0:T(8,128)S(1)} collective-permute-done((f32[1,2,8,768]{3,2,1,0:T(8,128)S(1)}, f32[1,2,8,768]{3,2,1,0:T(8,128)S(1)}, u32[]{:S(2)}, u32[]{:S(2)}) %collective-permute-start.38) | collective-permute-done | bytes 49184 | tf_op jit(solution)/shard_map/cond/branch_1_fun/ppermute | solution.py:43
  281.6 1.6 collective-permute-start.43
  283.3 2.7 collective-permute-start.41
  286.8 2.2 collective-permute-start.42
  289.0 10.9 %collective-permute-done.44.refs_5_ = f32[2,4,8,768]{3,2,1,0:T(8,128)S(1)} collective-permute-done((f32[2,4,8,768]{3,2,1,0:T(8,128)S(1)}, f32[2,4,8,768]{3,2,1,0:T(8,128)S(1)}, u32[]{:S(2)}, u32[]{:S(2)}) %collective-permute-start.44) | collective-permute-done | bytes 196640 | tf_op jit(solution)/shard_map/cond/branch_1_fun/ppermute | solution.py:43
  299.9 3.1 collective-permute-done.42.refs_1_
  303.8 2.3 collective-permute-start.47
  307.1 1.3 collective-permute-start.48
  308.4 3.2 interleave.9
  312.7 1.3 collective-permute-done.48.refs_5_
  316.7 9.0 %collective-permute-start.45 = (f32[48,8,3072]{2,1,0:T(8,128)}, f32[48,8,3072]{2,1,0:T(8,128)}, u32[]{:S(2)}, u32[]{:S(2)}) collective-permute-start(f32[48,8,3072]{2,1,0:T(8,128)} %bitcast.10.refs_6_.part), channel_id=1, source_target_pairs={{0,1},{1,0},{2,3},{3,2},{4,5},{5,4},{6,7},{7,6},{8,9},{9,8},{10,11... | collective-permute-start | bytes 14155784 | tf_op jit(solution)/shard_map/cond/branch_1_fun/ppermute | solution.py:43
  325.7 4.5 %put_half.4.refs_6_.refs_0_ = f32[2,48,8,3072]{3,2,1,0:T(8,128)} custom-call(s32[5]{0:T(128)S(1)} %shift-right-arithmetic_and_fusion.refs_0_._.refs_26_.bits, f32[48,8,3072]{2,1,0:T(8,128)} %bitcast.10.refs_6_.part, f32[8,4,8,768]{3,2,1,0:T(8,128)S(1)} %bitcast.31), custom_call_target="tpu_custom_call" | custom-call | tf_op jit(solution)/shard_map/cond/branch_1_fun/put_half/pallas_call | solution.py:204
  330.2 3.2 interleave.11
  333.5 7.5 %collective-permute-start.52 = (f32[48,4,8,768]{3,2,1,0:T(8,128)}, f32[48,4,8,768]{3,2,1,0:T(8,128)}, u32[]{:S(2)}, u32[]{:S(2)}) collective-permute-start(f32[48,4,8,768]{3,2,1,0:T(8,128)} %bitcast.16.part.refs_0_), channel_id=1, source_target_pairs={{0,1},{1,0},{2,3},{3,2},{4,5},{5,4},{6,7},{7,6},{8,9},{9,8},{10,11... | collective-permute-start | bytes 14155784 | tf_op jit(solution)/shard_map/cond/branch_1_fun/ppermute | solution.py:43
  341.7 4.6 %put_half.5 = (f32[2,48,8,2304]{3,2,1,0:T(8,128)}, f32[2,48,8,768]{3,2,1,0:T(8,128)}) custom-call(s32[5]{0:T(128)S(1)} %shift-right-arithmetic_and_fusion.refs_0_._.refs_26_.bits, f32[48,4,8,768]{3,2,1,0:T(8,128)} %bitcast.16.part.refs_0_, f32[48,4,8,768]{3,2,1,0:T(8,128)} %bitcast.16.part.refs_0_), custom_call_target="tpu_custom_call" | custom-call | tf_op jit(solution)/shard_map/cond/branch_1_fun/put_half/pallas_call | solution.py:204
  346.4 4.5 %put_half.6 = f32[2,48,8,3072]{3,2,1,0:T(8,128)} custom-call(s32[5]{0:T(128)S(1)} %shift-right-arithmetic_and_fusion.refs_0_._.refs_26_.bits, f32[48,8,3072]{2,1,0:T(8,128)} %collective-permute-done.45.part, f32[2,48,8,3072]{3,2,1,0:T(8,128)} %put_half.4.refs_6_.refs_0_, ...), custom_call_target="tpu_custom_call", output_to_operand_aliasing={{}: (2, {})} | custom-call | tf_op jit(solution)/shard_map/cond/branch_1_fun/put_half/pallas_call | solution.py:204
  350.9 4.7 %put_half.7 = (f32[2,48,8,2304]{3,2,1,0:T(8,128)}, f32[2,48,8,768]{3,2,1,0:T(8,128)}) custom-call(s32[5]{0:T(128)S(1)} %shift-right-arithmetic_and_fusion.refs_0_._.refs_26_.bits, f32[48,4,8,768]{3,2,1,0:T(8,128)} %collective-permute-done.52.part, ...), custom_call_target="tpu_custom_call", output_to_operand_aliasing={{0}: (2, {}), {1}: (3, {})} | custom-call | tf_op jit(solution)/shard_map/cond/branch_1_fun/put_half/pallas_call | solution.py:204
  356.5 8.1 %copy.98 = f32[3072,768]{1,0:T(8,128)} copy(f32[3072,768]{1,0:T(8,128)} %all-reduce.2.cloned.1.call-done) | data formatting | bytes 18874368
  (215 shorter events, 38.1 us)
Async XLA Ops:
  7.2 348.8 %all-reduce.2.cloned.1.call-start = ((), (), s32[]{:S(2)}) async-start(), calls=%async_computation | async-start | bytes 18874368 | tf_op jit(solution)/shard_map/psum | solution.py:1046
  34.1 35.9 %collective-permute-start = (f32[48,8,3072]{2,1,0:T(8,128)S(1)}, f32[48,8,3072]{2,1,0:T(8,128)S(1)}, u32[]{:S(2)}, u32[]{:S(2)}) collective-permute-start(f32[48,8,3072]{2,1,0:T(8,128)S(1)} %up_half.2.refs_3_), channel_id=1, source_target_pairs={{0,1},{1,0},{2,3},{3,2},{4,5},{5,4},{6,7},{7,6},{8,9},{9,8},{10,11... | collective-permute-start | bytes 14155784 | tf_op jit(solution)/shard_map/cond/branch_1_fun/ppermute | solution.py:43
  34.3 18.1 %slice-start.2 = ((s8[4718592]{0:T(1024)(128)(4,1)}), s8[4194304]{0:T(1024)(128)(4,1)S(1)}, s32[]{:S(2)}) async-start(s8[4718592]{0:T(1024)(128)(4,1)} %bitcast.62), calls=%async_computation.3 | async-start | bytes 8388608 | tf_op jit(solution)/shard_map/cond
  34.3 18.1 %slice-start.4 = ((s8[4718592]{0:T(1024)(128)(4,1)}), s8[4194304]{0:T(1024)(128)(4,1)S(1)}, s32[]{:S(2)}) async-start(s8[4718592]{0:T(1024)(128)(4,1)} %bitcast.64), calls=%async_computation.5 | async-start | bytes 8388608 | tf_op jit(solution)/shard_map/cond
  37.6 32.5 %copy-start = (f32[48,8,3072]{2,1,0:T(8,128)}, f32[48,8,3072]{2,1,0:T(8,128)S(1)}, u32[]{:S(2)}) copy-start(f32[48,8,3072]{2,1,0:T(8,128)S(1)} %up_half.3.refs_9_.refs_0_.refs_2_.refs_4_.refs_3_.refs_6_.refs_8_.refs_5_.refs_10_) | copy-start | bytes 14155780 | tf_op jit(solution)/shard_map/cond
  37.6 14.7 %copy-start.31 = (bf16[512,3072]{1,0:T(8,128)(2,1)S(1)}, bf16[512,3072]{1,0:T(8,128)(2,1)}, u32[]{:S(2)}) copy-start(bf16[512,3072]{1,0:T(8,128)(2,1)} %copy-done.30) | copy-start | bytes 9437188 | tf_op jit(solution)/shard_map/cond
  37.6 14.7 %slice-start.3 = ((s8[4718592]{0:T(1024)(128)(4,1)}), s8[524288]{0:T(1024)(128)(4,1)S(1)}, s32[]{:S(2)}) async-start(s8[4718592]{0:T(1024)(128)(4,1)} %bitcast.62), calls=%async_computation.4 | async-start | bytes 1048576 | tf_op jit(solution)/shard_map/cond
  48.4 13.9 %collective-permute-start.3 = (f32[6,80,128]{2,1,0:T(8,128)S(1)}, f32[6,80,128]{2,1,0:T(8,128)S(1)}, u32[]{:S(2)}, u32[]{:S(2)}) collective-permute-start(f32[6,80,128]{2,1,0:T(8,128)S(1)} %get-tuple-element.90.refs_4_), channel_id=1, source_target_pairs={{0,24},{1,25},{2,26},{3,27},{4,28},{5,29},{6,30},{7,31},{8,16},{9,... | collective-permute-start | bytes 737288 | tf_op jit(solution)/shard_map/cond/branch_1_fun/ppermute | solution.py:43
  52.0 17.1 %collective-permute-start.2 = (f32[6,80,128]{2,1,0:T(8,128)S(1)}, f32[6,80,128]{2,1,0:T(8,128)S(1)}, u32[]{:S(2)}, u32[]{:S(2)}) collective-permute-start(f32[6,80,128]{2,1,0:T(8,128)S(1)} %get-tuple-element.90.refs_4_), channel_id=1, source_target_pairs={{0,16},{1,17},{2,18},{3,19},{4,20},{5,21},{6,22},{7,23},{8,24},{9,... | collective-permute-start | bytes 737288 | tf_op jit(solution)/shard_map/cond/branch_1_fun/ppermute | solution.py:43
  52.2 17.8 %collective-permute-start.1 = (f32[6,80,128]{2,1,0:T(8,128)S(1)}, f32[6,80,128]{2,1,0:T(8,128)S(1)}, u32[]{:S(2)}, u32[]{:S(2)}) collective-permute-start(f32[6,80,128]{2,1,0:T(8,128)S(1)} %get-tuple-element.90.refs_4_), channel_id=1, source_target_pairs={{0,8},{1,9},{2,10},{3,11},{4,12},{5,13},{6,14},{7,15},{8,0},{9,1},... | collective-permute-start | bytes 737288 | tf_op jit(solution)/shard_map/cond/branch_1_fun/ppermute | solution.py:43
  73.1 43.0 %collective-permute-start.5 = (f32[8,8,3072]{2,1,0:T(8,128)}, f32[8,8,3072]{2,1,0:T(8,128)}, u32[]{:S(2)}, u32[]{:S(2)}) collective-permute-start(f32[8,8,3072]{2,1,0:T(8,128)} %get-tuple-element.93), channel_id=1, source_target_pairs={{0,16},{1,17},{2,18},{3,19},{4,20},{5,21},{6,22},{7,23},{8,24},{9,... | collective-permute-start | bytes 2359304 | tf_op jit(solution)/shard_map/cond/branch_1_fun/ppermute | solution.py:43
  73.8 42.3 %collective-permute-start.6 = (f32[8,8,3072]{2,1,0:T(8,128)}, f32[8,8,3072]{2,1,0:T(8,128)}, u32[]{:S(2)}, u32[]{:S(2)}) collective-permute-start(f32[8,8,3072]{2,1,0:T(8,128)} %get-tuple-element.94), channel_id=1, source_target_pairs={{0,2},{1,3},{2,0},{3,1},{4,6},{5,7},{6,4},{7,5},{8,10},{9,11},{10,... | collective-permute-start | bytes 2359304 | tf_op jit(solution)/shard_map/cond/branch_1_fun/ppermute | solution.py:43
  75.1 41.0 %collective-permute-start.4 = (f32[8,8,3072]{2,1,0:T(8,128)}, f32[8,8,3072]{2,1,0:T(8,128)}, u32[]{:S(2)}, u32[]{:S(2)}) collective-permute-start(f32[8,8,3072]{2,1,0:T(8,128)} %get-tuple-element.92.refs_12_), channel_id=1, source_target_pairs={{0,8},{1,9},{2,10},{3,11},{4,12},{5,13},{6,14},{7,15},{8,0},{9,1},... | collective-permute-start | bytes 2359304 | tf_op jit(solution)/shard_map/cond/branch_1_fun/ppermute | solution.py:43
  76.8 39.3 %slice-start = ((s8[4718592]{0:T(1024)(128)(4,1)}), s8[4194304]{0:T(1024)(128)(4,1)S(1)}, s32[]{:S(2)}) async-start(s8[4718592]{0:T(1024)(128)(4,1)} %bitcast.28), calls=%async_computation.1 | async-start | bytes 8388608 | tf_op jit(solution)/shard_map/cond
  84.4 31.7 %slice-start.1 = ((s8[4718592]{0:T(1024)(128)(4,1)}), s8[524288]{0:T(1024)(128)(4,1)S(1)}, s32[]{:S(2)}) async-start(s8[4718592]{0:T(1024)(128)(4,1)} %bitcast.28), calls=%async_computation.2 | async-start | bytes 1048576 | tf_op jit(solution)/shard_map/cond
  84.4 31.7 %copy-start.2 = (f32[48,8,3072]{2,1,0:T(8,128)S(1)}, f32[48,8,3072]{2,1,0:T(8,128)}, u32[]{:S(2)}) copy-start(f32[48,8,3072]{2,1,0:T(8,128)} %copy-done.1) | copy-start | bytes 14155780 | tf_op jit(solution)/shard_map/cond
  102.0 19.0 %copy-start.11 = (bf16[768,512]{1,0:T(8,128)(2,1)}, bf16[768,512]{1,0:T(8,128)(2,1)S(1)}, u32[]{:S(2)}) copy-start(bf16[768,512]{1,0:T(8,128)(2,1)S(1)} %get-tuple-element.102.refs_1_.refs_12_) | copy-start | bytes 2359300 | tf_op jit(solution)/shard_map/cond
  102.0 7.0 %collective-permute-start.9 = (f32[6,80,128]{2,1,0:T(8,128)S(1)}, f32[6,80,128]{2,1,0:T(8,128)S(1)}, u32[]{:S(2)}, u32[]{:S(2)}) collective-permute-start(f32[6,80,128]{2,1,0:T(8,128)S(1)} %get-tuple-element.105), channel_id=1, source_target_pairs={{0,24},{1,25},{2,26},{3,27},{4,28},{5,29},{6,30},{7,31},{8,16},{9,... | collective-permute-start | bytes 737288 | tf_op jit(solution)/shard_map/cond/branch_1_fun/ppermute | solution.py:43
  103.2 12.8 %collective-permute-start.8 = (f32[6,80,128]{2,1,0:T(8,128)S(1)}, f32[6,80,128]{2,1,0:T(8,128)S(1)}, u32[]{:S(2)}, u32[]{:S(2)}) collective-permute-start(f32[6,80,128]{2,1,0:T(8,128)S(1)} %get-tuple-element.105), channel_id=1, source_target_pairs={{0,16},{1,17},{2,18},{3,19},{4,20},{5,21},{6,22},{7,23},{8,24},{9,... | collective-permute-start | bytes 737288 | tf_op jit(solution)/shard_map/cond/branch_1_fun/ppermute | solution.py:43
  109.0 7.1 %collective-permute-start.7 = (f32[6,80,128]{2,1,0:T(8,128)S(1)}, f32[6,80,128]{2,1,0:T(8,128)S(1)}, u32[]{:S(2)}, u32[]{:S(2)}) collective-permute-start(f32[6,80,128]{2,1,0:T(8,128)S(1)} %get-tuple-element.105), channel_id=1, source_target_pairs={{0,8},{1,9},{2,10},{3,11},{4,12},{5,13},{6,14},{7,15},{8,0},{9,1},... | collective-permute-start | bytes 737288 | tf_op jit(solution)/shard_map/cond/branch_1_fun/ppermute | solution.py:43
  119.0 13.1 %collective-permute-start.11 = (f32[4,8,3072]{2,1,0:T(8,128)S(1)}, f32[4,8,3072]{2,1,0:T(8,128)S(1)}, u32[]{:S(2)}, u32[]{:S(2)}) collective-permute-start(f32[4,8,3072]{2,1,0:T(8,128)S(1)} %get-tuple-element.107), channel_id=1, source_target_pairs={{0,2},{1,3},{2,0},{3,1},{4,6},{5,7},{6,4},{7,5},{8,10},{9,11},{10,... | collective-permute-start | bytes 1179656 | tf_op jit(solution)/shard_map/cond/branch_1_fun/ppermute | solution.py:43
  119.2 12.8 %collective-permute-start.12 = (f32[4,8,3072]{2,1,0:T(8,128)S(1)}, f32[4,8,3072]{2,1,0:T(8,128)S(1)}, u32[]{:S(2)}, u32[]{:S(2)}) collective-permute-start(f32[4,8,3072]{2,1,0:T(8,128)S(1)} %get-tuple-element.108), channel_id=1, source_target_pairs={{0,8},{1,9},{2,10},{3,11},{4,12},{5,13},{6,14},{7,15},{8,0},{9,1},... | collective-permute-start | bytes 1179656 | tf_op jit(solution)/shard_map/cond/branch_1_fun/ppermute | solution.py:43
  120.1 12.0 %collective-permute-start.10 = (f32[4,8,3072]{2,1,0:T(8,128)S(1)}, f32[4,8,3072]{2,1,0:T(8,128)S(1)}, u32[]{:S(2)}, u32[]{:S(2)}) collective-permute-start(f32[4,8,3072]{2,1,0:T(8,128)S(1)} %get-tuple-element.106.refs_27_), channel_id=1, source_target_pairs={{0,16},{1,17},{2,18},{3,19},{4,20},{5,21},{6,22},{7,23},{8,24},{9,... | collective-permute-start | bytes 1179656 | tf_op jit(solution)/shard_map/cond/branch_1_fun/ppermute | solution.py:43
  141.1 11.8 %collective-permute-start.17 = (f32[48,4,8,768]{3,2,1,0:T(8,128)S(1)}, f32[48,4,8,768]{3,2,1,0:T(8,128)S(1)}, u32[]{:S(2)}, u32[]{:S(2)}) collective-permute-start(f32[48,4,8,768]{3,2,1,0:T(8,128)S(1)} %get-tuple-element.127), channel_id=1, source_target_pairs={{0,1},{1,0},{2,3},{3,2},{4,5},{5,4},{6,7},{7,6},{8,9},{9,8},{10,11... | collective-permute-start | bytes 14155784 | tf_op jit(solution)/shard_map/cond/branch_1_fun/ppermute | solution.py:43
  142.6 6.5 %collective-permute-start.14 = (f32[2,8,3072]{2,1,0:T(8,128)S(1)}, f32[2,8,3072]{2,1,0:T(8,128)S(1)}, u32[]{:S(2)}, u32[]{:S(2)}) collective-permute-start(f32[2,8,3072]{2,1,0:T(8,128)S(1)} %get-tuple-element.120), channel_id=1, source_target_pairs={{0,8},{1,9},{2,10},{3,11},{4,12},{5,13},{6,14},{7,15},{8,0},{9,1},... | collective-permute-start | bytes 589832 | tf_op jit(solution)/shard_map/cond/branch_1_fun/ppermute | solution.py:43
  143.4 6.2 %collective-permute-start.15 = (f32[2,8,3072]{2,1,0:T(8,128)S(1)}, f32[2,8,3072]{2,1,0:T(8,128)S(1)}, u32[]{:S(2)}, u32[]{:S(2)}) collective-permute-start(f32[2,8,3072]{2,1,0:T(8,128)S(1)} %get-tuple-element.121), channel_id=1, source_target_pairs={{0,16},{1,17},{2,18},{3,19},{4,20},{5,21},{6,22},{7,23},{8,24},{9,... | collective-permute-start | bytes 589832 | tf_op jit(solution)/shard_map/cond/branch_1_fun/ppermute | solution.py:43
  144.4 6.6 %collective-permute-start.13 = (f32[2,8,3072]{2,1,0:T(8,128)S(1)}, f32[2,8,3072]{2,1,0:T(8,128)S(1)}, u32[]{:S(2)}, u32[]{:S(2)}) collective-permute-start(f32[2,8,3072]{2,1,0:T(8,128)S(1)} %get-tuple-element.119.refs_31_), channel_id=1, source_target_pairs={{0,2},{1,3},{2,0},{3,1},{4,6},{5,7},{6,4},{7,5},{8,10},{9,11},{10,... | collective-permute-start | bytes 589832 | tf_op jit(solution)/shard_map/cond/branch_1_fun/ppermute | solution.py:43
  144.7 8.2 %collective-permute-start.18 = (f32[1,2,8,768]{3,2,1,0:T(8,128)S(1)}, f32[1,2,8,768]{3,2,1,0:T(8,128)S(1)}, u32[]{:S(2)}, u32[]{:S(2)}) collective-permute-start(f32[1,2,8,768]{3,2,1,0:T(8,128)S(1)} %bitcast.58), channel_id=1, source_target_pairs={{0,1},{1,0},{2,3},{3,2},{4,5},{5,4},{6,7},{7,6},{8,9},{9,8},{10,11... | collective-permute-start | bytes 147464 | tf_op jit(solution)/shard_map/cond/branch_1_fun/ppermute | solution.py:43
  153.9 27.3 %collective-permute-start.20 = (f32[8,4,8,768]{3,2,1,0:T(8,128)S(1)}, f32[8,4,8,768]{3,2,1,0:T(8,128)S(1)}, u32[]{:S(2)}, u32[]{:S(2)}) collective-permute-start(f32[8,4,8,768]{3,2,1,0:T(8,128)S(1)} %get-tuple-element.130), channel_id=1, source_target_pairs={{0,16},{1,17},{2,18},{3,19},{4,20},{5,21},{6,22},{7,23},{8,24},{9,... | collective-permute-start | bytes 2359304 | tf_op jit(solution)/shard_map/cond/branch_1_fun/ppermute | solution.py:43
  154.8 28.4 %collective-permute-start.21 = (f32[8,4,8,768]{3,2,1,0:T(8,128)S(1)}, f32[8,4,8,768]{3,2,1,0:T(8,128)S(1)}, u32[]{:S(2)}, u32[]{:S(2)}) collective-permute-start(f32[8,4,8,768]{3,2,1,0:T(8,128)S(1)} %get-tuple-element.131), channel_id=1, source_target_pairs={{0,2},{1,3},{2,0},{3,1},{4,6},{5,7},{6,4},{7,5},{8,10},{9,11},{10,... | collective-permute-start | bytes 2359304 | tf_op jit(solution)/shard_map/cond/branch_1_fun/ppermute | solution.py:43
  155.4 27.8 %collective-permute-start.19 = (f32[8,4,8,768]{3,2,1,0:T(8,128)S(1)}, f32[8,4,8,768]{3,2,1,0:T(8,128)S(1)}, u32[]{:S(2)}, u32[]{:S(2)}) collective-permute-start(f32[8,4,8,768]{3,2,1,0:T(8,128)S(1)} %get-tuple-element.129.refs_11_), channel_id=1, source_target_pairs={{0,8},{1,9},{2,10},{3,11},{4,12},{5,13},{6,14},{7,15},{8,0},{9,1},... | collective-permute-start | bytes 2359304 | tf_op jit(solution)/shard_map/cond/branch_1_fun/ppermute | solution.py:43
  156.7 24.5 %collective-permute-start.22 = (f32[1,2,8,768]{3,2,1,0:T(8,128)S(1)}, f32[1,2,8,768]{3,2,1,0:T(8,128)S(1)}, u32[]{:S(2)}, u32[]{:S(2)}) collective-permute-start(f32[1,2,8,768]{3,2,1,0:T(8,128)S(1)} %get-tuple-element.132.refs_9_), channel_id=1, source_target_pairs={{0,8},{1,9},{2,10},{3,11},{4,12},{5,13},{6,14},{7,15},{8,0},{9,1},... | collective-permute-start | bytes 147464 | tf_op jit(solution)/shard_map/cond/branch_1_fun/ppermute | solution.py:43
  184.0 21.1 %collective-permute-start.24 = (f32[4,4,8,768]{3,2,1,0:T(8,128)S(1)}, f32[4,4,8,768]{3,2,1,0:T(8,128)S(1)}, u32[]{:S(2)}, u32[]{:S(2)}) collective-permute-start(f32[4,4,8,768]{3,2,1,0:T(8,128)S(1)} %get-tuple-element.134), channel_id=1, source_target_pairs={{0,2},{1,3},{2,0},{3,1},{4,6},{5,7},{6,4},{7,5},{8,10},{9,11},{10,... | collective-permute-start | bytes 1179656 | tf_op jit(solution)/shard_map/cond/branch_1_fun/ppermute | solution.py:43
  184.1 21.0 %collective-permute-start.25 = (f32[4,4,8,768]{3,2,1,0:T(8,128)S(1)}, f32[4,4,8,768]{3,2,1,0:T(8,128)S(1)}, u32[]{:S(2)}, u32[]{:S(2)}) collective-permute-start(f32[4,4,8,768]{3,2,1,0:T(8,128)S(1)} %get-tuple-element.135), channel_id=1, source_target_pairs={{0,8},{1,9},{2,10},{3,11},{4,12},{5,13},{6,14},{7,15},{8,0},{9,1},... | collective-permute-start | bytes 1179656 | tf_op jit(solution)/shard_map/cond/branch_1_fun/ppermute | solution.py:43
  185.7 19.4 %collective-permute-start.23 = (f32[4,4,8,768]{3,2,1,0:T(8,128)S(1)}, f32[4,4,8,768]{3,2,1,0:T(8,128)S(1)}, u32[]{:S(2)}, u32[]{:S(2)}) collective-permute-start(f32[4,4,8,768]{3,2,1,0:T(8,128)S(1)} %get-tuple-element.133.refs_14_), channel_id=1, source_target_pairs={{0,16},{1,17},{2,18},{3,19},{4,20},{5,21},{6,22},{7,23},{8,24},{9,... | collective-permute-start | bytes 1179656 | tf_op jit(solution)/shard_map/cond/branch_1_fun/ppermute | solution.py:43
  185.7 45.7 %collective-permute-start.16 = (f32[6,8,3072]{2,1,0:T(8,128)S(1)}, f32[6,8,3072]{2,1,0:T(8,128)S(1)}, u32[]{:S(2)}, u32[]{:S(2)}) collective-permute-start(f32[6,8,3072]{2,1,0:T(8,128)S(1)} %sum_tiles.13.refs_8_.refs_0_.refs_2_.refs_4_), channel_id=1, source_target_pairs={{0,4},{1,5},{2,6},{3,7},{4,0},{5,1},{6,2},{7,3},{8,12},{9,13},{10,... | collective-permute-start | bytes 1769480 | tf_op jit(solution)/shard_map/cond/branch_1_fun/ppermute | solution.py:43
  187.1 16.1 %collective-permute-start.26 = (f32[1,2,8,768]{3,2,1,0:T(8,128)S(1)}, f32[1,2,8,768]{3,2,1,0:T(8,128)S(1)}, u32[]{:S(2)}, u32[]{:S(2)}) collective-permute-start(f32[1,2,8,768]{3,2,1,0:T(8,128)S(1)} %get-tuple-element.136.refs_12_), channel_id=1, source_target_pairs={{0,16},{1,17},{2,18},{3,19},{4,20},{5,21},{6,22},{7,23},{8,24},{9,... | collective-permute-start | bytes 147464 | tf_op jit(solution)/shard_map/cond/branch_1_fun/ppermute | solution.py:43
  205.8 24.7 %collective-permute-start.28 = (f32[2,4,8,768]{3,2,1,0:T(8,128)S(1)}, f32[2,4,8,768]{3,2,1,0:T(8,128)S(1)}, u32[]{:S(2)}, u32[]{:S(2)}) collective-permute-start(f32[2,4,8,768]{3,2,1,0:T(8,128)S(1)} %get-tuple-element.138), channel_id=1, source_target_pairs={{0,8},{1,9},{2,10},{3,11},{4,12},{5,13},{6,14},{7,15},{8,0},{9,1},... | collective-permute-start | bytes 589832 | tf_op jit(solution)/shard_map/cond/branch_1_fun/ppermute | solution.py:43
  207.5 23.0 %collective-permute-start.29 = (f32[2,4,8,768]{3,2,1,0:T(8,128)S(1)}, f32[2,4,8,768]{3,2,1,0:T(8,128)S(1)}, u32[]{:S(2)}, u32[]{:S(2)}) collective-permute-start(f32[2,4,8,768]{3,2,1,0:T(8,128)S(1)} %get-tuple-element.139), channel_id=1, source_target_pairs={{0,16},{1,17},{2,18},{3,19},{4,20},{5,21},{6,22},{7,23},{8,24},{9,... | collective-permute-start | bytes 589832 | tf_op jit(solution)/shard_map/cond/branch_1_fun/ppermute | solution.py:43
  207.5 23.0 %collective-permute-start.27 = (f32[2,4,8,768]{3,2,1,0:T(8,128)S(1)}, f32[2,4,8,768]{3,2,1,0:T(8,128)S(1)}, u32[]{:S(2)}, u32[]{:S(2)}) collective-permute-start(f32[2,4,8,768]{3,2,1,0:T(8,128)S(1)} %get-tuple-element.137.refs_17_), channel_id=1, source_target_pairs={{0,2},{1,3},{2,0},{3,1},{4,6},{5,7},{6,4},{7,5},{8,10},{9,11},{10,... | collective-permute-start | bytes 589832 | tf_op jit(solution)/shard_map/cond/branch_1_fun/ppermute | solution.py:43
  207.5 23.0 %collective-permute-start.30 = (f32[1,2,8,768]{3,2,1,0:T(8,128)S(1)}, f32[1,2,8,768]{3,2,1,0:T(8,128)S(1)}, u32[]{:S(2)}, u32[]{:S(2)}) collective-permute-start(f32[1,2,8,768]{3,2,1,0:T(8,128)S(1)} %get-tuple-element.140.refs_15_), channel_id=1, source_target_pairs={{0,2},{1,3},{2,0},{3,1},{4,6},{5,7},{6,4},{7,5},{8,10},{9,11},{10,... | collective-permute-start | bytes 147464 | tf_op jit(solution)/shard_map/cond/branch_1_fun/ppermute | solution.py:43
  232.0 11.6 %collective-permute-start.31 = (f32[2,8,3072]{2,1,0:T(8,128)S(1)}, f32[2,8,3072]{2,1,0:T(8,128)S(1)}, u32[]{:S(2)}, u32[]{:S(2)}) collective-permute-start(f32[2,8,3072]{2,1,0:T(8,128)S(1)} %get-tuple-element.142.refs_0_.refs_6_), channel_id=1, source_target_pairs={{0,2},{1,3},{2,0},{3,1},{4,6},{5,7},{6,4},{7,5},{8,10},{9,11},{10,... | collective-permute-start | bytes 589832 | tf_op jit(solution)/shard_map/cond/branch_1_fun/ppermute | solution.py:43
  234.4 9.2 %collective-permute-start.32 = (f32[2,8,3072]{2,1,0:T(8,128)S(1)}, f32[2,8,3072]{2,1,0:T(8,128)S(1)}, u32[]{:S(2)}, u32[]{:S(2)}) collective-permute-start(f32[2,8,3072]{2,1,0:T(8,128)S(1)} %get-tuple-element.143.refs_2_), channel_id=1, source_target_pairs={{0,8},{1,9},{2,10},{3,11},{4,12},{5,13},{6,14},{7,15},{8,0},{9,1},... | collective-permute-start | bytes 589832 | tf_op jit(solution)/shard_map/cond/branch_1_fun/ppermute | solution.py:43
  236.4 7.2 %collective-permute-start.33 = (f32[2,8,3072]{2,1,0:T(8,128)S(1)}, f32[2,8,3072]{2,1,0:T(8,128)S(1)}, u32[]{:S(2)}, u32[]{:S(2)}) collective-permute-start(f32[2,8,3072]{2,1,0:T(8,128)S(1)} %get-tuple-element.144.refs_4_), channel_id=1, source_target_pairs={{0,16},{1,17},{2,18},{3,19},{4,20},{5,21},{6,22},{7,23},{8,24},{9,... | collective-permute-start | bytes 589832 | tf_op jit(solution)/shard_map/cond/branch_1_fun/ppermute | solution.py:43
  236.4 43.3 %collective-permute-start.37 = (f32[6,4,8,768]{3,2,1,0:T(8,128)S(1)}, f32[6,4,8,768]{3,2,1,0:T(8,128)S(1)}, u32[]{:S(2)}, u32[]{:S(2)}) collective-permute-start(f32[6,4,8,768]{3,2,1,0:T(8,128)S(1)} %get-tuple-element.141.refs_6_.refs_0_.refs_2_.refs_4_), channel_id=1, source_target_pairs={{0,4},{1,5},{2,6},{3,7},{4,0},{5,1},{6,2},{7,3},{8,12},{9,13},{10,... | collective-permute-start | bytes 1769480 | tf_op jit(solution)/shard_map/cond/branch_1_fun/ppermute | solution.py:43
  244.3 36.0 %collective-permute-start.35 = (f32[4,8,3072]{2,1,0:T(8,128)S(1)}, f32[4,8,3072]{2,1,0:T(8,128)S(1)}, u32[]{:S(2)}, u32[]{:S(2)}) collective-permute-start(f32[4,8,3072]{2,1,0:T(8,128)S(1)} %bitcast.54), channel_id=1, source_target_pairs={{0,2},{1,3},{2,0},{3,1},{4,6},{5,7},{6,4},{7,5},{8,10},{9,11},{10,... | collective-permute-start | bytes 1179656 | tf_op jit(solution)/shard_map/cond/branch_1_fun/ppermute | solution.py:43
  244.7 35.6 %collective-permute-start.34 = (f32[4,8,3072]{2,1,0:T(8,128)S(1)}, f32[4,8,3072]{2,1,0:T(8,128)S(1)}, u32[]{:S(2)}, u32[]{:S(2)}) collective-permute-start(f32[4,8,3072]{2,1,0:T(8,128)S(1)} %bitcast.39), channel_id=1, source_target_pairs={{0,16},{1,17},{2,18},{3,19},{4,20},{5,21},{6,22},{7,23},{8,24},{9,... | collective-permute-start | bytes 1179656 | tf_op jit(solution)/shard_map/cond/branch_1_fun/ppermute | solution.py:43
  244.7 35.6 %collective-permute-start.36 = (f32[4,8,3072]{2,1,0:T(8,128)S(1)}, f32[4,8,3072]{2,1,0:T(8,128)S(1)}, u32[]{:S(2)}, u32[]{:S(2)}) collective-permute-start(f32[4,8,3072]{2,1,0:T(8,128)S(1)} %bitcast.56), channel_id=1, source_target_pairs={{0,8},{1,9},{2,10},{3,11},{4,12},{5,13},{6,14},{7,15},{8,0},{9,1},... | collective-permute-start | bytes 1179656 | tf_op jit(solution)/shard_map/cond/branch_1_fun/ppermute | solution.py:43
  247.9 31.8 %collective-permute-start.38 = (f32[1,2,8,768]{3,2,1,0:T(8,128)S(1)}, f32[1,2,8,768]{3,2,1,0:T(8,128)S(1)}, u32[]{:S(2)}, u32[]{:S(2)}) collective-permute-start(f32[1,2,8,768]{3,2,1,0:T(8,128)S(1)} %get-tuple-element.148.refs_6_), channel_id=1, source_target_pairs={{0,4},{1,5},{2,6},{3,7},{4,0},{5,1},{6,2},{7,3},{8,12},{9,13},{10,... | collective-permute-start | bytes 147464 | tf_op jit(solution)/shard_map/cond/branch_1_fun/ppermute | solution.py:43
  280.3 60.7 %copy-start.39 = (f32[1,2,8,768]{3,2,1,0:T(8,128)}, f32[1,2,8,768]{3,2,1,0:T(8,128)S(1)}, u32[]{:S(2)}) copy-start(f32[1,2,8,768]{3,2,1,0:T(8,128)S(1)} %get-tuple-element.165) | copy-start | bytes 147460 | tf_op jit(solution)/shard_map/cond
  281.3 25.8 %collective-permute-start.40 = (f32[8,8,3072]{2,1,0:T(8,128)S(1)}, f32[8,8,3072]{2,1,0:T(8,128)S(1)}, u32[]{:S(2)}, u32[]{:S(2)}) collective-permute-start(f32[8,8,3072]{2,1,0:T(8,128)S(1)} %bitcast.46), channel_id=1, source_target_pairs={{0,16},{1,17},{2,18},{3,19},{4,20},{5,21},{6,22},{7,23},{8,24},{9,... | collective-permute-start | bytes 2359304 | tf_op jit(solution)/shard_map/cond/branch_1_fun/ppermute | solution.py:43
  281.6 5.2 %collective-permute-start.43 = (f32[2,4,8,768]{3,2,1,0:T(8,128)S(1)}, f32[2,4,8,768]{3,2,1,0:T(8,128)S(1)}, u32[]{:S(2)}, u32[]{:S(2)}) collective-permute-start(f32[2,4,8,768]{3,2,1,0:T(8,128)S(1)} %get-tuple-element.153.refs_2_), channel_id=1, source_target_pairs={{0,8},{1,9},{2,10},{3,11},{4,12},{5,13},{6,14},{7,15},{8,0},{9,1},... | collective-permute-start | bytes 589832 | tf_op jit(solution)/shard_map/cond/branch_1_fun/ppermute | solution.py:43
  283.2 25.2 %collective-permute-start.39 = (f32[8,8,3072]{2,1,0:T(8,128)S(1)}, f32[8,8,3072]{2,1,0:T(8,128)S(1)}, u32[]{:S(2)}, u32[]{:S(2)}) collective-permute-start(f32[8,8,3072]{2,1,0:T(8,128)S(1)} %bitcast.33), channel_id=1, source_target_pairs={{0,8},{1,9},{2,10},{3,11},{4,12},{5,13},{6,14},{7,15},{8,0},{9,1},... | collective-permute-start | bytes 2359304 | tf_op jit(solution)/shard_map/cond/branch_1_fun/ppermute | solution.py:43
  283.3 25.1 %collective-permute-start.41 = (f32[8,8,3072]{2,1,0:T(8,128)S(1)}, f32[8,8,3072]{2,1,0:T(8,128)S(1)}, u32[]{:S(2)}, u32[]{:S(2)}) collective-permute-start(f32[8,8,3072]{2,1,0:T(8,128)S(1)} %bitcast.48), channel_id=1, source_target_pairs={{0,2},{1,3},{2,0},{3,1},{4,6},{5,7},{6,4},{7,5},{8,10},{9,11},{10,... | collective-permute-start | bytes 2359304 | tf_op jit(solution)/shard_map/cond/branch_1_fun/ppermute | solution.py:43
  286.0 14.0 %collective-permute-start.44 = (f32[2,4,8,768]{3,2,1,0:T(8,128)S(1)}, f32[2,4,8,768]{3,2,1,0:T(8,128)S(1)}, u32[]{:S(2)}, u32[]{:S(2)}) collective-permute-start(f32[2,4,8,768]{3,2,1,0:T(8,128)S(1)} %get-tuple-element.154.refs_4_), channel_id=1, source_target_pairs={{0,16},{1,17},{2,18},{3,19},{4,20},{5,21},{6,22},{7,23},{8,24},{9,... | collective-permute-start | bytes 589832 | tf_op jit(solution)/shard_map/cond/branch_1_fun/ppermute | solution.py:43
  286.8 16.2 %collective-permute-start.42 = (f32[2,4,8,768]{3,2,1,0:T(8,128)S(1)}, f32[2,4,8,768]{3,2,1,0:T(8,128)S(1)}, u32[]{:S(2)}, u32[]{:S(2)}) collective-permute-start(f32[2,4,8,768]{3,2,1,0:T(8,128)S(1)} %get-tuple-element.149.refs_6_.refs_0_), channel_id=1, source_target_pairs={{0,2},{1,3},{2,0},{3,1},{4,6},{5,7},{6,4},{7,5},{8,10},{9,11},{10,... | collective-permute-start | bytes 589832 | tf_op jit(solution)/shard_map/cond/branch_1_fun/ppermute | solution.py:43
  303.8 8.4 %collective-permute-start.47 = (f32[4,4,8,768]{3,2,1,0:T(8,128)S(1)}, f32[4,4,8,768]{3,2,1,0:T(8,128)S(1)}, u32[]{:S(2)}, u32[]{:S(2)}) collective-permute-start(f32[4,4,8,768]{3,2,1,0:T(8,128)S(1)} %bitcast.50), channel_id=1, source_target_pairs={{0,2},{1,3},{2,0},{3,1},{4,6},{5,7},{6,4},{7,5},{8,10},{9,11},{10,... | collective-permute-start | bytes 1179656 | tf_op jit(solution)/shard_map/cond/branch_1_fun/ppermute | solution.py:43
  306.1 6.6 %collective-permute-start.46 = (f32[4,4,8,768]{3,2,1,0:T(8,128)S(1)}, f32[4,4,8,768]{3,2,1,0:T(8,128)S(1)}, u32[]{:S(2)}, u32[]{:S(2)}) collective-permute-start(f32[4,4,8,768]{3,2,1,0:T(8,128)S(1)} %bitcast.36), channel_id=1, source_target_pairs={{0,16},{1,17},{2,18},{3,19},{4,20},{5,21},{6,22},{7,23},{8,24},{9,... | collective-permute-start | bytes 1179656 | tf_op jit(solution)/shard_map/cond/branch_1_fun/ppermute | solution.py:43
  307.1 6.9 %collective-permute-start.48 = (f32[4,4,8,768]{3,2,1,0:T(8,128)S(1)}, f32[4,4,8,768]{3,2,1,0:T(8,128)S(1)}, u32[]{:S(2)}, u32[]{:S(2)}) collective-permute-start(f32[4,4,8,768]{3,2,1,0:T(8,128)S(1)} %bitcast.52), channel_id=1, source_target_pairs={{0,8},{1,9},{2,10},{3,11},{4,12},{5,13},{6,14},{7,15},{8,0},{9,1},... | collective-permute-start | bytes 1179656 | tf_op jit(solution)/shard_map/cond/branch_1_fun/ppermute | solution.py:43
  315.0 15.3 %collective-permute-start.50 = (f32[8,4,8,768]{3,2,1,0:T(8,128)S(1)}, f32[8,4,8,768]{3,2,1,0:T(8,128)S(1)}, u32[]{:S(2)}, u32[]{:S(2)}) collective-permute-start(f32[8,4,8,768]{3,2,1,0:T(8,128)S(1)} %bitcast.42), channel_id=1, source_target_pairs={{0,16},{1,17},{2,18},{3,19},{4,20},{5,21},{6,22},{7,23},{8,24},{9,... | collective-permute-start | bytes 2359304 | tf_op jit(solution)/shard_map/cond/branch_1_fun/ppermute | solution.py:43
  315.5 14.7 %collective-permute-start.49 = (f32[8,4,8,768]{3,2,1,0:T(8,128)S(1)}, f32[8,4,8,768]{3,2,1,0:T(8,128)S(1)}, u32[]{:S(2)}, u32[]{:S(2)}) collective-permute-start(f32[8,4,8,768]{3,2,1,0:T(8,128)S(1)} %bitcast.30), channel_id=1, source_target_pairs={{0,8},{1,9},{2,10},{3,11},{4,12},{5,13},{6,14},{7,15},{8,0},{9,1},... | collective-permute-start | bytes 2359304 | tf_op jit(solution)/shard_map/cond/branch_1_fun/ppermute | solution.py:43
  316.6 13.6 %collective-permute-start.51 = (f32[8,4,8,768]{3,2,1,0:T(8,128)S(1)}, f32[8,4,8,768]{3,2,1,0:T(8,128)S(1)}, u32[]{:S(2)}, u32[]{:S(2)}) collective-permute-start(f32[8,4,8,768]{3,2,1,0:T(8,128)S(1)} %bitcast.44), channel_id=1, source_target_pairs={{0,2},{1,3},{2,0},{3,1},{4,6},{5,7},{6,4},{7,5},{8,10},{9,11},{10,... | collective-permute-start | bytes 2359304 | tf_op jit(solution)/shard_map/cond/branch_1_fun/ppermute | solution.py:43
  316.7 29.6 %collective-permute-start.45 = (f32[48,8,3072]{2,1,0:T(8,128)}, f32[48,8,3072]{2,1,0:T(8,128)}, u32[]{:S(2)}, u32[]{:S(2)}) collective-permute-start(f32[48,8,3072]{2,1,0:T(8,128)} %bitcast.10.refs_6_.part), channel_id=1, source_target_pairs={{0,1},{1,0},{2,3},{3,2},{4,5},{5,4},{6,7},{7,6},{8,9},{9,8},{10,11... | collective-permute-start | bytes 14155784 | tf_op jit(solution)/shard_map/cond/branch_1_fun/ppermute | solution.py:43
  333.5 17.4 %collective-permute-start.52 = (f32[48,4,8,768]{3,2,1,0:T(8,128)}, f32[48,4,8,768]{3,2,1,0:T(8,128)}, u32[]{:S(2)}, u32[]{:S(2)}) collective-permute-start(f32[48,4,8,768]{3,2,1,0:T(8,128)} %bitcast.16.part.refs_0_), channel_id=1, source_target_pairs={{0,1},{1,0},{2,3},{3,2},{4,5},{5,4},{6,7},{7,6},{8,9},{9,8},{10,11... | collective-permute-start | bytes 14155784 | tf_op jit(solution)/shard_map/cond/branch_1_fun/ppermute | solution.py:43
  (52 other events, 268.6 us)
Sparse Core Ops, SparseCore 0:
  27.2 257.2 all-reduce.1

commit v2 on v1

--- a/solution.py
+++ b/solution.py
@@ -423,7 +423,8 @@
         vec[r : r + 1] = ref[...].reshape(1, width)
     for r in range(3):
         vec[4 + r : 5 + r] = in_bias[r * width : (r + 1) * width].reshape(1, width)
-    vec[7:8] = feat_weight[...]
+    heads = feat_weight.shape[0]
+    vec[7:8] = jnp.concatenate([feat_weight[h : h + 1] for h in range(heads)], axis=1)
     up_bias[...] = up_bias_in[...].reshape(up_bias.shape)
     xhat, _ = normalise(tok[...])
     one = (xhat * vec[0:1] + vec[1:2]).astype(B16)
@@ -1035,7 +1036,7 @@
     start = span_starts[0, :1]
     small = (
         first_gain, first_shift, second_gain, second_shift, input_bias,
-        feature_weight.reshape(1, -1), up_bias,
+        feature_weight, up_bias,
     )
     first_t, second, second_t, proj, proj_t, angle, vec, up_bias_row = norms(
         place * length, tok, small, feature_freq

time: 372 us -> 371 us (level)
  no operation moved by 1% of the time
where the time goes in v2:
time: 371 us; the launch traced here: 370 us
  waiting for transfers between devices  142 us (38%)
  Pallas kernels  120 us (32%)
  starting transfers between devices  65.4 us (18%)
  local copies, waits for them, and re-layouts  26.2 us (7%)
  between operations  14.3 us (4%)
    ppermute x53, waiting for transfers between devices, swap(): return lax.ppermute(array, AXES, [(i, i ^ bit) for i in range(count)])  142 us
    ppermute x53, starting transfers between devices, swap(): return lax.ppermute(array, AXES, [(i, i ^ bit) for i in range(count)])  65.4 us
    pallas_call x4, Pallas kernels, put_half(): pl.pallas_call(kernel, grid_spec=pltpu.PrefetchScalarGridSpec(num_scalar_...  18.3 us
    pallas_call x1, Pallas kernels, attention(): pl.pallas_call(ordered(functools.partial(attention_kernel, size, partners...  17.6 us
    pallas_call x2, Pallas kernels, backward(): pl.pallas_call(ordered(functools.partial(backward_kernel, size, partners,...  16.1 us
    pallas_call x10, Pallas kernels, sum_tiles(): pl.pallas_call(kernel, grid_spec=pltpu.PrefetchScalarGridSpec(num_scalar_...  14.2 us
    cond x96, local copies, waits for them, and re-layouts  13.5 us
    pallas_call x1, Pallas kernels, mlp_part(): pl.pallas_call(mlp_kernel, grid=(hidden // tile,), in_specs=[full((rows,...  13.1 us
  transfers between devices with their start and end apart: 54, of which 21 were waited for; matrix products, arithmetic and copies ran while one was open for 1% of the time, Pallas kernels for 28%

profile of v2, /device:TPU:1, one launch (start us, length us, event | category | flops | bytes accessed | tf_op | source)
XLA Modules:
  0.0 370.4 jit_solution(12485885598912816816)
XLA Ops:
  7.2 3.7 %norms.1 = (bf16[768,512]{1,0:T(8,128)(2,1)}, bf16[512,768]{1,0:T(8,128)(2,1)}, bf16[768,512]{1,0:T(8,128)(2,1)}, f32[256,256]{1,0:T(8,128)S(1)}, f32[256,256]{1...) custom-call(s32[1]{0:T(128)S(6)} %mul.7.offset, bf16[512,768]{1,0:T(8,128)(2,1)} %bitcast.66, ...), custom_call_target="tpu_custom_call" | custom-call | tf_op jit(solution)/shard_map/norms/pallas_call | solution.py:454
  11.0 1.1 copy-done.26
  12.8 13.1 %mlp.1 = (bf16[512,3072]{1,0:T(8,128)(2,1)}, bf16[512,3072]{1,0:T(8,128)(2,1)S(1)}, f32[3072,768]{1,0:T(8,128)}, f32[1,3072]{1,0:T(1,128)S(1)}) custom-call(bf16[512,768]{1,0:T(8,128)(2,1)S(1)} %copy-done.26, bf16[512,768]{1,0:T(8,128)(2,1)} %bitcast.60, bf16[768,3072]{1,0:T(8,128)(2,1)} %up.1, f32[1,3072]{1,0:T(1,128)S(1)} %copy-done.27, bf16[3072,768]{1,0:T(8,128)(2,1)} %down.1), custom_call_target="tpu_custom_call" | custom-call | tf_op jit(solution)/shard_map/mlp/pallas_call | solution.py:489
  27.2 327.5 %conditional.1 = (f32[768,3072]{1,0:T(8,128)}, f32[768,2304]{1,0:T(8,128)}, f32[768,768]{1,0:T(8,128)}, f32[16,768]{1,0:T(8,128)}, bf16[1,512,768]{2,1,0:T(8,128...) conditional(s32[]{:T(128)} %bitcast.23, () %tuple.27, ...), branch_computations={%region_0.0_spmd, %region_1.0_spmd} | conditional | flops 4620 | bytes 423209344 | solution.py:1105
  28.7 4.3 %up_half.2.refs_3_ = f32[48,8,3072]{2,1,0:T(8,128)S(1)} custom-call(s32[5]{0:T(128)S(1)} %shift-right-arithmetic_and_fusion.refs_0_._.refs_26_.bits, bf16[768,512]{1,0:T(8,128)(2,1)} %get-tuple-element.78.refs_1_, bf16[512,3072]{1,0:T(8,128)(2,1)S(1)} %get-tuple-element.79.refs_2_.refs_1_), custom_call_target="tpu_custom_call" | custom-call | tf_op jit(solution)/shard_map/cond/branch_1_fun/up_half/pallas_call | solution.py:527
  33.1 3.3 up_half.3.refs_9_.refs_0_.refs_2_.refs_4_.refs_3_.refs_6_.refs_8_.refs_5_.refs_10_
  36.5 8.1 %features.1 = (bf16[768,512]{1,0:T(8,128)(2,1)S(1)}, bf16[768,512]{1,0:T(8,128)(2,1)S(1)}, bf16[768,512]{1,0:T(8,128)(2,1)S(1)}, f32[2,768,512]{2,1,0:T(8,128)S(...) custom-call(bf16[768,512]{1,0:T(8,128)(2,1)S(1)} %copy-done.34, bf16[768,2304]{1,0:T(8,128)(2,1)S(1)} %copy-done.28, ...), custom_call_target="tpu_custom_call" | custom-call | tf_op jit(solution)/shard_map/cond/branch_1_fun/features/pallas_call | solution.py:663
  44.6 1.7 copy-done.3
  47.3 3.6 collective-permute-start.3
  51.2 8.5 %mlp_tail.1 = (f32[512,768]{1,0:T(8,128)S(1)}, f32[512,768]{1,0:T(8,128)S(1)}) custom-call(bf16[512,3072]{1,0:T(8,128)(2,1)S(1)} %copy-done.36, bf16[512,3072]{1,0:T(8,128)(2,1)S(1)} %copy-done.31, bf16[768,3072]{1,0:T(8,128)(2,1)S(1)} %bitcast.63, bf16[3072,768]{1,0:T(8,128)(2,1)S(1)} %bitcast.65, f32[6,80,128]{2,1,0:T(8,128)S(1)} %get-tuple-element.90.refs_4_), custom_call_target="tpu_custom_call" | custom-call | tf_op jit(solution)/shard_map/cond/branch_1_fun/mlp_tail/pallas_call | solution.py:566
  59.7 1.2 copy-done.13
  61.2 6.8 %collective-permute-done.2.refs_8_.refs_10_ = f32[6,80,128]{2,1,0:T(8,128)S(1)} collective-permute-done((f32[6,80,128]{2,1,0:T(8,128)S(1)}, f32[6,80,128]{2,1,0:T(8,128)S(1)}, u32[]{:S(2)}, u32[]{:S(2)}) %collective-permute-start.2) | collective-permute-done | bytes 245792 | tf_op jit(solution)/shard_map/cond/branch_1_fun/ppermute | solution.py:43
  68.9 3.0 sum_tiles.10
  72.6 1.3 collective-permute-start.6
  75.6 1.3 copy-done.6
  76.9 1.4 copy-done.9
  82.1 1.1 copy-done.25
  83.2 17.6 %attention.1 = (bf16[768,512]{1,0:T(8,128)(2,1)S(1)}, f32[768,512]{1,0:T(8,128)S(1)}, f32[768,512]{1,0:T(8,128)S(1)}, f32[768,512]{1,0:T(8,128)S(1)}, f32[6,80,1...) custom-call(s32[1]{0:T(128)} %get-tuple-element.96.refs_0_, s32[1]{0:T(128)S(1)} %bitcast.76, bf16[768,512]{1,0:T(8,128)(2,1)S(1)} %copy-done.25, ...), custom_call_target="tpu_custom_call" | custom-call | tf_op jit(solution)/shard_map/cond/branch_1_fun/attention/pallas_call | solution.py:816
  100.8 1.3 collective-permute-start.9
  102.7 5.1 %collective-permute-done.9.refs_12_.refs_23_ = f32[6,80,128]{2,1,0:T(8,128)S(1)} collective-permute-done((f32[6,80,128]{2,1,0:T(8,128)S(1)}, f32[6,80,128]{2,1,0:T(8,128)S(1)}, u32[]{:S(2)}, u32[]{:S(2)}) %collective-permute-start.9) | collective-permute-done | bytes 245792 | tf_op jit(solution)/shard_map/cond/branch_1_fun/ppermute | solution.py:43
  108.8 1.4 copy-done.16
  110.2 3.3 results.1.refs_9_
  113.6 1.3 collective-permute-done.8.refs_11_.refs_22_
  115.0 2.8 sum_tiles.11
  119.8 8.9 %backward.2 = (f32[48,4,8,768]{3,2,1,0:T(8,128)S(1)}, f32[48,4,8,768]{3,2,1,0:T(8,128)S(1)}, f32[16,768]{1,0:T(8,128)S(1)}, f32[768,512]{1,0:T(8,128)S(1)}) custom-call(f32[768,512]{1,0:T(8,128)S(1)} %get-tuple-element.109.refs_0_, f32[768,512]{1,0:T(8,128)S(1)} %get-tuple-element.110.refs_1_, f32[768,512]{1,0:T(8,128)S(1)} %get-tuple-element.111.refs_2_, ...), custom_call_target="tpu_custom_call" | custom-call | tf_op jit(solution)/shard_map/cond/branch_1_fun/backward/pallas_call | solution.py:965
  128.7 2.2 collective-permute-done.11.refs_7_.refs_8_
  130.9 1.8 sum_tiles.12
  132.7 7.3 %backward.3 = (f32[48,4,8,768]{3,2,1,0:T(8,128)S(1)}, f32[48,4,8,768]{3,2,1,0:T(8,128)S(1)}, f32[16,768]{1,0:T(8,128)S(1)}, f32[768,512]{1,0:T(8,128)}, bf16[512,768]{1,0:T(8,128)(2,1)}) custom-call(f32[768,512]{1,0:T(8,128)S(1)} %get-tuple-element.109.refs_0_, ...), custom_call_target="tpu_custom_call", output_to_operand_aliasing={{0}: (29, {}), {1}: (30, {})} | custom-call | tf_op jit(solution)/shard_map/cond/branch_1_fun/backward/pallas_call | solution.py:965
  140.0 1.4 collective-permute-start.17
  144.4 3.6 collective-permute-done.14.refs_9_
  148.5 1.3 collective-permute-done.13.refs_4_
  149.8 2.0 sum_tiles.13.refs_8_.refs_0_.refs_2_.refs_4_
  154.3 1.3 collective-permute-start.19
  155.7 24.5 %collective-permute-done.22.refs_10_ = f32[1,2,8,768]{3,2,1,0:T(8,128)S(1)} collective-permute-done((f32[1,2,8,768]{3,2,1,0:T(8,128)S(1)}, f32[1,2,8,768]{3,2,1,0:T(8,128)S(1)}, u32[]{:S(2)}, u32[]{:S(2)}) %collective-permute-start.22) | collective-permute-done | bytes 49184 | tf_op jit(solution)/shard_map/cond/branch_1_fun/ppermute | solution.py:43
  180.2 1.7 collective-permute-done.21.refs_8_.refs_10_.refs_12_
  183.2 1.7 collective-permute-start.25
  185.6 1.5 collective-permute-start.26
  187.1 15.7 %collective-permute-done.26.refs_13_ = f32[1,2,8,768]{3,2,1,0:T(8,128)S(1)} collective-permute-done((f32[1,2,8,768]{3,2,1,0:T(8,128)S(1)}, f32[1,2,8,768]{3,2,1,0:T(8,128)S(1)}, u32[]{:S(2)}, u32[]{:S(2)}) %collective-permute-start.26) | collective-permute-done | bytes 49184 | tf_op jit(solution)/shard_map/cond/branch_1_fun/ppermute | solution.py:43
  204.6 1.5 collective-permute-start.30
  206.0 23.8 %collective-permute-done.30.refs_16_ = f32[1,2,8,768]{3,2,1,0:T(8,128)S(1)} collective-permute-done((f32[1,2,8,768]{3,2,1,0:T(8,128)S(1)}, f32[1,2,8,768]{3,2,1,0:T(8,128)S(1)}, u32[]{:S(2)}, u32[]{:S(2)}) %collective-permute-start.30) | collective-permute-done | bytes 49184 | tf_op jit(solution)/shard_map/cond/branch_1_fun/ppermute | solution.py:43
  231.3 2.4 collective-permute-start.31
  233.7 2.3 collective-permute-start.32
  236.0 6.6 %collective-permute-done.31.refs_1_ = f32[2,8,3072]{2,1,0:T(8,128)S(1)} collective-permute-done((f32[2,8,3072]{2,1,0:T(8,128)S(1)}, f32[2,8,3072]{2,1,0:T(8,128)S(1)}, u32[]{:S(2)}, u32[]{:S(2)}) %collective-permute-start.31) | collective-permute-done | bytes 196640 | tf_op jit(solution)/shard_map/cond/branch_1_fun/ppermute | solution.py:43
  244.0 3.7 collective-permute-start.36
  247.7 31.1 %collective-permute-done.38.refs_7_ = f32[1,2,8,768]{3,2,1,0:T(8,128)S(1)} collective-permute-done((f32[1,2,8,768]{3,2,1,0:T(8,128)S(1)}, f32[1,2,8,768]{3,2,1,0:T(8,128)S(1)}, u32[]{:S(2)}, u32[]{:S(2)}) %collective-permute-start.38) | collective-permute-done | bytes 49184 | tf_op jit(solution)/shard_map/cond/branch_1_fun/ppermute | solution.py:43
  281.4 1.1 collective-permute-start.43
  282.8 1.8 collective-permute-start.41
  285.9 1.8 collective-permute-start.42
  287.7 11.0 %collective-permute-done.44.refs_5_ = f32[2,4,8,768]{3,2,1,0:T(8,128)S(1)} collective-permute-done((f32[2,4,8,768]{3,2,1,0:T(8,128)S(1)}, f32[2,4,8,768]{3,2,1,0:T(8,128)S(1)}, u32[]{:S(2)}, u32[]{:S(2)}) %collective-permute-start.44) | collective-permute-done | bytes 196640 | tf_op jit(solution)/shard_map/cond/branch_1_fun/ppermute | solution.py:43
  298.6 2.7 collective-permute-done.42.refs_1_
  302.1 2.3 collective-permute-start.47
  304.4 1.2 collective-permute-start.46
  305.6 1.5 collective-permute-start.48
  307.1 3.2 interleave.9
  311.0 1.6 collective-permute-done.48.refs_5_
  313.9 1.5 collective-permute-start.49
  315.5 9.2 %collective-permute-start.45 = (f32[48,8,3072]{2,1,0:T(8,128)}, f32[48,8,3072]{2,1,0:T(8,128)}, u32[]{:S(2)}, u32[]{:S(2)}) collective-permute-start(f32[48,8,3072]{2,1,0:T(8,128)} %bitcast.10.refs_6_.part), channel_id=1, source_target_pairs={{0,1},{1,0},{2,3},{3,2},{4,5},{5,4},{6,7},{7,6},{8,9},{9,8},{10,11... | collective-permute-start | bytes 14155784 | tf_op jit(solution)/shard_map/cond/branch_1_fun/ppermute | solution.py:43
  324.8 4.5 %put_half.4.refs_6_.refs_0_ = f32[2,48,8,3072]{3,2,1,0:T(8,128)} custom-call(s32[5]{0:T(128)S(1)} %shift-right-arithmetic_and_fusion.refs_0_._.refs_26_.bits, f32[48,8,3072]{2,1,0:T(8,128)} %bitcast.10.refs_6_.part, f32[8,4,8,768]{3,2,1,0:T(8,128)S(1)} %bitcast.31), custom_call_target="tpu_custom_call" | custom-call | tf_op jit(solution)/shard_map/cond/branch_1_fun/put_half/pallas_call | solution.py:204
  329.3 3.2 interleave.11
  332.5 7.3 %collective-permute-start.52 = (f32[48,4,8,768]{3,2,1,0:T(8,128)}, f32[48,4,8,768]{3,2,1,0:T(8,128)}, u32[]{:S(2)}, u32[]{:S(2)}) collective-permute-start(f32[48,4,8,768]{3,2,1,0:T(8,128)} %bitcast.16.part.refs_0_), channel_id=1, source_target_pairs={{0,1},{1,0},{2,3},{3,2},{4,5},{5,4},{6,7},{7,6},{8,9},{9,8},{10,11... | collective-permute-start | bytes 14155784 | tf_op jit(solution)/shard_map/cond/branch_1_fun/ppermute | solution.py:43
  340.6 4.6 %put_half.5 = (f32[2,48,8,2304]{3,2,1,0:T(8,128)}, f32[2,48,8,768]{3,2,1,0:T(8,128)}) custom-call(s32[5]{0:T(128)S(1)} %shift-right-arithmetic_and_fusion.refs_0_._.refs_26_.bits, f32[48,4,8,768]{3,2,1,0:T(8,128)} %bitcast.16.part.refs_0_, f32[48,4,8,768]{3,2,1,0:T(8,128)} %bitcast.16.part.refs_0_), custom_call_target="tpu_custom_call" | custom-call | tf_op jit(solution)/shard_map/cond/branch_1_fun/put_half/pallas_call | solution.py:204
  345.3 4.5 %put_half.6 = f32[2,48,8,3072]{3,2,1,0:T(8,128)} custom-call(s32[5]{0:T(128)S(1)} %shift-right-arithmetic_and_fusion.refs_0_._.refs_26_.bits, f32[48,8,3072]{2,1,0:T(8,128)} %collective-permute-done.45.part, f32[2,48,8,3072]{3,2,1,0:T(8,128)} %put_half.4.refs_6_.refs_0_, ...), custom_call_target="tpu_custom_call", output_to_operand_aliasing={{}: (2, {})} | custom-call | tf_op jit(solution)/shard_map/cond/branch_1_fun/put_half/pallas_call | solution.py:204
  349.8 4.7 %put_half.7 = (f32[2,48,8,2304]{3,2,1,0:T(8,128)}, f32[2,48,8,768]{3,2,1,0:T(8,128)}) custom-call(s32[5]{0:T(128)S(1)} %shift-right-arithmetic_and_fusion.refs_0_._.refs_26_.bits, f32[48,4,8,768]{3,2,1,0:T(8,128)} %collective-permute-done.52.part, ...), custom_call_target="tpu_custom_call", output_to_operand_aliasing={{0}: (2, {}), {1}: (3, {})} | custom-call | tf_op jit(solution)/shard_map/cond/branch_1_fun/put_half/pallas_call | solution.py:204
  355.4 8.1 %copy.98 = f32[3072,768]{1,0:T(8,128)} copy(f32[3072,768]{1,0:T(8,128)} %all-reduce.2.cloned.1.call-done) | data formatting | bytes 18874368
  (214 shorter events, 37.0 us)
Async XLA Ops:
  7.2 347.6 %all-reduce.2.cloned.1.call-start = ((), (), s32[]{:S(2)}) async-start(), calls=%async_computation | async-start | bytes 18874368 | tf_op jit(solution)/shard_map/psum | solution.py:1047
  33.0 35.9 %collective-permute-start = (f32[48,8,3072]{2,1,0:T(8,128)S(1)}, f32[48,8,3072]{2,1,0:T(8,128)S(1)}, u32[]{:S(2)}, u32[]{:S(2)}) collective-permute-start(f32[48,8,3072]{2,1,0:T(8,128)S(1)} %up_half.2.refs_3_), channel_id=1, source_target_pairs={{0,1},{1,0},{2,3},{3,2},{4,5},{5,4},{6,7},{7,6},{8,9},{9,8},{10,11... | collective-permute-start | bytes 14155784 | tf_op jit(solution)/shard_map/cond/branch_1_fun/ppermute | solution.py:43
  33.1 18.1 %slice-start.2 = ((s8[4718592]{0:T(1024)(128)(4,1)}), s8[4194304]{0:T(1024)(128)(4,1)S(1)}, s32[]{:S(2)}) async-start(s8[4718592]{0:T(1024)(128)(4,1)} %bitcast.62), calls=%async_computation.3 | async-start | bytes 8388608 | tf_op jit(solution)/shard_map/cond
  33.1 18.1 %slice-start.4 = ((s8[4718592]{0:T(1024)(128)(4,1)}), s8[4194304]{0:T(1024)(128)(4,1)S(1)}, s32[]{:S(2)}) async-start(s8[4718592]{0:T(1024)(128)(4,1)} %bitcast.64), calls=%async_computation.5 | async-start | bytes 8388608 | tf_op jit(solution)/shard_map/cond
  36.4 32.5 %copy-start = (f32[48,8,3072]{2,1,0:T(8,128)}, f32[48,8,3072]{2,1,0:T(8,128)S(1)}, u32[]{:S(2)}) copy-start(f32[48,8,3072]{2,1,0:T(8,128)S(1)} %up_half.3.refs_9_.refs_0_.refs_2_.refs_4_.refs_3_.refs_6_.refs_8_.refs_5_.refs_10_) | copy-start | bytes 14155780 | tf_op jit(solution)/shard_map/cond
  36.5 14.7 %copy-start.31 = (bf16[512,3072]{1,0:T(8,128)(2,1)S(1)}, bf16[512,3072]{1,0:T(8,128)(2,1)}, u32[]{:S(2)}) copy-start(bf16[512,3072]{1,0:T(8,128)(2,1)} %copy-done.30) | copy-start | bytes 9437188 | tf_op jit(solution)/shard_map/cond
  36.5 14.7 %slice-start.3 = ((s8[4718592]{0:T(1024)(128)(4,1)}), s8[524288]{0:T(1024)(128)(4,1)S(1)}, s32[]{:S(2)}) async-start(s8[4718592]{0:T(1024)(128)(4,1)} %bitcast.62), calls=%async_computation.4 | async-start | bytes 1048576 | tf_op jit(solution)/shard_map/cond
  47.3 13.9 %collective-permute-start.3 = (f32[6,80,128]{2,1,0:T(8,128)S(1)}, f32[6,80,128]{2,1,0:T(8,128)S(1)}, u32[]{:S(2)}, u32[]{:S(2)}) collective-permute-start(f32[6,80,128]{2,1,0:T(8,128)S(1)} %get-tuple-element.90.refs_4_), channel_id=1, source_target_pairs={{0,24},{1,25},{2,26},{3,27},{4,28},{5,29},{6,30},{7,31},{8,16},{9,... | collective-permute-start | bytes 737288 | tf_op jit(solution)/shard_map/cond/branch_1_fun/ppermute | solution.py:43
  50.9 17.1 %collective-permute-start.2 = (f32[6,80,128]{2,1,0:T(8,128)S(1)}, f32[6,80,128]{2,1,0:T(8,128)S(1)}, u32[]{:S(2)}, u32[]{:S(2)}) collective-permute-start(f32[6,80,128]{2,1,0:T(8,128)S(1)} %get-tuple-element.90.refs_4_), channel_id=1, source_target_pairs={{0,16},{1,17},{2,18},{3,19},{4,20},{5,21},{6,22},{7,23},{8,24},{9,... | collective-permute-start | bytes 737288 | tf_op jit(solution)/shard_map/cond/branch_1_fun/ppermute | solution.py:43
  51.1 17.8 %collective-permute-start.1 = (f32[6,80,128]{2,1,0:T(8,128)S(1)}, f32[6,80,128]{2,1,0:T(8,128)S(1)}, u32[]{:S(2)}, u32[]{:S(2)}) collective-permute-start(f32[6,80,128]{2,1,0:T(8,128)S(1)} %get-tuple-element.90.refs_4_), channel_id=1, source_target_pairs={{0,8},{1,9},{2,10},{3,11},{4,12},{5,13},{6,14},{7,15},{8,0},{9,1},... | collective-permute-start | bytes 737288 | tf_op jit(solution)/shard_map/cond/branch_1_fun/ppermute | solution.py:43
  71.9 43.0 %collective-permute-start.5 = (f32[8,8,3072]{2,1,0:T(8,128)}, f32[8,8,3072]{2,1,0:T(8,128)}, u32[]{:S(2)}, u32[]{:S(2)}) collective-permute-start(f32[8,8,3072]{2,1,0:T(8,128)} %get-tuple-element.93), channel_id=1, source_target_pairs={{0,16},{1,17},{2,18},{3,19},{4,20},{5,21},{6,22},{7,23},{8,24},{9,... | collective-permute-start | bytes 2359304 | tf_op jit(solution)/shard_map/cond/branch_1_fun/ppermute | solution.py:43
  72.6 42.3 %collective-permute-start.6 = (f32[8,8,3072]{2,1,0:T(8,128)}, f32[8,8,3072]{2,1,0:T(8,128)}, u32[]{:S(2)}, u32[]{:S(2)}) collective-permute-start(f32[8,8,3072]{2,1,0:T(8,128)} %get-tuple-element.94), channel_id=1, source_target_pairs={{0,2},{1,3},{2,0},{3,1},{4,6},{5,7},{6,4},{7,5},{8,10},{9,11},{10,... | collective-permute-start | bytes 2359304 | tf_op jit(solution)/shard_map/cond/branch_1_fun/ppermute | solution.py:43
  73.9 41.0 %collective-permute-start.4 = (f32[8,8,3072]{2,1,0:T(8,128)}, f32[8,8,3072]{2,1,0:T(8,128)}, u32[]{:S(2)}, u32[]{:S(2)}) collective-permute-start(f32[8,8,3072]{2,1,0:T(8,128)} %get-tuple-element.92.refs_12_), channel_id=1, source_target_pairs={{0,8},{1,9},{2,10},{3,11},{4,12},{5,13},{6,14},{7,15},{8,0},{9,1},... | collective-permute-start | bytes 2359304 | tf_op jit(solution)/shard_map/cond/branch_1_fun/ppermute | solution.py:43
  75.6 39.3 %slice-start = ((s8[4718592]{0:T(1024)(128)(4,1)}), s8[4194304]{0:T(1024)(128)(4,1)S(1)}, s32[]{:S(2)}) async-start(s8[4718592]{0:T(1024)(128)(4,1)} %bitcast.28), calls=%async_computation.1 | async-start | bytes 8388608 | tf_op jit(solution)/shard_map/cond
  83.2 31.7 %slice-start.1 = ((s8[4718592]{0:T(1024)(128)(4,1)}), s8[524288]{0:T(1024)(128)(4,1)S(1)}, s32[]{:S(2)}) async-start(s8[4718592]{0:T(1024)(128)(4,1)} %bitcast.28), calls=%async_computation.2 | async-start | bytes 1048576 | tf_op jit(solution)/shard_map/cond
  83.2 31.7 %copy-start.2 = (f32[48,8,3072]{2,1,0:T(8,128)S(1)}, f32[48,8,3072]{2,1,0:T(8,128)}, u32[]{:S(2)}) copy-start(f32[48,8,3072]{2,1,0:T(8,128)} %copy-done.1) | copy-start | bytes 14155780 | tf_op jit(solution)/shard_map/cond
  100.8 19.0 %copy-start.11 = (bf16[768,512]{1,0:T(8,128)(2,1)}, bf16[768,512]{1,0:T(8,128)(2,1)S(1)}, u32[]{:S(2)}) copy-start(bf16[768,512]{1,0:T(8,128)(2,1)S(1)} %get-tuple-element.102.refs_1_.refs_12_) | copy-start | bytes 2359300 | tf_op jit(solution)/shard_map/cond
  100.8 7.0 %collective-permute-start.9 = (f32[6,80,128]{2,1,0:T(8,128)S(1)}, f32[6,80,128]{2,1,0:T(8,128)S(1)}, u32[]{:S(2)}, u32[]{:S(2)}) collective-permute-start(f32[6,80,128]{2,1,0:T(8,128)S(1)} %get-tuple-element.105), channel_id=1, source_target_pairs={{0,24},{1,25},{2,26},{3,27},{4,28},{5,29},{6,30},{7,31},{8,16},{9,... | collective-permute-start | bytes 737288 | tf_op jit(solution)/shard_map/cond/branch_1_fun/ppermute | solution.py:43
  102.1 12.8 %collective-permute-start.8 = (f32[6,80,128]{2,1,0:T(8,128)S(1)}, f32[6,80,128]{2,1,0:T(8,128)S(1)}, u32[]{:S(2)}, u32[]{:S(2)}) collective-permute-start(f32[6,80,128]{2,1,0:T(8,128)S(1)} %get-tuple-element.105), channel_id=1, source_target_pairs={{0,16},{1,17},{2,18},{3,19},{4,20},{5,21},{6,22},{7,23},{8,24},{9,... | collective-permute-start | bytes 737288 | tf_op jit(solution)/shard_map/cond/branch_1_fun/ppermute | solution.py:43
  107.8 7.1 %collective-permute-start.7 = (f32[6,80,128]{2,1,0:T(8,128)S(1)}, f32[6,80,128]{2,1,0:T(8,128)S(1)}, u32[]{:S(2)}, u32[]{:S(2)}) collective-permute-start(f32[6,80,128]{2,1,0:T(8,128)S(1)} %get-tuple-element.105), channel_id=1, source_target_pairs={{0,8},{1,9},{2,10},{3,11},{4,12},{5,13},{6,14},{7,15},{8,0},{9,1},... | collective-permute-start | bytes 737288 | tf_op jit(solution)/shard_map/cond/branch_1_fun/ppermute | solution.py:43
  117.8 13.1 %collective-permute-start.11 = (f32[4,8,3072]{2,1,0:T(8,128)S(1)}, f32[4,8,3072]{2,1,0:T(8,128)S(1)}, u32[]{:S(2)}, u32[]{:S(2)}) collective-permute-start(f32[4,8,3072]{2,1,0:T(8,128)S(1)} %get-tuple-element.107), channel_id=1, source_target_pairs={{0,2},{1,3},{2,0},{3,1},{4,6},{5,7},{6,4},{7,5},{8,10},{9,11},{10,... | collective-permute-start | bytes 1179656 | tf_op jit(solution)/shard_map/cond/branch_1_fun/ppermute | solution.py:43
  118.1 12.8 %collective-permute-start.12 = (f32[4,8,3072]{2,1,0:T(8,128)S(1)}, f32[4,8,3072]{2,1,0:T(8,128)S(1)}, u32[]{:S(2)}, u32[]{:S(2)}) collective-permute-start(f32[4,8,3072]{2,1,0:T(8,128)S(1)} %get-tuple-element.108), channel_id=1, source_target_pairs={{0,8},{1,9},{2,10},{3,11},{4,12},{5,13},{6,14},{7,15},{8,0},{9,1},... | collective-permute-start | bytes 1179656 | tf_op jit(solution)/shard_map/cond/branch_1_fun/ppermute | solution.py:43
  118.9 12.0 %collective-permute-start.10 = (f32[4,8,3072]{2,1,0:T(8,128)S(1)}, f32[4,8,3072]{2,1,0:T(8,128)S(1)}, u32[]{:S(2)}, u32[]{:S(2)}) collective-permute-start(f32[4,8,3072]{2,1,0:T(8,128)S(1)} %get-tuple-element.106.refs_27_), channel_id=1, source_target_pairs={{0,16},{1,17},{2,18},{3,19},{4,20},{5,21},{6,22},{7,23},{8,24},{9,... | collective-permute-start | bytes 1179656 | tf_op jit(solution)/shard_map/cond/branch_1_fun/ppermute | solution.py:43
  140.0 11.8 %collective-permute-start.17 = (f32[48,4,8,768]{3,2,1,0:T(8,128)S(1)}, f32[48,4,8,768]{3,2,1,0:T(8,128)S(1)}, u32[]{:S(2)}, u32[]{:S(2)}) collective-permute-start(f32[48,4,8,768]{3,2,1,0:T(8,128)S(1)} %get-tuple-element.127), channel_id=1, source_target_pairs={{0,1},{1,0},{2,3},{3,2},{4,5},{5,4},{6,7},{7,6},{8,9},{9,8},{10,11... | collective-permute-start | bytes 14155784 | tf_op jit(solution)/shard_map/cond/branch_1_fun/ppermute | solution.py:43
  141.5 6.5 %collective-permute-start.14 = (f32[2,8,3072]{2,1,0:T(8,128)S(1)}, f32[2,8,3072]{2,1,0:T(8,128)S(1)}, u32[]{:S(2)}, u32[]{:S(2)}) collective-permute-start(f32[2,8,3072]{2,1,0:T(8,128)S(1)} %get-tuple-element.120), channel_id=1, source_target_pairs={{0,8},{1,9},{2,10},{3,11},{4,12},{5,13},{6,14},{7,15},{8,0},{9,1},... | collective-permute-start | bytes 589832 | tf_op jit(solution)/shard_map/cond/branch_1_fun/ppermute | solution.py:43
  142.2 6.2 %collective-permute-start.15 = (f32[2,8,3072]{2,1,0:T(8,128)S(1)}, f32[2,8,3072]{2,1,0:T(8,128)S(1)}, u32[]{:S(2)}, u32[]{:S(2)}) collective-permute-start(f32[2,8,3072]{2,1,0:T(8,128)S(1)} %get-tuple-element.121), channel_id=1, source_target_pairs={{0,16},{1,17},{2,18},{3,19},{4,20},{5,21},{6,22},{7,23},{8,24},{9,... | collective-permute-start | bytes 589832 | tf_op jit(solution)/shard_map/cond/branch_1_fun/ppermute | solution.py:43
  143.2 6.6 %collective-permute-start.13 = (f32[2,8,3072]{2,1,0:T(8,128)S(1)}, f32[2,8,3072]{2,1,0:T(8,128)S(1)}, u32[]{:S(2)}, u32[]{:S(2)}) collective-permute-start(f32[2,8,3072]{2,1,0:T(8,128)S(1)} %get-tuple-element.119.refs_31_), channel_id=1, source_target_pairs={{0,2},{1,3},{2,0},{3,1},{4,6},{5,7},{6,4},{7,5},{8,10},{9,11},{10,... | collective-permute-start | bytes 589832 | tf_op jit(solution)/shard_map/cond/branch_1_fun/ppermute | solution.py:43
  143.5 8.3 %collective-permute-start.18 = (f32[1,2,8,768]{3,2,1,0:T(8,128)S(1)}, f32[1,2,8,768]{3,2,1,0:T(8,128)S(1)}, u32[]{:S(2)}, u32[]{:S(2)}) collective-permute-start(f32[1,2,8,768]{3,2,1,0:T(8,128)S(1)} %bitcast.58), channel_id=1, source_target_pairs={{0,1},{1,0},{2,3},{3,2},{4,5},{5,4},{6,7},{7,6},{8,9},{9,8},{10,11... | collective-permute-start | bytes 147464 | tf_op jit(solution)/shard_map/cond/branch_1_fun/ppermute | solution.py:43
  152.7 27.4 %collective-permute-start.20 = (f32[8,4,8,768]{3,2,1,0:T(8,128)S(1)}, f32[8,4,8,768]{3,2,1,0:T(8,128)S(1)}, u32[]{:S(2)}, u32[]{:S(2)}) collective-permute-start(f32[8,4,8,768]{3,2,1,0:T(8,128)S(1)} %get-tuple-element.130), channel_id=1, source_target_pairs={{0,16},{1,17},{2,18},{3,19},{4,20},{5,21},{6,22},{7,23},{8,24},{9,... | collective-permute-start | bytes 2359304 | tf_op jit(solution)/shard_map/cond/branch_1_fun/ppermute | solution.py:43
  153.6 28.2 %collective-permute-start.21 = (f32[8,4,8,768]{3,2,1,0:T(8,128)S(1)}, f32[8,4,8,768]{3,2,1,0:T(8,128)S(1)}, u32[]{:S(2)}, u32[]{:S(2)}) collective-permute-start(f32[8,4,8,768]{3,2,1,0:T(8,128)S(1)} %get-tuple-element.131), channel_id=1, source_target_pairs={{0,2},{1,3},{2,0},{3,1},{4,6},{5,7},{6,4},{7,5},{8,10},{9,11},{10,... | collective-permute-start | bytes 2359304 | tf_op jit(solution)/shard_map/cond/branch_1_fun/ppermute | solution.py:43
  154.3 27.6 %collective-permute-start.19 = (f32[8,4,8,768]{3,2,1,0:T(8,128)S(1)}, f32[8,4,8,768]{3,2,1,0:T(8,128)S(1)}, u32[]{:S(2)}, u32[]{:S(2)}) collective-permute-start(f32[8,4,8,768]{3,2,1,0:T(8,128)S(1)} %get-tuple-element.129.refs_11_), channel_id=1, source_target_pairs={{0,8},{1,9},{2,10},{3,11},{4,12},{5,13},{6,14},{7,15},{8,0},{9,1},... | collective-permute-start | bytes 2359304 | tf_op jit(solution)/shard_map/cond/branch_1_fun/ppermute | solution.py:43
  155.5 24.7 %collective-permute-start.22 = (f32[1,2,8,768]{3,2,1,0:T(8,128)S(1)}, f32[1,2,8,768]{3,2,1,0:T(8,128)S(1)}, u32[]{:S(2)}, u32[]{:S(2)}) collective-permute-start(f32[1,2,8,768]{3,2,1,0:T(8,128)S(1)} %get-tuple-element.132.refs_9_), channel_id=1, source_target_pairs={{0,8},{1,9},{2,10},{3,11},{4,12},{5,13},{6,14},{7,15},{8,0},{9,1},... | collective-permute-start | bytes 147464 | tf_op jit(solution)/shard_map/cond/branch_1_fun/ppermute | solution.py:43
  182.6 20.2 %collective-permute-start.24 = (f32[4,4,8,768]{3,2,1,0:T(8,128)S(1)}, f32[4,4,8,768]{3,2,1,0:T(8,128)S(1)}, u32[]{:S(2)}, u32[]{:S(2)}) collective-permute-start(f32[4,4,8,768]{3,2,1,0:T(8,128)S(1)} %get-tuple-element.134), channel_id=1, source_target_pairs={{0,2},{1,3},{2,0},{3,1},{4,6},{5,7},{6,4},{7,5},{8,10},{9,11},{10,... | collective-permute-start | bytes 1179656 | tf_op jit(solution)/shard_map/cond/branch_1_fun/ppermute | solution.py:43
  183.2 19.6 %collective-permute-start.25 = (f32[4,4,8,768]{3,2,1,0:T(8,128)S(1)}, f32[4,4,8,768]{3,2,1,0:T(8,128)S(1)}, u32[]{:S(2)}, u32[]{:S(2)}) collective-permute-start(f32[4,4,8,768]{3,2,1,0:T(8,128)S(1)} %get-tuple-element.135), channel_id=1, source_target_pairs={{0,8},{1,9},{2,10},{3,11},{4,12},{5,13},{6,14},{7,15},{8,0},{9,1},... | collective-permute-start | bytes 1179656 | tf_op jit(solution)/shard_map/cond/branch_1_fun/ppermute | solution.py:43
  184.9 18.0 %collective-permute-start.23 = (f32[4,4,8,768]{3,2,1,0:T(8,128)S(1)}, f32[4,4,8,768]{3,2,1,0:T(8,128)S(1)}, u32[]{:S(2)}, u32[]{:S(2)}) collective-permute-start(f32[4,4,8,768]{3,2,1,0:T(8,128)S(1)} %get-tuple-element.133.refs_14_), channel_id=1, source_target_pairs={{0,16},{1,17},{2,18},{3,19},{4,20},{5,21},{6,22},{7,23},{8,24},{9,... | collective-permute-start | bytes 1179656 | tf_op jit(solution)/shard_map/cond/branch_1_fun/ppermute | solution.py:43
  184.9 45.8 %collective-permute-start.16 = (f32[6,8,3072]{2,1,0:T(8,128)S(1)}, f32[6,8,3072]{2,1,0:T(8,128)S(1)}, u32[]{:S(2)}, u32[]{:S(2)}) collective-permute-start(f32[6,8,3072]{2,1,0:T(8,128)S(1)} %sum_tiles.13.refs_8_.refs_0_.refs_2_.refs_4_), channel_id=1, source_target_pairs={{0,4},{1,5},{2,6},{3,7},{4,0},{5,1},{6,2},{7,3},{8,12},{9,13},{10,... | collective-permute-start | bytes 1769480 | tf_op jit(solution)/shard_map/cond/branch_1_fun/ppermute | solution.py:43
  185.6 17.2 %collective-permute-start.26 = (f32[1,2,8,768]{3,2,1,0:T(8,128)S(1)}, f32[1,2,8,768]{3,2,1,0:T(8,128)S(1)}, u32[]{:S(2)}, u32[]{:S(2)}) collective-permute-start(f32[1,2,8,768]{3,2,1,0:T(8,128)S(1)} %get-tuple-element.136.refs_12_), channel_id=1, source_target_pairs={{0,16},{1,17},{2,18},{3,19},{4,20},{5,21},{6,22},{7,23},{8,24},{9,... | collective-permute-start | bytes 147464 | tf_op jit(solution)/shard_map/cond/branch_1_fun/ppermute | solution.py:43
  203.6 26.2 %collective-permute-start.28 = (f32[2,4,8,768]{3,2,1,0:T(8,128)S(1)}, f32[2,4,8,768]{3,2,1,0:T(8,128)S(1)}, u32[]{:S(2)}, u32[]{:S(2)}) collective-permute-start(f32[2,4,8,768]{3,2,1,0:T(8,128)S(1)} %get-tuple-element.138), channel_id=1, source_target_pairs={{0,8},{1,9},{2,10},{3,11},{4,12},{5,13},{6,14},{7,15},{8,0},{9,1},... | collective-permute-start | bytes 589832 | tf_op jit(solution)/shard_map/cond/branch_1_fun/ppermute | solution.py:43
  204.6 25.2 %collective-permute-start.29 = (f32[2,4,8,768]{3,2,1,0:T(8,128)S(1)}, f32[2,4,8,768]{3,2,1,0:T(8,128)S(1)}, u32[]{:S(2)}, u32[]{:S(2)}) collective-permute-start(f32[2,4,8,768]{3,2,1,0:T(8,128)S(1)} %get-tuple-element.139), channel_id=1, source_target_pairs={{0,16},{1,17},{2,18},{3,19},{4,20},{5,21},{6,22},{7,23},{8,24},{9,... | collective-permute-start | bytes 589832 | tf_op jit(solution)/shard_map/cond/branch_1_fun/ppermute | solution.py:43
  204.6 25.2 %collective-permute-start.27 = (f32[2,4,8,768]{3,2,1,0:T(8,128)S(1)}, f32[2,4,8,768]{3,2,1,0:T(8,128)S(1)}, u32[]{:S(2)}, u32[]{:S(2)}) collective-permute-start(f32[2,4,8,768]{3,2,1,0:T(8,128)S(1)} %get-tuple-element.137.refs_17_), channel_id=1, source_target_pairs={{0,2},{1,3},{2,0},{3,1},{4,6},{5,7},{6,4},{7,5},{8,10},{9,11},{10,... | collective-permute-start | bytes 589832 | tf_op jit(solution)/shard_map/cond/branch_1_fun/ppermute | solution.py:43
  204.6 25.2 %collective-permute-start.30 = (f32[1,2,8,768]{3,2,1,0:T(8,128)S(1)}, f32[1,2,8,768]{3,2,1,0:T(8,128)S(1)}, u32[]{:S(2)}, u32[]{:S(2)}) collective-permute-start(f32[1,2,8,768]{3,2,1,0:T(8,128)S(1)} %get-tuple-element.140.refs_15_), channel_id=1, source_target_pairs={{0,2},{1,3},{2,0},{3,1},{4,6},{5,7},{6,4},{7,5},{8,10},{9,11},{10,... | collective-permute-start | bytes 147464 | tf_op jit(solution)/shard_map/cond/branch_1_fun/ppermute | solution.py:43
  231.3 11.3 %collective-permute-start.31 = (f32[2,8,3072]{2,1,0:T(8,128)S(1)}, f32[2,8,3072]{2,1,0:T(8,128)S(1)}, u32[]{:S(2)}, u32[]{:S(2)}) collective-permute-start(f32[2,8,3072]{2,1,0:T(8,128)S(1)} %get-tuple-element.142.refs_0_.refs_6_), channel_id=1, source_target_pairs={{0,2},{1,3},{2,0},{3,1},{4,6},{5,7},{6,4},{7,5},{8,10},{9,11},{10,... | collective-permute-start | bytes 589832 | tf_op jit(solution)/shard_map/cond/branch_1_fun/ppermute | solution.py:43
  233.7 8.9 %collective-permute-start.32 = (f32[2,8,3072]{2,1,0:T(8,128)S(1)}, f32[2,8,3072]{2,1,0:T(8,128)S(1)}, u32[]{:S(2)}, u32[]{:S(2)}) collective-permute-start(f32[2,8,3072]{2,1,0:T(8,128)S(1)} %get-tuple-element.143.refs_2_), channel_id=1, source_target_pairs={{0,8},{1,9},{2,10},{3,11},{4,12},{5,13},{6,14},{7,15},{8,0},{9,1},... | collective-permute-start | bytes 589832 | tf_op jit(solution)/shard_map/cond/branch_1_fun/ppermute | solution.py:43
  236.0 6.6 %collective-permute-start.33 = (f32[2,8,3072]{2,1,0:T(8,128)S(1)}, f32[2,8,3072]{2,1,0:T(8,128)S(1)}, u32[]{:S(2)}, u32[]{:S(2)}) collective-permute-start(f32[2,8,3072]{2,1,0:T(8,128)S(1)} %get-tuple-element.144.refs_4_), channel_id=1, source_target_pairs={{0,16},{1,17},{2,18},{3,19},{4,20},{5,21},{6,22},{7,23},{8,24},{9,... | collective-permute-start | bytes 589832 | tf_op jit(solution)/shard_map/cond/branch_1_fun/ppermute | solution.py:43
  236.0 42.8 %collective-permute-start.37 = (f32[6,4,8,768]{3,2,1,0:T(8,128)S(1)}, f32[6,4,8,768]{3,2,1,0:T(8,128)S(1)}, u32[]{:S(2)}, u32[]{:S(2)}) collective-permute-start(f32[6,4,8,768]{3,2,1,0:T(8,128)S(1)} %get-tuple-element.141.refs_6_.refs_0_.refs_2_.refs_4_), channel_id=1, source_target_pairs={{0,4},{1,5},{2,6},{3,7},{4,0},{5,1},{6,2},{7,3},{8,12},{9,13},{10,... | collective-permute-start | bytes 1769480 | tf_op jit(solution)/shard_map/cond/branch_1_fun/ppermute | solution.py:43
  243.4 36.0 %collective-permute-start.35 = (f32[4,8,3072]{2,1,0:T(8,128)S(1)}, f32[4,8,3072]{2,1,0:T(8,128)S(1)}, u32[]{:S(2)}, u32[]{:S(2)}) collective-permute-start(f32[4,8,3072]{2,1,0:T(8,128)S(1)} %bitcast.54), channel_id=1, source_target_pairs={{0,2},{1,3},{2,0},{3,1},{4,6},{5,7},{6,4},{7,5},{8,10},{9,11},{10,... | collective-permute-start | bytes 1179656 | tf_op jit(solution)/shard_map/cond/branch_1_fun/ppermute | solution.py:43
  244.0 35.4 %collective-permute-start.34 = (f32[4,8,3072]{2,1,0:T(8,128)S(1)}, f32[4,8,3072]{2,1,0:T(8,128)S(1)}, u32[]{:S(2)}, u32[]{:S(2)}) collective-permute-start(f32[4,8,3072]{2,1,0:T(8,128)S(1)} %bitcast.39), channel_id=1, source_target_pairs={{0,16},{1,17},{2,18},{3,19},{4,20},{5,21},{6,22},{7,23},{8,24},{9,... | collective-permute-start | bytes 1179656 | tf_op jit(solution)/shard_map/cond/branch_1_fun/ppermute | solution.py:43
  244.0 35.4 %collective-permute-start.36 = (f32[4,8,3072]{2,1,0:T(8,128)S(1)}, f32[4,8,3072]{2,1,0:T(8,128)S(1)}, u32[]{:S(2)}, u32[]{:S(2)}) collective-permute-start(f32[4,8,3072]{2,1,0:T(8,128)S(1)} %bitcast.56), channel_id=1, source_target_pairs={{0,8},{1,9},{2,10},{3,11},{4,12},{5,13},{6,14},{7,15},{8,0},{9,1},... | collective-permute-start | bytes 1179656 | tf_op jit(solution)/shard_map/cond/branch_1_fun/ppermute | solution.py:43
  247.7 31.1 %collective-permute-start.38 = (f32[1,2,8,768]{3,2,1,0:T(8,128)S(1)}, f32[1,2,8,768]{3,2,1,0:T(8,128)S(1)}, u32[]{:S(2)}, u32[]{:S(2)}) collective-permute-start(f32[1,2,8,768]{3,2,1,0:T(8,128)S(1)} %get-tuple-element.148.refs_6_), channel_id=1, source_target_pairs={{0,4},{1,5},{2,6},{3,7},{4,0},{5,1},{6,2},{7,3},{8,12},{9,13},{10,... | collective-permute-start | bytes 147464 | tf_op jit(solution)/shard_map/cond/branch_1_fun/ppermute | solution.py:43
  279.4 60.5 %copy-start.39 = (f32[1,2,8,768]{3,2,1,0:T(8,128)}, f32[1,2,8,768]{3,2,1,0:T(8,128)S(1)}, u32[]{:S(2)}) copy-start(f32[1,2,8,768]{3,2,1,0:T(8,128)S(1)} %get-tuple-element.165) | copy-start | bytes 147460 | tf_op jit(solution)/shard_map/cond
  280.4 25.2 %collective-permute-start.40 = (f32[8,8,3072]{2,1,0:T(8,128)S(1)}, f32[8,8,3072]{2,1,0:T(8,128)S(1)}, u32[]{:S(2)}, u32[]{:S(2)}) collective-permute-start(f32[8,8,3072]{2,1,0:T(8,128)S(1)} %bitcast.46), channel_id=1, source_target_pairs={{0,16},{1,17},{2,18},{3,19},{4,20},{5,21},{6,22},{7,23},{8,24},{9,... | collective-permute-start | bytes 2359304 | tf_op jit(solution)/shard_map/cond/branch_1_fun/ppermute | solution.py:43
  281.4 4.5 %collective-permute-start.43 = (f32[2,4,8,768]{3,2,1,0:T(8,128)S(1)}, f32[2,4,8,768]{3,2,1,0:T(8,128)S(1)}, u32[]{:S(2)}, u32[]{:S(2)}) collective-permute-start(f32[2,4,8,768]{3,2,1,0:T(8,128)S(1)} %get-tuple-element.153.refs_2_), channel_id=1, source_target_pairs={{0,8},{1,9},{2,10},{3,11},{4,12},{5,13},{6,14},{7,15},{8,0},{9,1},... | collective-permute-start | bytes 589832 | tf_op jit(solution)/shard_map/cond/branch_1_fun/ppermute | solution.py:43
  282.5 24.6 %collective-permute-start.39 = (f32[8,8,3072]{2,1,0:T(8,128)S(1)}, f32[8,8,3072]{2,1,0:T(8,128)S(1)}, u32[]{:S(2)}, u32[]{:S(2)}) collective-permute-start(f32[8,8,3072]{2,1,0:T(8,128)S(1)} %bitcast.33), channel_id=1, source_target_pairs={{0,8},{1,9},{2,10},{3,11},{4,12},{5,13},{6,14},{7,15},{8,0},{9,1},... | collective-permute-start | bytes 2359304 | tf_op jit(solution)/shard_map/cond/branch_1_fun/ppermute | solution.py:43
  282.8 24.3 %collective-permute-start.41 = (f32[8,8,3072]{2,1,0:T(8,128)S(1)}, f32[8,8,3072]{2,1,0:T(8,128)S(1)}, u32[]{:S(2)}, u32[]{:S(2)}) collective-permute-start(f32[8,8,3072]{2,1,0:T(8,128)S(1)} %bitcast.48), channel_id=1, source_target_pairs={{0,2},{1,3},{2,0},{3,1},{4,6},{5,7},{6,4},{7,5},{8,10},{9,11},{10,... | collective-permute-start | bytes 2359304 | tf_op jit(solution)/shard_map/cond/branch_1_fun/ppermute | solution.py:43
  284.6 14.0 %collective-permute-start.44 = (f32[2,4,8,768]{3,2,1,0:T(8,128)S(1)}, f32[2,4,8,768]{3,2,1,0:T(8,128)S(1)}, u32[]{:S(2)}, u32[]{:S(2)}) collective-permute-start(f32[2,4,8,768]{3,2,1,0:T(8,128)S(1)} %get-tuple-element.154.refs_4_), channel_id=1, source_target_pairs={{0,16},{1,17},{2,18},{3,19},{4,20},{5,21},{6,22},{7,23},{8,24},{9,... | collective-permute-start | bytes 589832 | tf_op jit(solution)/shard_map/cond/branch_1_fun/ppermute | solution.py:43
  285.9 15.5 %collective-permute-start.42 = (f32[2,4,8,768]{3,2,1,0:T(8,128)S(1)}, f32[2,4,8,768]{3,2,1,0:T(8,128)S(1)}, u32[]{:S(2)}, u32[]{:S(2)}) collective-permute-start(f32[2,4,8,768]{3,2,1,0:T(8,128)S(1)} %get-tuple-element.149.refs_6_.refs_0_), channel_id=1, source_target_pairs={{0,2},{1,3},{2,0},{3,1},{4,6},{5,7},{6,4},{7,5},{8,10},{9,11},{10,... | collective-permute-start | bytes 589832 | tf_op jit(solution)/shard_map/cond/branch_1_fun/ppermute | solution.py:43
  302.1 8.7 %collective-permute-start.47 = (f32[4,4,8,768]{3,2,1,0:T(8,128)S(1)}, f32[4,4,8,768]{3,2,1,0:T(8,128)S(1)}, u32[]{:S(2)}, u32[]{:S(2)}) collective-permute-start(f32[4,4,8,768]{3,2,1,0:T(8,128)S(1)} %bitcast.50), channel_id=1, source_target_pairs={{0,2},{1,3},{2,0},{3,1},{4,6},{5,7},{6,4},{7,5},{8,10},{9,11},{10,... | collective-permute-start | bytes 1179656 | tf_op jit(solution)/shard_map/cond/branch_1_fun/ppermute | solution.py:43
  304.4 6.6 %collective-permute-start.46 = (f32[4,4,8,768]{3,2,1,0:T(8,128)S(1)}, f32[4,4,8,768]{3,2,1,0:T(8,128)S(1)}, u32[]{:S(2)}, u32[]{:S(2)}) collective-permute-start(f32[4,4,8,768]{3,2,1,0:T(8,128)S(1)} %bitcast.36), channel_id=1, source_target_pairs={{0,16},{1,17},{2,18},{3,19},{4,20},{5,21},{6,22},{7,23},{8,24},{9,... | collective-permute-start | bytes 1179656 | tf_op jit(solution)/shard_map/cond/branch_1_fun/ppermute | solution.py:43
  305.6 7.0 %collective-permute-start.48 = (f32[4,4,8,768]{3,2,1,0:T(8,128)S(1)}, f32[4,4,8,768]{3,2,1,0:T(8,128)S(1)}, u32[]{:S(2)}, u32[]{:S(2)}) collective-permute-start(f32[4,4,8,768]{3,2,1,0:T(8,128)S(1)} %bitcast.52), channel_id=1, source_target_pairs={{0,8},{1,9},{2,10},{3,11},{4,12},{5,13},{6,14},{7,15},{8,0},{9,1},... | collective-permute-start | bytes 1179656 | tf_op jit(solution)/shard_map/cond/branch_1_fun/ppermute | solution.py:43
  313.5 15.8 %collective-permute-start.50 = (f32[8,4,8,768]{3,2,1,0:T(8,128)S(1)}, f32[8,4,8,768]{3,2,1,0:T(8,128)S(1)}, u32[]{:S(2)}, u32[]{:S(2)}) collective-permute-start(f32[8,4,8,768]{3,2,1,0:T(8,128)S(1)} %bitcast.42), channel_id=1, source_target_pairs={{0,16},{1,17},{2,18},{3,19},{4,20},{5,21},{6,22},{7,23},{8,24},{9,... | collective-permute-start | bytes 2359304 | tf_op jit(solution)/shard_map/cond/branch_1_fun/ppermute | solution.py:43
  313.9 15.4 %collective-permute-start.49 = (f32[8,4,8,768]{3,2,1,0:T(8,128)S(1)}, f32[8,4,8,768]{3,2,1,0:T(8,128)S(1)}, u32[]{:S(2)}, u32[]{:S(2)}) collective-permute-start(f32[8,4,8,768]{3,2,1,0:T(8,128)S(1)} %bitcast.30), channel_id=1, source_target_pairs={{0,8},{1,9},{2,10},{3,11},{4,12},{5,13},{6,14},{7,15},{8,0},{9,1},... | collective-permute-start | bytes 2359304 | tf_op jit(solution)/shard_map/cond/branch_1_fun/ppermute | solution.py:43
  315.4 13.9 %collective-permute-start.51 = (f32[8,4,8,768]{3,2,1,0:T(8,128)S(1)}, f32[8,4,8,768]{3,2,1,0:T(8,128)S(1)}, u32[]{:S(2)}, u32[]{:S(2)}) collective-permute-start(f32[8,4,8,768]{3,2,1,0:T(8,128)S(1)} %bitcast.44), channel_id=1, source_target_pairs={{0,2},{1,3},{2,0},{3,1},{4,6},{5,7},{6,4},{7,5},{8,10},{9,11},{10,... | collective-permute-start | bytes 2359304 | tf_op jit(solution)/shard_map/cond/branch_1_fun/ppermute | solution.py:43
  315.5 29.7 %collective-permute-start.45 = (f32[48,8,3072]{2,1,0:T(8,128)}, f32[48,8,3072]{2,1,0:T(8,128)}, u32[]{:S(2)}, u32[]{:S(2)}) collective-permute-start(f32[48,8,3072]{2,1,0:T(8,128)} %bitcast.10.refs_6_.part), channel_id=1, source_target_pairs={{0,1},{1,0},{2,3},{3,2},{4,5},{5,4},{6,7},{7,6},{8,9},{9,8},{10,11... | collective-permute-start | bytes 14155784 | tf_op jit(solution)/shard_map/cond/branch_1_fun/ppermute | solution.py:43
  332.5 17.3 %collective-permute-start.52 = (f32[48,4,8,768]{3,2,1,0:T(8,128)}, f32[48,4,8,768]{3,2,1,0:T(8,128)}, u32[]{:S(2)}, u32[]{:S(2)}) collective-permute-start(f32[48,4,8,768]{3,2,1,0:T(8,128)} %bitcast.16.part.refs_0_), channel_id=1, source_target_pairs={{0,1},{1,0},{2,3},{3,2},{4,5},{5,4},{6,7},{7,6},{8,9},{9,8},{10,11... | collective-permute-start | bytes 14155784 | tf_op jit(solution)/shard_map/cond/branch_1_fun/ppermute | solution.py:43
  (52 other events, 266.8 us)
Sparse Core Ops, SparseCore 0:
  26.1 256.8 all-reduce.1
